TPU v7x, 32 devices: a whole 2x2x4 slice. The times are simulated.
32 devices in a mesh: seq: 16 (over z, x, core), head: 2 (over y).
Axes of the slice: x: 2, y: 2, z: 4, core: 2. Of those that a mesh axis runs over, the one named last changes fastest.
Arguments:
- draft_query: bfloat16 [1, 96, 8192], P(None, 'seq', 'head'), may hold values from -28 to 28
- draft_key: bfloat16 [1, 96, 1024], P(None, 'seq', 'head'), may hold values from -8 to 8
- draft_value: bfloat16 [1, 96, 1024], P(None, 'seq', 'head'), may hold values from -48 to 48
- cache_key: bfloat16 [1, 16384, 1024], P(None, 'seq', 'head'), may hold values from -16 to 16
- cache_value: bfloat16 [1, 16384, 1024], P(None, 'seq', 'head'), may hold values from -48 to 48
- accepted: int32 [1], replicated, may hold values from 0 to 96
- cache_len: int32 [1], replicated, may hold values from 4096 to 16288
- out_weight: bfloat16 [8192, 8192], P('head', 'seq'), may hold values from -0.0625 to 0.0625
Outputs:
- projected: bfloat16 [1, 96, 8192], P(None, 'head', 'seq')
- new_key: bfloat16 [1, 16384, 1024], P(None, 'seq', 'head')
- new_value: bfloat16 [1, 16384, 1024], P(None, 'seq', 'head')
All inputs are finite; a program needn't handle non-finite values.
Results may differ from a plain program's by a relative error of at most 0.0052.
Values may be sent and summed in bfloat16 or wider, within the bound.
No kernel may reach another device: no remote copies, remote signals or barrier semaphores. Data moves between devices by JAX's collectives and lax.ppermute only.
A program may use at most 64 MiB of HBM per device.

v0:
```python
import math

import jax
import jax.numpy as jnp
from jax import lax
from jax.sharding import PartitionSpec as P

QH = 64
KVH = 8
HD = 128


masked_score = -1e30


def largest_divisor(count_all, upper_bound):
    divisor = min(count_all, upper_bound)
    while count_all % divisor != 0:
        divisor = divisor - 1
    return divisor


def partial_block(
    query_block,
    position_block,
    keys_cache,
    values_cache,
    keys_draft,
    values_draft,
    live_cache,
    draft_positions,
):
    scale_factor = 1.0 / math.sqrt(HD)
    cache_scores = (
        jnp.einsum("qkgd,ckd->qkgc", query_block, keys_cache, preferred_element_type=jnp.float32)
        * scale_factor
    )
    draft_scores = (
        jnp.einsum("qkgd,ukd->qkgu", query_block, keys_draft, preferred_element_type=jnp.float32)
        * scale_factor
    )
    cache_mask = live_cache[None, None, None, :]
    draft_mask = (draft_positions[None, :] <= position_block[:, None])[:, None, None, :]
    maxima = jnp.maximum(
        jnp.max(jnp.where(cache_mask, cache_scores, masked_score), axis=-1),
        jnp.max(jnp.where(draft_mask, draft_scores, masked_score), axis=-1),
    )
    cache_probs = jnp.where(cache_mask, jnp.exp(cache_scores - maxima[..., None]), 0.0).astype(
        jnp.bfloat16
    )
    draft_probs = jnp.where(draft_mask, jnp.exp(draft_scores - maxima[..., None]), 0.0).astype(
        jnp.bfloat16
    )
    totals = jnp.sum(cache_probs.astype(jnp.float32), axis=-1) + jnp.sum(
        draft_probs.astype(jnp.float32), axis=-1
    )
    weighted = jnp.einsum(
        "qkgc,ckd->qkgd", cache_probs, values_cache, preferred_element_type=jnp.float32
    )
    weighted = weighted + jnp.einsum(
        "qkgu,ukd->qkgd", draft_probs, values_draft, preferred_element_type=jnp.float32
    )
    return (maxima, totals, weighted)


def on_device(
    draft_query, draft_key, draft_value, cache_key, cache_value, accepted, cache_len, out_weight
):
    seq_index = lax.axis_index("seq")
    requests = draft_query.shape[0]
    local_rows = draft_key.shape[1]
    cache_rows = cache_key.shape[1]
    heads_kv = draft_key.shape[2] // HD
    group_size = QH // KVH
    heads_q = heads_kv * group_size
    gathered = lax.all_gather(draft_query, "seq", axis=1, tiled=True)
    all_rows = gathered.shape[1]
    cache_positions = seq_index * cache_rows + jnp.arange(cache_rows, dtype=jnp.int32)
    draft_positions = seq_index * local_rows + jnp.arange(local_rows, dtype=jnp.int32)
    block_rows = largest_divisor(all_rows, 64)
    blocks = all_rows // block_rows
    position_blocks = jnp.arange(all_rows, dtype=jnp.int32).reshape(blocks, block_rows)

    def one_request(request_data):
        queries, keys_cache, values_cache, keys_draft, values_draft, length = request_data
        live_cache = cache_positions < length
        keys_cache = keys_cache.reshape(cache_rows, heads_kv, HD)
        values_cache = values_cache.reshape(cache_rows, heads_kv, HD)
        keys_draft = keys_draft.reshape(local_rows, heads_kv, HD)
        values_draft = values_draft.reshape(local_rows, heads_kv, HD)
        query_blocks = queries.reshape(blocks, block_rows, heads_kv, group_size, HD)

        def one_block(block_data):
            query_block, position_block = block_data
            return partial_block(
                query_block,
                position_block,
                keys_cache,
                values_cache,
                keys_draft,
                values_draft,
                live_cache,
                draft_positions,
            )

        maxima, totals, weighted = lax.map(one_block, (query_blocks, position_blocks))
        return (
            maxima.reshape(all_rows, heads_q),
            totals.reshape(all_rows, heads_q),
            weighted.reshape(all_rows, heads_q * HD),
        )

    maxima, totals, weighted = lax.map(
        one_request, (gathered, cache_key, cache_value, draft_key, draft_value, cache_len)
    )
    shaped_max = maxima.reshape(requests, 1, all_rows, heads_q)
    shaped_tot = totals.reshape(requests, 1, all_rows, heads_q)
    shaped_sum = weighted.reshape(requests, 1, all_rows, heads_q * HD)
    block_max, block_tot, block_sum = (
        lax.all_to_all(shaped_max, "seq", split_axis=2, concat_axis=1, tiled=True),
        lax.all_to_all(shaped_tot, "seq", split_axis=2, concat_axis=1, tiled=True),
        lax.all_to_all(shaped_sum, "seq", split_axis=2, concat_axis=1, tiled=True),
    )
    overall_max = jnp.max(block_max, axis=1, keepdims=True)
    factors = jnp.exp(block_max - overall_max)
    block_sum = block_sum.reshape(requests, block_sum.shape[1], local_rows, heads_q, HD)
    numerator = jnp.sum(block_sum * factors[..., None], axis=1)
    denominator = jnp.sum(block_tot * factors, axis=1)
    attention = (
        (numerator / denominator[..., None])
        .reshape(requests, local_rows, heads_q * HD)
        .astype(jnp.bfloat16)
    )
    head_terms = jnp.einsum(
        "rtc,cd->rtd",
        lax.all_gather(attention, "seq", axis=1, tiled=True),
        out_weight,
        preferred_element_type=jnp.float32,
    )
    projected = lax.psum_scatter(head_terms, "head", scatter_dimension=1, tiled=True).astype(
        jnp.bfloat16
    )
    whole_keys, whole_values = (
        lax.all_gather(draft_key, "seq", axis=1, tiled=True),
        lax.all_gather(draft_value, "seq", axis=1, tiled=True),
    )
    offsets = cache_positions[None, :] - cache_len[:, None]
    chosen = (offsets >= 0) & (offsets < accepted[:, None])
    indices = jnp.clip(offsets, 0, all_rows - 1)
    select_rows = jax.vmap(lambda rows_all, index_row: rows_all[index_row])
    new_key = jnp.where(chosen[..., None], select_rows(whole_keys, indices), cache_key)
    new_value = jnp.where(chosen[..., None], select_rows(whole_values, indices), cache_value)
    return (projected, new_key, new_value)


def solution(mesh):
    in_specs = (
        P(None, "seq", "head"),
        P(None, "seq", "head"),
        P(None, "seq", "head"),
        P(None, "seq", "head"),
        P(None, "seq", "head"),
        P(),
        P(),
        P("head", "seq"),
    )
    out_specs = (P(None, "head", "seq"), P(None, "seq", "head"), P(None, "seq", "head"))
    return jax.shard_map(
        on_device, mesh=mesh, in_specs=in_specs, out_specs=out_specs, check_vma=False
    )
```

profile of v0, /device:TPU:0, one launch (start us, length us, event | category | flops | bytes accessed | tf_op | source)
XLA Modules:
  0.0 230.7 jit_solution(6076850852194880270)
XLA Ops:
  8.1 27.5 %all_gather.12 = bf16[1,96,4096]{2,0,1:T(2,128)(2,1)S(1)} all-gather(bf16[1,6,4096]{2,0,1:T(2,128)(2,1)S(1)} %copy.120), channel_id=1, replica_groups=mesh['seq'=16,'head'=2] {'seq'}, dimensions={1}, use_global_device_ids=true | all-gather | bytes 835584 | tf_op jit(solution)/shard_map/all_gather | solution.py:76
  35.6 4.8 %reduce.4 = bf16[96,4096]{1,0:T(8,128)(2,1)S(1)} reduce(bf16[1,96,4096]{2,0,1:T(2,128)(2,1)S(1)} %all_gather.12, bf16[]{:T(256)} %constant.99), dimensions={0}, to_apply=%all_gather.12.reduce_sub_computation | reduce | bytes 1572866 | tf_op jit(solution)/shard_map/all_gather | solution.py:76
  45.5 33.6 %while.26 = (s32[]{:T(128)}, f32[2,48,4,8]{1,0,3,2:T(2,128)S(1)}, f32[2,48,4,8]{1,0,3,2:T(2,128)S(1)}, f32[2,48,4,8,128]{4,3,2,1,0:T(8,128)}, bf16[2,48,4,8,128]...) while((s32[]{:T(128)}, f32[2,48,4,8]{1,0,3,2:T(2,128)S(1)}, ...), condition=%wide.region_5.6_spmd.clone, body=%wide.region_0.5_spmd.clone.sunk | while | flops 830750976 | bytes 26134152 | solution.py:106
  46.2 3.7 %fusion.52 = (f32[48,4,8]{2,0,1:T(8,128)S(1)}, f32[4,48,8,1024]{3,2,1,0:T(8,128)}) fusion(pred[1024]{0:T(1024)(128)(4,1)S(1)} %add_compare_fusion.2, bf16[1024,4,128]{2,0,1:T(8,128)(2,1)S(1)} %get-tuple-element.386, bf16[2,48,4,8,128]{4,3,2,1,0:T(8,128)(2,1)S(1)} %get-tuple-element.385, s32[]{:T(128)S(6)} %copy.198), kind=kOutput, calls=%fused_computation.6.clone.1 | convolution fusion | flops 407370240 | bytes 7740420 | tf_op jit(solution)/shard_map/while/body/eval_jaxpr/while/body/eval_jaxpr/qkgd,ckd->qkgc/dot_general | solution.py:35
  49.9 1.8 fusion.53
  52.4 3.6 %convert_reduce_fusion.4 = f32[48,4,8]{2,0,1:T(8,128)S(1)} fusion(f32[48,4,8]{2,0,1:T(8,128)S(1)} %max.24, f32[4,48,8,1024]{3,2,1,0:T(8,128)} %get-tuple-element.348, pred[1024]{0:T(1024)(128)(4,1)S(1)} %add_compare_fusion.2), kind=kLoop, calls=%fused_computation.10.clone.1 | loop fusion | flops 9435648 | bytes 6304768 | tf_op jit(solution)/shard_map/while/body/eval_jaxpr/while/body/eval_jaxpr/reduce_sum | solution.py:54
  56.4 4.3 %fusion.56 = f32[4,48,8,128]{3,2,1,0:T(8,128)S(1)} fusion(bf16[1024,4,128]{2,0,1:T(8,128)(2,1)} %get-tuple-element.389, f32[4,48,8,1024]{3,2,1,0:T(8,128)} %get-tuple-element.348, f32[48,4,8]{2,0,1:T(8,128)S(1)} %max.24, pred[1024]{0:T(1024)(128)(4,1)S(1)} %add_compare_fusion.2), kind=kOutput, calls=%fused_computation.13.clone.1 | convolution fusion | flops 408944640 | bytes 8133632 | tf_op jit(solution)/shard_map/while/body/eval_jaxpr/while/body/eval_jaxpr/qkgc,ckd->qkgd/dot_general | solution.py:57
  63.0 3.7 %fusion.52 = (f32[48,4,8]{2,0,1:T(8,128)S(1)}, f32[4,48,8,1024]{3,2,1,0:T(8,128)}) fusion(pred[1024]{0:T(1024)(128)(4,1)S(1)} %add_compare_fusion.2, bf16[1024,4,128]{2,0,1:T(8,128)(2,1)S(1)} %get-tuple-element.386, bf16[2,48,4,8,128]{4,3,2,1,0:T(8,128)(2,1)S(1)} %get-tuple-element.385, s32[]{:T(128)S(6)} %copy.198), kind=kOutput, calls=%fused_computation.6.clone.1 | convolution fusion | flops 407370240 | bytes 7740420 | tf_op jit(solution)/shard_map/while/body/eval_jaxpr/while/body/eval_jaxpr/qkgd,ckd->qkgc/dot_general | solution.py:35
  66.7 1.8 fusion.53
  69.2 3.6 %convert_reduce_fusion.4 = f32[48,4,8]{2,0,1:T(8,128)S(1)} fusion(f32[48,4,8]{2,0,1:T(8,128)S(1)} %max.24, f32[4,48,8,1024]{3,2,1,0:T(8,128)} %get-tuple-element.348, pred[1024]{0:T(1024)(128)(4,1)S(1)} %add_compare_fusion.2), kind=kLoop, calls=%fused_computation.10.clone.1 | loop fusion | flops 9435648 | bytes 6304768 | tf_op jit(solution)/shard_map/while/body/eval_jaxpr/while/body/eval_jaxpr/reduce_sum | solution.py:54
  73.2 4.3 %fusion.56 = f32[4,48,8,128]{3,2,1,0:T(8,128)S(1)} fusion(bf16[1024,4,128]{2,0,1:T(8,128)(2,1)} %get-tuple-element.389, f32[4,48,8,1024]{3,2,1,0:T(8,128)} %get-tuple-element.348, f32[48,4,8]{2,0,1:T(8,128)S(1)} %max.24, pred[1024]{0:T(1024)(128)(4,1)S(1)} %add_compare_fusion.2), kind=kOutput, calls=%fused_computation.13.clone.1 | convolution fusion | flops 408944640 | bytes 8133632 | tf_op jit(solution)/shard_map/while/body/eval_jaxpr/while/body/eval_jaxpr/qkgc,ckd->qkgd/dot_general | solution.py:57
  81.3 5.8 %all-to-all-start.2 = ((f32[16,1,192]{2,1,0:T(1,128)}), f32[16,1,192]{2,1,0:T(1,128)S(1)}, u32[]{:S(2)}, u32[]{:S(2)}) async-start(f32[16,1,192]{2,1,0:T(1,128)} %reshape.322), calls=%async_computation.2 | async-start | bytes 32768 | tf_op jit(solution)/shard_map/all_to_all | solution.py:121
  88.2 5.4 %all-to-all-done.2 = f32[16,1,192]{2,1,0:T(1,128)S(1)} async-done(((f32[16,1,192]{2,1,0:T(1,128)}), f32[16,1,192]{2,1,0:T(1,128)S(1)}, u32[]{:S(2)}, u32[]{:S(2)}) %all-to-all-start.2) | async-done | bytes 12320 | tf_op jit(solution)/shard_map/all_to_all | solution.py:121
  93.6 9.1 %all_to_all.39 = f32[16,1,192]{2,1,0:T(1,128)S(1)} all-to-all(f32[16,1,192]{2,1,0:T(1,128)S(1)} %reshape.324), channel_id=1, replica_groups=mesh['seq'=16,'head'=2] {'seq'}, dimensions={0} | all-to-all | bytes 24576 | tf_op jit(solution)/shard_map/all_to_all | solution.py:120
  102.7 3.7 %all-to-all-start = ((f32[1,1,96,4096]{3,1,0,2:T(1,128)}), f32[1,1,96,4096]{3,1,0,2:T(1,128)S(1)}, u32[]{:S(2)}, u32[]{:S(2)}) async-start(f32[1,1,96,4096]{3,1,0,2:T(1,128)} %bitcast.148), calls=%async_computation | async-start | bytes 3145728 | tf_op jit(solution)/shard_map/all_to_all | solution.py:122
  107.8 42.1 %all_gather.15 = bf16[1,96,512]{2,0,1:T(2,128)(2,1)S(1)} all-gather(bf16[1,6,512]{2,0,1:T(2,128)(2,1)S(1)} %copy.137), channel_id=1, replica_groups=mesh['seq'=16,'head'=2] {'seq'}, dimensions={1}, use_global_device_ids=true | all-gather | bytes 104448 | tf_op jit(solution)/shard_map/all_gather | solution.py:145
  153.7 3.3 %multiply_reduce_fusion = f32[6,4096]{1,0:T(8,128)S(1)} fusion(f32[1,1,16,6,4096]{4,1,3,2,0:T(1,128)S(1)} %bitcast.143, f32[1,1,16,6,4096]{4,1,3,2,0:T(1,128)S(1)} %bitcast.144), kind=kLoop, calls=%fused_computation.38 | loop fusion | flops 761856 | bytes 3244032 | tf_op jit(solution)/shard_map/reduce_sum | solution.py:127
  157.1 29.5 %all_gather.13 = bf16[1,96,4096]{2,0,1:T(2,128)(2,1)S(1)} all-gather(bf16[1,6,4096]{2,0,1:T(2,128)(2,1)S(1)} %copy.134), channel_id=1, replica_groups=mesh['seq'=16,'head'=2] {'seq'}, dimensions={1}, use_global_device_ids=true | all-gather | bytes 835584 | tf_op jit(solution)/shard_map/all_gather | solution.py:136
  186.6 1.8 convolution_bitcast_fusion
  188.4 18.6 %all_gather.14 = bf16[1,96,512]{2,0,1:T(2,128)(2,1)S(1)} all-gather(bf16[1,6,512]{2,0,1:T(2,128)(2,1)S(1)} %copy.135), channel_id=1, replica_groups=mesh['seq'=16,'head'=2] {'seq'}, dimensions={1}, use_global_device_ids=true | all-gather | bytes 104448 | tf_op jit(solution)/shard_map/all_gather | solution.py:144
  207.1 6.1 %gather_fusion.1 = bf16[1024,512]{1,0:T(8,128)(2,1)S(1)} fusion(bf16[1,96,512]{2,1,0:T(8,128)(2,1)S(1)} %copy.138, s32[1024]{0:T(1024)S(1)} %bitcast.139), kind=kCustom, calls=%fused_computation.1 | custom fusion | bytes 2105344 | tf_op jit(solution)/shard_map/vmap()/gather | solution.py:150
  213.2 6.1 %gather_fusion = bf16[1024,512]{1,0:T(8,128)(2,1)S(1)} fusion(bf16[1,96,512]{2,1,0:T(8,128)(2,1)S(1)} %copy.136, s32[1024]{0:T(1024)S(1)} %bitcast.140), kind=kCustom, calls=%fused_computation | custom fusion | bytes 2105344 | tf_op jit(solution)/shard_map/vmap()/gather | solution.py:150
  219.4 2.9 %bitcast_select_fusion.2 = (bf16[1,1024,512]{2,1,0:T(8,128)(2,1)}, bf16[1,1024,512]{2,1,0:T(8,128)(2,1)}) fusion(bf16[1,1024,512]{2,1,0:T(8,128)(2,1)} %param.14, bf16[1024,512]{1,0:T(8,128)(2,1)S(1)} %gather_fusion.1, pred[1024]{0:T(1024)(128)(4,1)S(1)} %fusion.32, bf16[1,1024,512]{2,1,0:T(8,128)(2,1)S(1)} %copy-done.1, bf16[1024,512]{1,0:T(8,128)(2,1)S(1)} %gather_fusion), kind=kLoop, calls=%fused_computation.40 | loop fusion | flops 1048576 | bytes 6292480 | tf_op jit(solution)/shard_map/jit(_where)/select_n | solution.py:152
  222.3 1.5 convert_element_type.27
  (92 shorter events, 19.5 us)
Async XLA Ops:
  40.5 5.0 %copy-start.2 = (bf16[1,6,512]{2,1,0:T(8,128)(2,1)S(1)}, bf16[1,6,512]{2,1,0:T(8,128)(2,1)}, u32[]{:S(2)}) copy-start(bf16[1,6,512]{2,1,0:T(8,128)(2,1)} %param.12) | copy-start | bytes 18436
  40.5 5.0 %copy-start.3 = (bf16[1,6,512]{2,1,0:T(8,128)(2,1)S(1)}, bf16[1,6,512]{2,1,0:T(8,128)(2,1)}, u32[]{:S(2)}) copy-start(bf16[1,6,512]{2,1,0:T(8,128)(2,1)} %param.11) | copy-start | bytes 18436
  81.3 12.3 %all-to-all-start.2 = ((f32[16,1,192]{2,1,0:T(1,128)}), f32[16,1,192]{2,1,0:T(1,128)S(1)}, u32[]{:S(2)}, u32[]{:S(2)}) async-start(f32[16,1,192]{2,1,0:T(1,128)} %reshape.322), calls=%async_computation.2 | async-start | bytes 32768 | tf_op jit(solution)/shard_map/all_to_all | solution.py:121
  102.7 50.5 %all-to-all-start = ((f32[1,1,96,4096]{3,1,0,2:T(1,128)}), f32[1,1,96,4096]{3,1,0,2:T(1,128)S(1)}, u32[]{:S(2)}, u32[]{:S(2)}) async-start(f32[1,1,96,4096]{3,1,0,2:T(1,128)} %bitcast.148), calls=%async_computation | async-start | bytes 3145728 | tf_op jit(solution)/shard_map/all_to_all | solution.py:122
  106.4 115.9 %reduce-scatter.2.cloned.1.call-start = ((), (), s32[]{:S(2)}) async-start(), calls=%async_computation.4 | async-start | bytes 294912 | tf_op jit(solution)/shard_map/reduce_scatter | solution.py:140
  153.2 33.4 %copy-start = (bf16[4096,512]{1,0:T(8,128)(2,1)S(1)}, bf16[4096,512]{1,0:T(8,128)(2,1)}, u32[]{:S(2)}) copy-start(bf16[4096,512]{1,0:T(8,128)(2,1)} %param.17) | copy-start | bytes 12582916
  213.2 6.2 %copy-start.1 = (bf16[1,1024,512]{2,1,0:T(8,128)(2,1)S(1)}, bf16[1,1024,512]{2,1,0:T(8,128)(2,1)}, u32[]{:S(2)}) copy-start(bf16[1,1024,512]{2,1,0:T(8,128)(2,1)} %param.13) | copy-start | bytes 3145732
Sparse Core Ops, SparseCore 0:
  188.5 10.0 reduce-scatter.1
where the time goes:
time: 231 us
  blocking collectives  127 us (55%)
  local copies, waits for them, and re-layouts  26.4 us (11%)
  other arithmetic  24.6 us (11%)
  matrix products  22.1 us (10%)
  between operations  15.6 us (7%)
  starting transfers between devices  9.57 us (4%)
  waiting for transfers between devices  5.45 us (2%)
    all_gather x1, blocking collectives, on_device(): lax.all_gather(draft_value, 'seq', axis=1, tiled=True)  42.1 us
    all_gather x1, blocking collectives, on_device(): lax.all_gather(attention, 'seq', axis=1, tiled=True)  29.5 us
    all_gather x1, blocking collectives, on_device(): gathered = lax.all_gather(draft_query, 'seq', axis=1, tiled=True)  27.5 us
    all_gather x1, blocking collectives, on_device(): lax.all_gather(draft_key, 'seq', axis=1, tiled=True)  18.6 us
    gather x3, local copies, waits for them, and re-layouts, on_device(): select_rows = jax.vmap(lambda rows_all, index_row: rows_all[index_row])  12.3 us
    all_to_all x1, blocking collectives, on_device(): lax.all_to_all(shaped_max, 'seq', split_axis=2, concat_axis=1, tiled=True)  9.06 us
    dot_general x2, matrix products, partial_block(): jnp.einsum('qkgc,ckd->qkgd', cache_probs, values_cache, preferred_element...  8.67 us
    unnamed x21, local copies, waits for them, and re-layouts  7.58 us
  transfers between devices with their start and end apart: 3, of which 1 were waited for; matrix products, arithmetic and copies ran while one was open for 8% of the time, Pallas kernels for 0%

commit v1 on v0

v1 whole, which is shorter than its diff:
```python
import functools
import math

import jax
import jax.numpy as jnp
from jax import lax
from jax.experimental import pallas as pl
from jax.experimental.pallas import tpu as pltpu
from jax.sharding import PartitionSpec as P

QH = 64
KVH = 8
HD = 128
GROUP = QH // KVH
LANES = 128

DEAD = -1e30
FLOOR = -1e29
LOG2_SCALE = math.log2(math.e) / math.sqrt(HD)
VMEM_BYTES = 48 * 1024 * 1024

bf16 = jnp.bfloat16
f32 = jnp.float32


def round_up(n, m):
    return -(-n // m) * m


def stat_rows(units):
    return round_up(3 * round_up(units, 8), 16)


def pad_rows(x, rows):
    if x.shape[0] == rows:
        return x
    return jnp.concatenate([x, jnp.zeros((rows - x.shape[0], x.shape[1]), x.dtype)], axis=0)


def columns_to_rows(columns, unit):
    lane = lax.broadcasted_iota(jnp.int32, (unit, LANES), 1)
    square = jnp.zeros((unit, LANES), f32)
    for place, column in columns:
        square = jnp.where(lane == place, column, square)
    return jnp.transpose(pad_rows(square, LANES))


def split_total(total):
    high = total.astype(bf16)
    return high, (total - high.astype(f32)).astype(bf16)


def write_message(out_ref, row, shift, total):
    high, low = split_total(total)
    rows = jnp.concatenate([shift, high.astype(f32), low.astype(f32)], axis=0)
    out_ref[row : row + stat_rows(shift.shape[0]), :] = pad_rows(
        rows, stat_rows(shift.shape[0])
    ).astype(bf16)


def attend_kernel(rel, unit_rows, split, as_message, scal, q_ref, k_ref, v_ref, *rest):
    if split == 2:
        kv_ref, d_ref, *outs = rest
    else:
        d_ref, *outs = rest
    units, heads, unit, _ = q_ref.shape
    keys = k_ref.shape[0]
    seq, length = scal[0], scal[1]
    chip = lax.div(seq, split)
    count = units * heads
    count8 = round_up(count, 8)
    step = max(n for n in range(1, units + 1) if units % n == 0 and n * unit <= 384)
    columns = []
    out_ref = outs[0]
    key_index = lax.broadcasted_iota(jnp.int32, (1, keys), 1)
    for head in range(heads):
        lanes = slice(head * HD, (head + 1) * HD)
        pieces = [(k_ref[:, lanes], v_ref[:, lanes], key_index + seq * keys < length)]
        if split == 2:
            values = slice((heads + head) * HD, (heads + head + 1) * HD)
            other = seq + 1 - 2 * lax.rem(seq, 2)
            pieces.append(
                (kv_ref[:, lanes], kv_ref[:, values], key_index + other * keys < length)
            )
        for start in range(0, units, step):
            rows = step * unit
            queries = q_ref[start : start + step, head].reshape(rows, HD)
            time = jnp.concatenate(
                [
                    lax.shift_right_logical(lax.broadcasted_iota(jnp.int32, (unit, LANES), 0), 3)
                    + unit_rows * jnp.bitwise_xor(chip, rel[start + n])
                    for n in range(step)
                ],
                axis=0,
            )
            draft = lax.broadcasted_iota(jnp.int32, (rows, LANES), 1)
            causal = (draft < unit_rows) & (draft + unit_rows * chip <= time)
            scores, rhs = [], []
            for keys_piece, values_piece, live in pieces + [
                (d_ref[head, :LANES], d_ref[head, LANES:], causal)
            ]:
                score = lax.dot_general(
                    queries, keys_piece, (((1,), (1,)), ((), ())), preferred_element_type=f32
                )
                scores.append(jnp.where(live, score * LOG2_SCALE, DEAD))
                rhs.append(values_piece)
            top = functools.reduce(
                jnp.maximum, [jnp.max(s, axis=1, keepdims=True) for s in scores]
            )
            shift = jnp.maximum(top, FLOOR).astype(bf16).astype(f32)
            probs = [jnp.exp2(s - shift).astype(bf16) for s in scores]
            total = sum(jnp.sum(p.astype(f32), axis=1, keepdims=True) for p in probs)
            weighted = sum(
                jnp.dot(p, v, preferred_element_type=f32) for p, v in zip(probs, rhs)
            )
            for n in range(step):
                place = (start + n) * heads + head
                part = slice(n * unit, (n + 1) * unit)
                out_ref[place * unit : (place + 1) * unit, :] = weighted[part].astype(out_ref.dtype)
                columns.append((place, shift[part]))
                columns.append((count8 + place, total[part]))
    stats = columns_to_rows(columns, unit)
    if as_message:
        write_message(out_ref, count * unit, stats[:count8], stats[count8 : 2 * count8])
    else:
        outs[1][...] = stats[: 2 * count8]


def attend(scal, q, rel, unit_rows, split, cache_k, cache_v, kv_other, drafts, as_message):
    units, heads, unit, _ = q.shape
    keys = cache_k.shape[0]
    count = units * heads
    if as_message:
        out_shape = jax.ShapeDtypeStruct((count * unit + stat_rows(count), LANES), bf16)
        out_specs = pl.BlockSpec(out_shape.shape, lambda i, s: (0, 0))
    else:
        out_shape = (
            jax.ShapeDtypeStruct((count * unit, LANES), f32),
            jax.ShapeDtypeStruct((2 * round_up(count, 8), LANES), f32),
        )
        out_specs = tuple(pl.BlockSpec(o.shape, lambda i, s: (0, 0)) for o in out_shape)
    cache_spec = pl.BlockSpec((keys, heads * HD), lambda i, s: (0, lax.rem(s[0], split)))
    in_specs = [pl.BlockSpec(q.shape, lambda i, s: (0, 0, 0, 0)), cache_spec, cache_spec]
    operands = [q, cache_k, cache_v]
    if split == 2:
        in_specs.append(pl.BlockSpec(kv_other.shape, lambda i, s: (0, 0)))
        operands.append(kv_other)
    in_specs.append(pl.BlockSpec(drafts.shape, lambda i, s: (0, 0, 0)))
    operands.append(drafts)
    scores = count * unit * (split * keys + LANES)
    return pl.pallas_call(
        functools.partial(attend_kernel, rel, unit_rows, split, as_message),
        grid_spec=pltpu.PrefetchScalarGridSpec(
            num_scalar_prefetch=1, grid=(1,), in_specs=in_specs, out_specs=out_specs
        ),
        out_shape=out_shape,
        compiler_params=pltpu.CompilerParams(vmem_limit_bytes=VMEM_BYTES),
        cost_estimate=pl.CostEstimate(
            flops=4 * scores * HD, bytes_accessed=4 * split * keys * heads * HD, transcendentals=scores
        ),
    )(scal, *operands)


def merge_kernel(unit, mode, num_ref, stat_ref, msg_ref, *outs):
    rows = num_ref.shape[0]
    count = rows // unit
    count8 = stat_ref.shape[0] // 2
    own_shift, own_total = stat_ref[:count8], stat_ref[count8:]
    sent = msg_ref[rows:, :].astype(f32)
    shift = sent[:count8]
    total = sent[count8 : 2 * count8] + sent[2 * count8 : 3 * count8]
    half = count // 2
    if mode == "final":
        shift = pad_rows(jnp.concatenate([shift[half:count], shift[:half]], axis=0), count8)
        total = pad_rows(jnp.concatenate([total[half:count], total[:half]], axis=0), count8)
    new_shift = jnp.maximum(own_shift, shift)
    own_factor = jnp.exp2(own_shift - new_shift)
    factor = jnp.exp2(shift - new_shift)
    new_total = own_total * own_factor + total * factor
    if mode == "final":
        new_total = jnp.where(new_total > 0, new_total, 1.0)
        own_factor = own_factor / new_total
        factor = factor / new_total
    factors = jnp.transpose(pad_rows(jnp.concatenate([own_factor, factor], axis=0), LANES))
    for n in range(count):
        source = (n + half) % count if mode == "final" else n
        merged = num_ref[n * unit : (n + 1) * unit, :] * factors[:unit, n : n + 1]
        merged = merged + (
            msg_ref[source * unit : (source + 1) * unit, :].astype(f32)
            * factors[:unit, count8 + n : count8 + n + 1]
        )
        here = slice(n * unit, (n + 1) * unit)
        if mode == "final":
            outs[0][here, :] = merged.astype(bf16)
        elif mode == "all":
            outs[0][here, :] = merged
            outs[2][here, :] = merged.astype(bf16)
        elif n < half:
            outs[0][here, :] = merged
        else:
            outs[2][(n - half) * unit : (n - half + 1) * unit, :] = merged.astype(bf16)
    if mode == "all":
        outs[1][...] = jnp.concatenate([new_shift, new_total], axis=0)
        write_message(outs[2], rows, new_shift, new_total)
    elif mode == "half":
        half8 = round_up(half, 8)
        outs[1][...] = jnp.concatenate(
            [pad_rows(new_shift[:half], half8), pad_rows(new_total[:half], half8)], axis=0
        )
        write_message(
            outs[2],
            half * unit,
            pad_rows(new_shift[half:count], half8),
            pad_rows(new_total[half:count], half8),
        )


def merge(unit, mode, num, stats, message):
    rows = num.shape[0]
    if mode == "final":
        out_shape = jax.ShapeDtypeStruct((rows, LANES), bf16)
    else:
        rows = rows // 2 if mode == "half" else rows
        count = rows // unit
        out_shape = (
            jax.ShapeDtypeStruct((rows, LANES), f32),
            jax.ShapeDtypeStruct((2 * round_up(count, 8), LANES), f32),
            jax.ShapeDtypeStruct((rows + stat_rows(count), LANES), bf16),
        )
    return pl.pallas_call(
        functools.partial(merge_kernel, unit, mode),
        out_shape=out_shape,
        compiler_params=pltpu.CompilerParams(vmem_limit_bytes=VMEM_BYTES),
    )(num, stats, message)


def project_kernel(rel, split, n_head, scal, *refs):
    sources = refs[: 2 * split]
    w_ref = refs[2 * split]
    outs = refs[2 * split + 1 : -2]
    rows_ref, lhs_ref = refs[-2:]
    seq, head = scal[0], scal[2]
    chip = lax.div(seq, split)
    core = lax.rem(seq, split)
    heads_kv = rows_ref.shape[0]
    units, heads, unit, _ = sources[0].shape
    chips = 2 * units
    first = head * (chips // n_head) if n_head == 2 else 0
    for side in range(split):
        owner = core if side == 0 else 1 - core
        for part in range(2):
            x_ref = sources[2 * side + part]
            for n in range(units):
                place = lax.rem(jnp.bitwise_xor(chip, rel[part][n]) - first + chips, chips)
                for h in range(heads):
                    rows_ref[
                        owner * heads + h, pl.ds(pl.multiple_of(place * unit, unit), unit), :
                    ] = x_ref[n, h].astype(f32)
    rows = lhs_ref.shape[0]
    for kv in range(heads_kv):
        for g in range(GROUP):
            lanes = slice((kv * GROUP + g) * HD, (kv * GROUP + g + 1) * HD)
            lhs_ref[:, lanes] = rows_ref[kv, pl.ds(g, rows, stride=GROUP), :].astype(bf16)
    result = jnp.dot(lhs_ref[...], w_ref[...], preferred_element_type=f32)
    if n_head == 2:
        outs[0][...] = result[: rows // 2]
        outs[1][...] = result[rows // 2 :]
    else:
        outs[0][...] = result


def project(scal, rel, split, n_head, sources, weight):
    units, heads, unit, _ = sources[0].shape
    heads_kv = heads * split
    rows = 2 * units * unit // GROUP
    columns = weight.shape[1]
    if n_head == 2:
        out_shape = (jax.ShapeDtypeStruct((rows // 2, columns), f32),) * 2
    else:
        out_shape = (jax.ShapeDtypeStruct((rows, columns), f32),)
    return pl.pallas_call(
        functools.partial(project_kernel, rel, split, n_head),
        in_specs=[pl.BlockSpec(memory_space=pltpu.SMEM)]
        + [pl.BlockSpec(memory_space=pltpu.VMEM)] * (2 * split + 1),
        out_shape=out_shape,
        scratch_shapes=[
            pltpu.VMEM((heads_kv, 2 * units * unit, LANES), f32),
            pltpu.VMEM((rows, heads_kv * GROUP * HD), bf16),
        ],
        compiler_params=pltpu.CompilerParams(vmem_limit_bytes=VMEM_BYTES),
    )(scal, *sources, weight)


def one_request(n_seq, n_head, dq, dk, dv, ck, cv, accepted, length, weight):
    seq = lax.axis_index("seq")
    local_rows = dq.shape[0]
    heads_kv = dk.shape[1] // HD
    cache_rows = ck.shape[0]
    split = 2 if heads_kv % 2 == 0 else 1
    heads = heads_kv // split
    unit_rows = local_rows * split
    unit = unit_rows * GROUP
    n_bits = n_seq.bit_length() - 1
    bits = list(range(n_bits - 1, split - 2, -1))

    def swap(x, bit):
        return lax.ppermute(x, "seq", [(i, i ^ (1 << bit)) for i in range(n_seq)])

    scal = jnp.stack([seq, length, lax.axis_index("head")]).astype(jnp.int32)
    chip = seq // split
    core = seq % split

    q4 = dq.reshape(local_rows, heads_kv, GROUP * HD // LANES, LANES).transpose(1, 0, 2, 3)
    q4 = q4.reshape(heads_kv, local_rows * GROUP, LANES)
    dk4 = dk.reshape(local_rows, heads_kv, HD).transpose(1, 0, 2)
    dv4 = dv.reshape(local_rows, heads_kv, HD).transpose(1, 0, 2)
    pack = jnp.concatenate([q4, dk4, dv4], axis=1)
    kv_other = None
    if split == 2:
        mine = lax.dynamic_slice_in_dim(pack, core * heads, heads, 0)
        recv = swap(lax.dynamic_slice_in_dim(pack, (1 - core) * heads, heads, 0), 0)
        parts = [jnp.where(core == 0, mine, recv), jnp.where(core == 0, recv, mine)]
        width = heads * HD
        kv_other = swap(
            jnp.concatenate(
                [
                    lax.dynamic_slice_in_dim(ck, (1 - core) * width, width, 1),
                    lax.dynamic_slice_in_dim(cv, (1 - core) * width, width, 1),
                ],
                axis=1,
            ),
            0,
        )
    else:
        parts = [pack]
    cut = local_rows * GROUP
    q = jnp.concatenate([p[:, :cut] for p in parts], axis=1)[None]
    d_key = jnp.concatenate([p[:, cut : cut + local_rows] for p in parts], axis=1)
    d_value = jnp.concatenate([p[:, cut + local_rows :] for p in parts], axis=1)
    spare = ((0, 0), (0, LANES - unit_rows), (0, 0))
    drafts = jnp.concatenate([jnp.pad(d_key, spare), jnp.pad(d_value, spare)], axis=1)

    rel = [0]
    for bit in bits[:-1]:
        q = jnp.concatenate([q, swap(q, bit)], axis=0)
        rel = rel + [r | (1 << bit) // split for r in rel]
    near = bits[-1]
    rel_far = [r | (1 << near) // split for r in rel]
    q_far = swap(q, near)

    run = functools.partial(attend, scal)
    message = run(q, rel, unit_rows, split, ck, cv, kv_other, drafts, True)
    num, stats = run(q_far, rel_far, unit_rows, split, ck, cv, kv_other, drafts, False)
    message = swap(message, near)
    for bit in reversed(bits[:-1]):
        mode = "all" if bit == bits[0] else "half"
        num, stats, message = merge(unit, mode, num, stats, message)
        message = swap(message, bit)
    att = merge(unit, "final", num, stats, message).reshape(-1, heads, unit, LANES)
    for bit in bits[1:-1]:
        att = jnp.concatenate([att, swap(att, bit)], axis=0)
    att_near = swap(att, near)
    sources = [att, att_near]
    if split == 2:
        sources += [swap(att, 0), swap(att_near, 0)]
    result = project(scal, (rel_far, rel), split, n_head, sources, weight)
    if n_head == 2:
        keep, send = result
        projected = keep + lax.ppermute(send, "head", [(0, 1), (1, 0)])
    else:
        projected = lax.psum_scatter(result[0], "head", scatter_dimension=0, tiled=True)

    dkv = jnp.concatenate([d_key, d_value], axis=1)[None]
    for bit in bits:
        dkv = jnp.concatenate([dkv, swap(dkv, bit)], axis=0)
    if split == 2:
        other = swap(dkv, 0)
        dkv = jnp.concatenate(
            [jnp.where(core == 0, dkv, other), jnp.where(core == 0, other, dkv)], axis=1
        )
    every = jnp.asarray(rel + rel_far, jnp.int32)
    source = (chip ^ every)[:, None] * unit_rows + jnp.arange(unit_rows, dtype=jnp.int32)
    source = source.reshape(-1)
    place = seq * cache_rows + jnp.arange(cache_rows, dtype=jnp.int32) - length
    pick = (place[:, None] == source[None, :]) & (source < accepted)[None, :]
    chosen = ((place >= 0) & (place < accepted))[:, None]

    def append(cache, rows):
        rows = rows.transpose(0, 2, 1, 3).reshape(-1, heads_kv * HD)
        moved = jnp.dot(pick.astype(bf16), rows, preferred_element_type=f32).astype(bf16)
        return jnp.where(chosen, moved, cache)

    new_key = append(ck, dkv[:, :, :unit_rows])
    new_value = append(cv, dkv[:, :, unit_rows:])
    return projected.astype(bf16), new_key, new_value


def on_device(n_seq, n_head, dq, dk, dv, ck, cv, accepted, cache_len, weight):
    results = [
        one_request(
            n_seq, n_head, dq[r], dk[r], dv[r], ck[r], cv[r], accepted[r], cache_len[r], weight
        )
        for r in range(dq.shape[0])
    ]
    return tuple(jnp.stack(parts) for parts in zip(*results))


def solution(mesh):
    in_specs = (
        P(None, "seq", "head"),
        P(None, "seq", "head"),
        P(None, "seq", "head"),
        P(None, "seq", "head"),
        P(None, "seq", "head"),
        P(),
        P(),
        P("head", "seq"),
    )
    out_specs = (P(None, "head", "seq"), P(None, "seq", "head"), P(None, "seq", "head"))
    return jax.shard_map(
        functools.partial(on_device, mesh.shape["seq"], mesh.shape["head"]),
        mesh=mesh,
        in_specs=in_specs,
        out_specs=out_specs,
        check_vma=False,
    )
```

time: 231 us -> 64.2 us (0.28)
  blocking collectives: 127 us -> 0 us
  local copies, waits for them, and re-layouts: 26.4 us -> 2.34 us
  other arithmetic: 24.6 us -> 2.78 us
  matrix products: 22.1 us -> 3.81 us
  waiting for transfers between devices: 5.45 us -> 21.7 us
  between operations: 15.6 us -> 2.2 us
  Pallas kernels: 0 us -> 11 us
  starting transfers between devices: 9.57 us -> 20.1 us
    all_gather x4 -> x0, blocking collectives: 118 us -> none  [the longest x1 42.1 us: on_device(): lax.all_gather(draft_value, 'seq', axis=1, tiled=True)]
    ppermute x0 -> x17, waiting for transfers between devices: none -> 21.7 us  [the longest x16 19.9 us: swap(): return lax.ppermute(x, 'seq', [(i, i ^ 1 << bit) for i in range(n_seq)])]
    ppermute x0 -> x17, starting transfers between devices: none -> 20.1 us  [the longest x16 18.5 us: swap(): return lax.ppermute(x, 'seq', [(i, i ^ 1 << bit) for i in range(n_seq)])]
    dot_general x9 -> x2, matrix products: 22.1 us -> 3.81 us  [append(): jnp.dot(pick.astype(bf16), rows, preferred_element_type=f32).astype(bf16)]
    gather x3 -> x0, local copies, waits for them, and re-layouts: 12.3 us -> none  [on_device(): select_rows = jax.vmap(lambda rows_all, index_row: rows_all[index_row])]
    pallas_call x0 -> x6, Pallas kernels: none -> 11 us  [the longest x2 8.46 us: attend(): pl.pallas_call(functools.partial(attend_kernel, rel, unit_rows, split, as...]
    reduce_sum x6 -> x0, other arithmetic: 10.8 us -> none  [the longest x2 7.28 us: partial_block(): jnp.sum(cache_probs.astype(jnp.float32), axis=-1)]
    all_to_all x2 -> x0, starting transfers between devices: 9.53 us -> none  [the longest x1 5.82 us: on_device(): lax.all_to_all(shaped_tot, 'seq', split_axis=2, concat_axis=1, tiled=True)]
  transfers between devices with their start and end apart: 3 -> 17, of which waited for: 1 -> 8; matrix products, arithmetic and copies ran while one was open for 8% -> 10% of each run, Pallas kernels for 0% -> 15%
where the time goes in v1:
time: 64.2 us; the launch traced here: 63.9 us
  waiting for transfers between devices  21.7 us (34%)
  starting transfers between devices  20.1 us (31%)
  Pallas kernels  11 us (17%)
  matrix products  3.81 us (6%)
  other arithmetic  2.78 us (4%)
  local copies, waits for them, and re-layouts  2.34 us (4%)
  between operations  2.2 us (3%)
    ppermute x16, waiting for transfers between devices, swap(): return lax.ppermute(x, 'seq', [(i, i ^ 1 << bit) for i in range(n_seq)])  19.9 us
    ppermute x16, starting transfers between devices, swap(): return lax.ppermute(x, 'seq', [(i, i ^ 1 << bit) for i in range(n_seq)])  18.5 us
    pallas_call x2, Pallas kernels, attend(): pl.pallas_call(functools.partial(attend_kernel, rel, unit_rows, split, as...  8.46 us
    dot_general x2, matrix products, append(): jnp.dot(pick.astype(bf16), rows, preferred_element_type=f32).astype(bf16)  3.81 us
    ppermute x1, waiting for transfers between devices, one_request(): projected = keep + lax.ppermute(send, 'head', [(0, 1), (1, 0)])  1.76 us
    ppermute x1, starting transfers between devices, one_request(): projected = keep + lax.ppermute(send, 'head', [(0, 1), (1, 0)])  1.62 us
    pallas_call x1, Pallas kernels, project(): pl.pallas_call(functools.partial(project_kernel, rel, split, n_head), in_...  1.53 us
  transfers between devices with their start and end apart: 17, of which 8 were waited for; matrix products, arithmetic and copies ran while one was open for 10% of the time, Pallas kernels for 15%

profile of v1, /device:TPU:0, one launch (start us, length us, event | category | flops | bytes accessed | tf_op | source)
XLA Modules:
  0.0 63.9 jit_solution(17094023141931060926)
XLA Ops:
  0.6 0.8 %copy_bitcast_fusion.1 = bf16[4,48,128]{2,1,0:T(8,128)(2,1)S(1)} fusion(bf16[1,6,32,128]{3,1,2,0:T(8,128)(2,1)} %bitcast.65), kind=kLoop, calls=%fused_computation.46 | loop fusion | bytes 98304 | tf_op jit(solution)/shard_map/reshape | solution.py:314
  1.5 0.7 %pad_maximum_fusion.7 = bf16[4,60,128]{2,1,0:T(8,128)(2,1)S(1)} fusion(bf16[4,6,128]{2,1,0:T(8,128)(2,1)} %bitcast.66, bf16[4,6,128]{2,1,0:T(8,128)(2,1)} %bitcast.67, bf16[4,48,128]{2,1,0:T(8,128)(2,1)S(1)} %copy_bitcast_fusion.1), kind=kLoop, calls=%fused_computation.41 | loop fusion | flops 184320 | bytes 122880 | tf_op jit(solution)/shard_map/concatenate | solution.py:317
  2.8 1.3 %dynamic-slice_bitcast_fusion = (bf16[1024,256]{1,0:T(8,128)(2,1)S(1)}, bf16[1024,256]{1,0:T(8,128)(2,1)S(1)}) fusion(bf16[1,1024,512]{2,1,0:T(8,128)(2,1)} %param.13, s32[]{:T(128)S(6)} %select_n.58, bf16[1,1024,512]{2,1,0:T(8,128)(2,1)} %param.12), kind=kLoop, calls=%fused_computation.7 | loop fusion | bytes 2097156 | tf_op jit(solution)/shard_map/dynamic_slice | solution.py:328
  4.1 1.1 %pad_maximum_fusion = bf16[1024,512]{1,0:T(8,128)(2,1)} fusion(bf16[1024,256]{1,0:T(8,128)(2,1)S(1)} %get-tuple-element.35, bf16[1024,256]{1,0:T(8,128)(2,1)S(1)} %get-tuple-element.36), kind=kLoop, calls=%fused_computation.6 | loop fusion | flops 2097152 | bytes 2097152 | tf_op jit(solution)/shard_map/concatenate | solution.py:325
  6.8 4.1 %collective-permute-start.1 = (bf16[1,2,96,128]{3,2,1,0:T(8,128)(2,1)S(1)}, bf16[1,2,96,128]{3,2,1,0:T(8,128)(2,1)S(1)}, u32[]{:S(2)}, u32[]{:S(2)}) collective-permute-start(bf16[1,2,96,128]{3,2,1,0:T(8,128)(2,1)S(1)} %maximum_bitcast_fusion), channel_id=1, source_target_pairs={{0,16},{2,18},{4,20},{6,22},{8,24},{10,26},{12,28},{14,30},{16,0},... | collective-permute-start | bytes 147464 | tf_op jit(solution)/shard_map/ppermute | solution.py:307
  11.1 2.4 %collective-permute-done.1 = bf16[1,2,96,128]{3,2,1,0:T(8,128)(2,1)S(1)} collective-permute-done((bf16[1,2,96,128]{3,2,1,0:T(8,128)(2,1)S(1)}, bf16[1,2,96,128]{3,2,1,0:T(8,128)(2,1)S(1)}, u32[]{:S(2)}, u32[]{:S(2)}) %collective-permute-start.1) | collective-permute-done | bytes 49184 | tf_op jit(solution)/shard_map/ppermute | solution.py:307
  13.5 1.6 %collective-permute-start.2 = (bf16[2,2,96,128]{3,2,1,0:T(8,128)(2,1)S(1)}, bf16[2,2,96,128]{3,2,1,0:T(8,128)(2,1)S(1)}, u32[]{:S(2)}, u32[]{:S(2)}) collective-permute-start(bf16[2,2,96,128]{3,2,1,0:T(8,128)(2,1)S(1)} %pad_maximum_fusion.5), channel_id=1, source_target_pairs={{0,8},{2,10},{4,12},{6,14},{8,0},{10,2},{12,4},{14,6},{16,24},{18,... | collective-permute-start | bytes 294920 | tf_op jit(solution)/shard_map/ppermute | solution.py:307
  15.1 3.1 %collective-permute-done.2 = bf16[2,2,96,128]{3,2,1,0:T(8,128)(2,1)S(1)} collective-permute-done((bf16[2,2,96,128]{3,2,1,0:T(8,128)(2,1)S(1)}, bf16[2,2,96,128]{3,2,1,0:T(8,128)(2,1)S(1)}, u32[]{:S(2)}, u32[]{:S(2)}) %collective-permute-start.2) | collective-permute-done | bytes 98336 | tf_op jit(solution)/shard_map/ppermute | solution.py:307
  18.2 2.4 %collective-permute-start.3 = (bf16[4,2,96,128]{3,2,1,0:T(8,128)(2,1)S(1)}, bf16[4,2,96,128]{3,2,1,0:T(8,128)(2,1)S(1)}, u32[]{:S(2)}, u32[]{:S(2)}) collective-permute-start(bf16[4,2,96,128]{3,2,1,0:T(8,128)(2,1)S(1)} %pad_maximum_fusion.1.q_ref), channel_id=1, source_target_pairs={{0,4},{2,6},{4,0},{6,2},{8,12},{10,14},{12,8},{14,10},{16,20},{18,... | collective-permute-start | bytes 589832 | tf_op jit(solution)/shard_map/ppermute | solution.py:307
  20.6 4.2 %shard_map.113 = bf16[800,128]{1,0:T(8,128)(2,1)S(1)} custom-call(s32[3]{0:T(128)S(1)} %pad_add_fusion.scal, bf16[4,2,96,128]{3,2,1,0:T(8,128)(2,1)S(1)} %pad_maximum_fusion.1.q_ref, bf16[1024,512]{1,0:T(8,128)(2,1)S(1)} %bitcast.57, bf16[1024,512]{1,0:T(8,128)(2,1)S(1)} %bitcast.59, bf16[1024,512]{1,0:T(8,128)(2,1)S(1)} %collective-permute-done.4.rest_0_, ...), custom_call_target="tpu_custom_call" | custom-call | flops 855638016 | bytes 2097152 | tf_op jit(solution)/shard_map/pallas_call | solution.py:151
  25.0 1.2 %collective-permute-start.14 = (bf16[2,2,24,128]{3,2,1,0:T(8,128)(2,1)S(1)}, bf16[2,2,24,128]{3,2,1,0:T(8,128)(2,1)S(1)}, u32[]{:S(2)}, u32[]{:S(2)}) collective-permute-start(bf16[2,2,24,128]{3,2,1,0:T(8,128)(2,1)S(1)} %pad_maximum_fusion.9), channel_id=1, source_target_pairs={{0,8},{2,10},{4,12},{6,14},{8,0},{10,2},{12,4},{14,6},{16,24},{18,... | collective-permute-start | bytes 73736 | tf_op jit(solution)/shard_map/ppermute | solution.py:307
  26.2 4.2 %shard_map.112 = (f32[768,128]{1,0:T(8,128)S(1)}, f32[16,128]{1,0:T(8,128)S(1)}) custom-call(s32[3]{0:T(128)S(1)} %pad_add_fusion.scal, bf16[4,2,96,128]{3,2,1,0:T(8,128)(2,1)S(1)} %collective-permute-done.3.q_ref, bf16[1024,512]{1,0:T(8,128)(2,1)S(1)} %bitcast.58, bf16[1024,512]{1,0:T(8,128)(2,1)S(1)} %bitcast.60, ...), custom_call_target="tpu_custom_call" | custom-call | flops 855638016 | bytes 2097152 | tf_op jit(solution)/shard_map/pallas_call | solution.py:151
  31.8 2.0 %collective-permute-start.15 = (bf16[4,2,24,128]{3,2,1,0:T(8,128)(2,1)S(1)}, bf16[4,2,24,128]{3,2,1,0:T(8,128)(2,1)S(1)}, u32[]{:S(2)}, u32[]{:S(2)}) collective-permute-start(bf16[4,2,24,128]{3,2,1,0:T(8,128)(2,1)S(1)} %pad_maximum_fusion.8), channel_id=1, source_target_pairs={{0,4},{2,6},{4,0},{6,2},{8,12},{10,14},{12,8},{14,10},{16,20},{18,... | collective-permute-start | bytes 147464 | tf_op jit(solution)/shard_map/ppermute | solution.py:307
  33.9 2.0 %collective-permute-done.6.msg_ref = bf16[416,128]{1,0:T(8,128)(2,1)S(1)} collective-permute-done((bf16[416,128]{1,0:T(8,128)(2,1)S(1)}, bf16[416,128]{1,0:T(8,128)(2,1)S(1)}, u32[]{:S(2)}, u32[]{:S(2)}) %collective-permute-start.6) | collective-permute-done | bytes 106528 | tf_op jit(solution)/shard_map/ppermute | solution.py:307
  36.2 3.9 %collective-permute-start.7 = (bf16[416,128]{1,0:T(8,128)(2,1)S(1)}, bf16[416,128]{1,0:T(8,128)(2,1)S(1)}, u32[]{:S(2)}, u32[]{:S(2)}) collective-permute-start(bf16[416,128]{1,0:T(8,128)(2,1)S(1)} %get-tuple-element.20), channel_id=1, source_target_pairs={{0,16},{2,18},{4,20},{6,22},{8,24},{10,26},{12,28},{14,30},{16,0},... | collective-permute-start | bytes 319496 | tf_op jit(solution)/shard_map/ppermute | solution.py:307
  40.1 3.5 %collective-permute-done.7.msg_ref = bf16[416,128]{1,0:T(8,128)(2,1)S(1)} collective-permute-done((bf16[416,128]{1,0:T(8,128)(2,1)S(1)}, bf16[416,128]{1,0:T(8,128)(2,1)S(1)}, u32[]{:S(2)}, u32[]{:S(2)}) %collective-permute-start.7) | collective-permute-done | bytes 106528 | tf_op jit(solution)/shard_map/ppermute | solution.py:307
  44.1 4.5 %collective-permute-done.8 = bf16[2,2,96,128]{3,2,1,0:T(8,128)(2,1)S(1)} collective-permute-done((bf16[2,2,96,128]{3,2,1,0:T(8,128)(2,1)S(1)}, bf16[2,2,96,128]{3,2,1,0:T(8,128)(2,1)S(1)}, u32[]{:S(2)}, u32[]{:S(2)}) %collective-permute-start.8) | collective-permute-done | bytes 98336 | tf_op jit(solution)/shard_map/ppermute | solution.py:307
  48.7 1.6 %collective-permute-start.9 = (bf16[4,2,96,128]{3,2,1,0:T(8,128)(2,1)S(1)}, bf16[4,2,96,128]{3,2,1,0:T(8,128)(2,1)S(1)}, u32[]{:S(2)}, u32[]{:S(2)}) collective-permute-start(bf16[4,2,96,128]{3,2,1,0:T(8,128)(2,1)S(1)} %pad_maximum_fusion.2.refs_0_), channel_id=1, source_target_pairs={{0,4},{2,6},{4,0},{6,2},{8,12},{10,14},{12,8},{14,10},{16,20},{18,... | collective-permute-start | bytes 589832 | tf_op jit(solution)/shard_map/ppermute | solution.py:307
  50.4 4.0 %collective-permute-done.9.refs_1_ = bf16[4,2,96,128]{3,2,1,0:T(8,128)(2,1)S(1)} collective-permute-done((bf16[4,2,96,128]{3,2,1,0:T(8,128)(2,1)S(1)}, bf16[4,2,96,128]{3,2,1,0:T(8,128)(2,1)S(1)}, u32[]{:S(2)}, u32[]{:S(2)}) %collective-permute-start.9) | collective-permute-done | bytes 196640 | tf_op jit(solution)/shard_map/ppermute | solution.py:307
  54.5 1.9 %fusion.1 = bf16[1,1024,512]{2,1,0:T(8,128)(2,1)} fusion(pred[1024]{0:T(1024)(128)(4,1)S(1)} %compare_and_fusion.3, s32[96]{0:T(128)S(1)} %add.69, s32[1024]{0:T(1024)S(1)} %add_subtract_fusion, pred[96]{0:T(512)(128)(4,1)S(1)} %broadcast_compare_fusion, bf16[12,8,4,128]{3,2,1,0:T(4,128)(2,1)S(1)} %bitcast.64, bf16[1,1024,512]{2,1,0:T(8,128)(2,1)S(1)} %copy-done), kind=kOutput, calls=%fused_computation.3 | convolution fusion | flops 101908480 | bytes 2201056 | tf_op jit(solution)/shard_map/dot_general | solution.py:390
  56.5 1.5 %shard_map.117 = (f32[48,512]{1,0:T(8,128)S(1)}, f32[48,512]{1,0:T(8,128)S(1)}) custom-call(s32[3]{0:T(128)S(1)} %pad_add_fusion.scal, bf16[4,2,96,128]{3,2,1,0:T(8,128)(2,1)S(1)} %pad_maximum_fusion.2.refs_0_, bf16[4,2,96,128]{3,2,1,0:T(8,128)(2,1)S(1)} %collective-permute-done.9.refs_1_, bf16[4,2,96,128]{3,2,1,0:T(8,128)(2,1)S(1)} %collective-permute-done.10.refs_2_, ...), custom_call_target="tpu_custom_call" | custom-call | tf_op jit(solution)/shard_map/pallas_call | solution.py:281
  58.0 1.6 %collective-permute-start.12 = (f32[48,512]{1,0:T(8,128)S(1)}, f32[48,512]{1,0:T(8,128)S(1)}, u32[]{:S(2)}, u32[]{:S(2)}) collective-permute-start(f32[48,512]{1,0:T(8,128)S(1)} %get-tuple-element.22), channel_id=1, source_target_pairs={{0,1},{1,0},{2,3},{3,2},{4,5},{5,4},{6,7},{7,6},{8,9},{9,8},{10,11... | collective-permute-start | bytes 294920 | tf_op jit(solution)/shard_map/ppermute | solution.py:369
  59.6 1.9 %fusion.3 = bf16[1,1024,512]{2,1,0:T(8,128)(2,1)} fusion(pred[1024]{0:T(1024)(128)(4,1)S(1)} %compare_and_fusion.3, s32[96]{0:T(128)S(1)} %add.69, s32[1024]{0:T(1024)S(1)} %add_subtract_fusion, pred[96]{0:T(512)(128)(4,1)S(1)} %broadcast_compare_fusion, bf16[12,8,4,128]{3,2,1,0:T(4,128)(2,1)S(1)} %bitcast.63, bf16[1,1024,512]{2,1,0:T(8,128)(2,1)S(1)} %copy-done.1), kind=kOutput, calls=%fused_computation.5 | convolution fusion | flops 101908480 | bytes 2201056 | tf_op jit(solution)/shard_map/dot_general | solution.py:390
  61.5 1.8 %collective-permute-done.12 = f32[48,512]{1,0:T(8,128)S(1)} collective-permute-done((f32[48,512]{1,0:T(8,128)S(1)}, f32[48,512]{1,0:T(8,128)S(1)}, u32[]{:S(2)}, u32[]{:S(2)}) %collective-permute-start.12) | collective-permute-done | bytes 98336 | tf_op jit(solution)/shard_map/ppermute | solution.py:369
  (58 shorter events, 4.2 us)
Async XLA Ops:
  2.2 4.5 %collective-permute-start = (bf16[2,60,128]{2,1,0:T(8,128)(2,1)S(1)}, bf16[2,60,128]{2,1,0:T(8,128)(2,1)S(1)}, u32[]{:S(2)}, u32[]{:S(2)}) collective-permute-start(bf16[2,60,128]{2,1,0:T(8,128)(2,1)S(1)} %constant_dynamic-slice_fusion), channel_id=1, source_target_pairs={{0,2},{2,0},{4,6},{6,4},{8,10},{10,8},{12,14},{14,12},{16,18},{18,... | collective-permute-start | bytes 92168 | tf_op jit(solution)/shard_map/ppermute | solution.py:307
  2.8 3.7 %copy-start.3 = (s32[8]{0:T(128)S(1)}, s32[8]{0:T(128)}, u32[]{:S(2)}) copy-start(s32[8]{0:T(128)} %constant.51.clone) | copy-start | bytes 100
  4.0 16.6 %copy-start = (bf16[1,1024,512]{2,1,0:T(8,128)(2,1)S(1)}, bf16[1,1024,512]{2,1,0:T(8,128)(2,1)}, u32[]{:S(2)}) copy-start(bf16[1,1024,512]{2,1,0:T(8,128)(2,1)} %param.12) | copy-start | bytes 3145732
  4.1 16.6 %copy-start.1 = (bf16[1,1024,512]{2,1,0:T(8,128)(2,1)S(1)}, bf16[1,1024,512]{2,1,0:T(8,128)(2,1)}, u32[]{:S(2)}) copy-start(bf16[1,1024,512]{2,1,0:T(8,128)(2,1)} %param.13) | copy-start | bytes 3145732
  5.1 15.5 %collective-permute-start.4 = (bf16[1024,512]{1,0:T(8,128)(2,1)}, bf16[1024,512]{1,0:T(8,128)(2,1)S(1)}, u32[]{:S(2)}, u32[]{:S(2)}) collective-permute-start(bf16[1024,512]{1,0:T(8,128)(2,1)} %pad_maximum_fusion), channel_id=1, source_target_pairs={{0,2},{2,0},{4,6},{6,4},{8,10},{10,8},{12,14},{14,12},{16,18},{18,... | collective-permute-start | bytes 3145736 | tf_op jit(solution)/shard_map/ppermute | solution.py:307
  6.8 6.7 %collective-permute-start.1 = (bf16[1,2,96,128]{3,2,1,0:T(8,128)(2,1)S(1)}, bf16[1,2,96,128]{3,2,1,0:T(8,128)(2,1)S(1)}, u32[]{:S(2)}, u32[]{:S(2)}) collective-permute-start(bf16[1,2,96,128]{3,2,1,0:T(8,128)(2,1)S(1)} %maximum_bitcast_fusion), channel_id=1, source_target_pairs={{0,16},{2,18},{4,20},{6,22},{8,24},{10,26},{12,28},{14,30},{16,0},... | collective-permute-start | bytes 147464 | tf_op jit(solution)/shard_map/ppermute | solution.py:307
  11.0 14.0 %collective-permute-start.13 = (bf16[1,2,24,128]{3,2,1,0:T(8,128)(2,1)S(1)}, bf16[1,2,24,128]{3,2,1,0:T(8,128)(2,1)S(1)}, u32[]{:S(2)}, u32[]{:S(2)}) collective-permute-start(bf16[1,2,24,128]{3,2,1,0:T(8,128)(2,1)S(1)} %maximum_bitcast_fusion.1), channel_id=1, source_target_pairs={{0,16},{2,18},{4,20},{6,22},{8,24},{10,26},{12,28},{14,30},{16,0},... | collective-permute-start | bytes 36872 | tf_op jit(solution)/shard_map/ppermute | solution.py:307
  13.5 4.7 %collective-permute-start.2 = (bf16[2,2,96,128]{3,2,1,0:T(8,128)(2,1)S(1)}, bf16[2,2,96,128]{3,2,1,0:T(8,128)(2,1)S(1)}, u32[]{:S(2)}, u32[]{:S(2)}) collective-permute-start(bf16[2,2,96,128]{3,2,1,0:T(8,128)(2,1)S(1)} %pad_maximum_fusion.5), channel_id=1, source_target_pairs={{0,8},{2,10},{4,12},{6,14},{8,0},{10,2},{12,4},{14,6},{16,24},{18,... | collective-permute-start | bytes 294920 | tf_op jit(solution)/shard_map/ppermute | solution.py:307
  18.2 8.0 %collective-permute-start.3 = (bf16[4,2,96,128]{3,2,1,0:T(8,128)(2,1)S(1)}, bf16[4,2,96,128]{3,2,1,0:T(8,128)(2,1)S(1)}, u32[]{:S(2)}, u32[]{:S(2)}) collective-permute-start(bf16[4,2,96,128]{3,2,1,0:T(8,128)(2,1)S(1)} %pad_maximum_fusion.1.q_ref), channel_id=1, source_target_pairs={{0,4},{2,6},{4,0},{6,2},{8,12},{10,14},{12,8},{14,10},{16,20},{18,... | collective-permute-start | bytes 589832 | tf_op jit(solution)/shard_map/ppermute | solution.py:307
  24.9 5.8 %collective-permute-start.5 = (bf16[800,128]{1,0:T(8,128)(2,1)S(1)}, bf16[800,128]{1,0:T(8,128)(2,1)S(1)}, u32[]{:S(2)}, u32[]{:S(2)}) collective-permute-start(bf16[800,128]{1,0:T(8,128)(2,1)S(1)} %shard_map.113), channel_id=1, source_target_pairs={{0,4},{2,6},{4,0},{6,2},{8,12},{10,14},{12,8},{14,10},{16,20},{18,... | collective-permute-start | bytes 614408 | tf_op jit(solution)/shard_map/ppermute | solution.py:307
  25.0 6.8 %collective-permute-start.14 = (bf16[2,2,24,128]{3,2,1,0:T(8,128)(2,1)S(1)}, bf16[2,2,24,128]{3,2,1,0:T(8,128)(2,1)S(1)}, u32[]{:S(2)}, u32[]{:S(2)}) collective-permute-start(bf16[2,2,24,128]{3,2,1,0:T(8,128)(2,1)S(1)} %pad_maximum_fusion.9), channel_id=1, source_target_pairs={{0,8},{2,10},{4,12},{6,14},{8,0},{10,2},{12,4},{14,6},{16,24},{18,... | collective-permute-start | bytes 73736 | tf_op jit(solution)/shard_map/ppermute | solution.py:307
  31.1 4.8 %collective-permute-start.6 = (bf16[416,128]{1,0:T(8,128)(2,1)S(1)}, bf16[416,128]{1,0:T(8,128)(2,1)S(1)}, u32[]{:S(2)}, u32[]{:S(2)}) collective-permute-start(bf16[416,128]{1,0:T(8,128)(2,1)S(1)} %get-tuple-element.17), channel_id=1, source_target_pairs={{0,8},{2,10},{4,12},{6,14},{8,0},{10,2},{12,4},{14,6},{16,24},{18,... | collective-permute-start | bytes 319496 | tf_op jit(solution)/shard_map/ppermute | solution.py:307
  31.8 12.2 %collective-permute-start.15 = (bf16[4,2,24,128]{3,2,1,0:T(8,128)(2,1)S(1)}, bf16[4,2,24,128]{3,2,1,0:T(8,128)(2,1)S(1)}, u32[]{:S(2)}, u32[]{:S(2)}) collective-permute-start(bf16[4,2,24,128]{3,2,1,0:T(8,128)(2,1)S(1)} %pad_maximum_fusion.8), channel_id=1, source_target_pairs={{0,4},{2,6},{4,0},{6,2},{8,12},{10,14},{12,8},{14,10},{16,20},{18,... | collective-permute-start | bytes 147464 | tf_op jit(solution)/shard_map/ppermute | solution.py:307
  36.2 7.5 %collective-permute-start.7 = (bf16[416,128]{1,0:T(8,128)(2,1)S(1)}, bf16[416,128]{1,0:T(8,128)(2,1)S(1)}, u32[]{:S(2)}, u32[]{:S(2)}) collective-permute-start(bf16[416,128]{1,0:T(8,128)(2,1)S(1)} %get-tuple-element.20), channel_id=1, source_target_pairs={{0,16},{2,18},{4,20},{6,22},{8,24},{10,26},{12,28},{14,30},{16,0},... | collective-permute-start | bytes 319496 | tf_op jit(solution)/shard_map/ppermute | solution.py:307
  43.6 12.8 %copy-start.2 = (bf16[4096,512]{1,0:T(8,128)(2,1)S(1)}, bf16[4096,512]{1,0:T(8,128)(2,1)}, u32[]{:S(2)}) copy-start(bf16[4096,512]{1,0:T(8,128)(2,1)} %refs_4_.1) | copy-start | bytes 12582916
  44.0 4.7 %collective-permute-start.8 = (bf16[2,2,96,128]{3,2,1,0:T(8,128)(2,1)S(1)}, bf16[2,2,96,128]{3,2,1,0:T(8,128)(2,1)S(1)}, u32[]{:S(2)}, u32[]{:S(2)}) collective-permute-start(bf16[2,2,96,128]{3,2,1,0:T(8,128)(2,1)S(1)} %bitcast.61), channel_id=1, source_target_pairs={{0,8},{2,10},{4,12},{6,14},{8,0},{10,2},{12,4},{14,6},{16,24},{18,... | collective-permute-start | bytes 294920 | tf_op jit(solution)/shard_map/ppermute | solution.py:307
  44.1 6.2 %collective-permute-start.16 = (bf16[8,2,24,128]{3,2,1,0:T(8,128)(2,1)S(1)}, bf16[8,2,24,128]{3,2,1,0:T(8,128)(2,1)S(1)}, u32[]{:S(2)}, u32[]{:S(2)}) collective-permute-start(bf16[8,2,24,128]{3,2,1,0:T(8,128)(2,1)S(1)} %pad_maximum_fusion.6), channel_id=1, source_target_pairs={{0,2},{2,0},{4,6},{6,4},{8,10},{10,8},{12,14},{14,12},{16,18},{18,... | collective-permute-start | bytes 294920 | tf_op jit(solution)/shard_map/ppermute | solution.py:307
  48.7 5.7 %collective-permute-start.9 = (bf16[4,2,96,128]{3,2,1,0:T(8,128)(2,1)S(1)}, bf16[4,2,96,128]{3,2,1,0:T(8,128)(2,1)S(1)}, u32[]{:S(2)}, u32[]{:S(2)}) collective-permute-start(bf16[4,2,96,128]{3,2,1,0:T(8,128)(2,1)S(1)} %pad_maximum_fusion.2.refs_0_), channel_id=1, source_target_pairs={{0,4},{2,6},{4,0},{6,2},{8,12},{10,14},{12,8},{14,10},{16,20},{18,... | collective-permute-start | bytes 589832 | tf_op jit(solution)/shard_map/ppermute | solution.py:307
  50.3 6.2 %collective-permute-start.10 = (bf16[4,2,96,128]{3,2,1,0:T(8,128)(2,1)S(1)}, bf16[4,2,96,128]{3,2,1,0:T(8,128)(2,1)S(1)}, u32[]{:S(2)}, u32[]{:S(2)}) collective-permute-start(bf16[4,2,96,128]{3,2,1,0:T(8,128)(2,1)S(1)} %pad_maximum_fusion.2.refs_0_), channel_id=1, source_target_pairs={{0,2},{2,0},{4,6},{6,4},{8,10},{10,8},{12,14},{14,12},{16,18},{18,... | collective-permute-start | bytes 589832 | tf_op jit(solution)/shard_map/ppermute | solution.py:307
  54.4 2.1 %collective-permute-start.11 = (bf16[4,2,96,128]{3,2,1,0:T(8,128)(2,1)S(1)}, bf16[4,2,96,128]{3,2,1,0:T(8,128)(2,1)S(1)}, u32[]{:S(2)}, u32[]{:S(2)}) collective-permute-start(bf16[4,2,96,128]{3,2,1,0:T(8,128)(2,1)S(1)} %collective-permute-done.9.refs_1_), channel_id=1, source_target_pairs={{0,2},{2,0},{4,6},{6,4},{8,10},{10,8},{12,14},{14,12},{16,18},{18,... | collective-permute-start | bytes 589832 | tf_op jit(solution)/shard_map/ppermute | solution.py:307
  58.0 5.3 %collective-permute-start.12 = (f32[48,512]{1,0:T(8,128)S(1)}, f32[48,512]{1,0:T(8,128)S(1)}, u32[]{:S(2)}, u32[]{:S(2)}) collective-permute-start(f32[48,512]{1,0:T(8,128)S(1)} %get-tuple-element.22), channel_id=1, source_target_pairs={{0,1},{1,0},{2,3},{3,2},{4,5},{5,4},{6,7},{7,6},{8,9},{9,8},{10,11... | collective-permute-start | bytes 294920 | tf_op jit(solution)/shard_map/ppermute | solution.py:369

commit v2 on v1

v2 whole, which is shorter than its diff:
```python
import functools
import math

import jax
import jax.numpy as jnp
from jax import lax
from jax.experimental import pallas as pl
from jax.experimental.pallas import tpu as pltpu
from jax.sharding import PartitionSpec as P

QH = 64
KVH = 8
HD = 128
GROUP = QH // KVH
LANES = 128

DEAD = -1e30
FLOOR = -(2.0**96)
LOG2_SCALE = math.log2(math.e) / math.sqrt(HD)
VMEM_BYTES = 48 * 1024 * 1024

bf16 = jnp.bfloat16
f32 = jnp.float32


def round_up(n, m):
    return -(-n // m) * m


def stat_rows(units):
    return round_up(3 * round_up(units, 8), 16)


def pad_rows(x, rows):
    if x.shape[0] == rows:
        return x
    return jnp.concatenate([x, jnp.zeros((rows - x.shape[0], x.shape[1]), x.dtype)], axis=0)


def columns_to_rows(columns, unit):
    lane = lax.broadcasted_iota(jnp.int32, (unit, LANES), 1)
    square = jnp.zeros((unit, LANES), f32)
    for place, column in columns:
        square = jnp.where(lane == place, column, square)
    return jnp.transpose(pad_rows(square, LANES))


def split_total(total):
    high = total.astype(bf16)
    return high, (total - high.astype(f32)).astype(bf16)


def write_message(out_ref, row, shift, total):
    high, low = split_total(total)
    rows = jnp.concatenate([shift, high.astype(f32), low.astype(f32)], axis=0)
    out_ref[row : row + stat_rows(shift.shape[0]), :] = pad_rows(
        rows, stat_rows(shift.shape[0])
    ).astype(bf16)


def row_of(place, local_rows, core):
    return place + jnp.where(place < local_rows, core, -core) * local_rows


def attend_kernel(rel, unit_rows, split, as_message, n_after, len_ref, q_ref, *rest):
    caches = rest[: 2 * split]
    d_ref = rest[2 * split]
    outs = rest[2 * split + 1 + n_after :]
    units, heads = q_ref.shape[:2]
    unit = unit_rows * GROUP
    keys = caches[0].shape[0]
    seq, length = lax.axis_index("seq"), len_ref[0]
    chip = lax.div(seq, split)
    count = units * heads
    count8 = round_up(count, 8)
    step = max(n for n in range(1, units + 1) if units % n == 0 and n * unit <= 384)
    columns = []
    out_ref = outs[0]
    key_index = lax.broadcasted_iota(jnp.int32, (1, keys), 1)
    core = lax.rem(seq, split)
    local_rows = unit_rows // split
    ones = jnp.ones((keys, LANES), bf16)
    draft = lax.broadcasted_iota(jnp.int32, (1, LANES), 1)
    draft_row = unit_rows * chip + row_of(draft, local_rows, core)
    unit_row = row_of(
        lax.shift_right_logical(lax.broadcasted_iota(jnp.int32, (unit, LANES), 0), 3),
        local_rows,
        core,
    )
    for head in range(heads):
        lanes = slice(head * HD, (head + 1) * HD)
        draft_values = jnp.concatenate([d_ref[head, LANES:], ones[:LANES]], axis=1)
        for start in range(0, units, step):
            rows = step * unit
            queries = q_ref[start : start + step, head].reshape(rows, HD)
            time = jnp.concatenate(
                [
                    unit_row + unit_rows * jnp.bitwise_xor(chip, rel[start + n])
                    for n in range(step)
                ],
                axis=0,
            )
            draft_scores = lax.dot_general(
                queries, d_ref[head, :LANES], (((1,), (1,)), ((), ())), preferred_element_type=f32
            )
            draft_scores = jnp.where(draft_row <= time, draft_scores * LOG2_SCALE, DEAD)
            tops, sums = [], []
            for side in range(split):
                k_ref, v_ref = caches[2 * side : 2 * side + 2]
                block = seq if side == 0 else seq + 1 - 2 * core
                score = lax.dot_general(
                    queries, k_ref[:, lanes], (((1,), (1,)), ((), ())), preferred_element_type=f32
                )
                score = jnp.where(key_index + block * keys < length, score * LOG2_SCALE, DEAD)
                inside = (draft >= side * local_rows) & (draft < (side + 1) * local_rows)
                own_drafts = jnp.where(inside, draft_scores, DEAD)
                top = jnp.maximum(
                    jnp.max(score, axis=1, keepdims=True), jnp.max(own_drafts, axis=1, keepdims=True)
                )
                top = jnp.maximum(top, FLOOR)
                tops.append(top)
                values_ones = jnp.concatenate([v_ref[:, lanes], ones], axis=1)
                sums.append(
                    jnp.dot(
                        jnp.exp2(score - top).astype(bf16), values_ones, preferred_element_type=f32
                    )
                    + jnp.dot(
                        jnp.exp2(own_drafts - top).astype(bf16),
                        draft_values,
                        preferred_element_type=f32,
                    )
                )
            shift = functools.reduce(jnp.maximum, tops).astype(bf16).astype(f32)
            both = sum(part * jnp.exp2(top - shift) for part, top in zip(sums, tops))
            weighted, total = both[:, :HD], both[:, HD : HD + 1]
            for n in range(step):
                place = (start + n) * heads + head
                part = slice(n * unit, (n + 1) * unit)
                out_ref[place * unit : (place + 1) * unit, :] = weighted[part].astype(out_ref.dtype)
                columns.append((place, shift[part]))
                columns.append((count8 + place, total[part]))
    stats = columns_to_rows(columns, unit)
    if as_message:
        write_message(out_ref, count * unit, stats[:count8], stats[count8 : 2 * count8])
    else:
        outs[1][...] = stats[: 2 * count8]


def attend(length, q, rel, unit_rows, split, caches, drafts, as_message, after=()):
    units, heads = q.shape[:2]
    unit = unit_rows * GROUP
    keys = caches[0].shape[0]
    count = units * heads
    if as_message:
        out_shape = (jax.ShapeDtypeStruct((count * unit + stat_rows(count), LANES), bf16),)
    else:
        out_shape = (
            jax.ShapeDtypeStruct((count * unit, LANES), f32),
            jax.ShapeDtypeStruct((2 * round_up(count, 8), LANES), f32),
        )
    cache_spec = pl.BlockSpec((keys, heads * HD), lambda i, s: (0, 0))
    other_spec = pl.BlockSpec(
        (keys, heads * HD), lambda i, s: (0, lax.rem(lax.axis_index("seq"), split))
    )
    in_specs = [pl.BlockSpec(q.shape, lambda i, s: (0, 0, 0, 0))]
    in_specs += [cache_spec] * 2 + [other_spec] * (len(caches) - 2)
    in_specs += [pl.BlockSpec(drafts.shape, lambda i, s: (0, 0, 0))]
    in_specs += [pl.BlockSpec(memory_space=pl.ANY)] * len(after)
    scores = count * unit * (split * keys + LANES)
    return pl.pallas_call(
        functools.partial(attend_kernel, rel, unit_rows, split, as_message, len(after)),
        grid_spec=pltpu.PrefetchScalarGridSpec(
            num_scalar_prefetch=1,
            grid=(1,),
            in_specs=in_specs,
            out_specs=tuple(pl.BlockSpec(o.shape, lambda i, s: (0, 0)) for o in out_shape),
        ),
        out_shape=out_shape,
        compiler_params=pltpu.CompilerParams(vmem_limit_bytes=VMEM_BYTES),
        cost_estimate=pl.CostEstimate(
            flops=4 * scores * HD, bytes_accessed=4 * split * keys * heads * HD, transcendentals=scores
        ),
    )(length, q, *caches, drafts, *after)


def merge_kernel(unit, mode, num_ref, stat_ref, msg_ref, *outs):
    rows = num_ref.shape[0]
    count = rows // unit
    count8 = stat_ref.shape[0] // 2
    own_shift, own_total = stat_ref[:count8], stat_ref[count8:]
    sent = msg_ref[rows:, :].astype(f32)
    shift = sent[:count8]
    total = sent[count8 : 2 * count8] + sent[2 * count8 : 3 * count8]
    half = count // 2
    if mode == "final":
        shift = pad_rows(jnp.concatenate([shift[half:count], shift[:half]], axis=0), count8)
        total = pad_rows(jnp.concatenate([total[half:count], total[:half]], axis=0), count8)
    new_shift = jnp.maximum(own_shift, shift)
    own_factor = jnp.exp2(own_shift - new_shift)
    factor = jnp.exp2(shift - new_shift)
    new_total = own_total * own_factor + total * factor
    if mode == "final":
        new_total = jnp.where(new_total > 0, new_total, 1.0)
        own_factor = own_factor / new_total
        factor = factor / new_total
    factors = jnp.transpose(pad_rows(jnp.concatenate([own_factor, factor], axis=0), LANES))
    for n in range(count):
        source = (n + half) % count if mode == "final" else n
        merged = num_ref[n * unit : (n + 1) * unit, :] * factors[:unit, n : n + 1]
        merged = merged + (
            msg_ref[source * unit : (source + 1) * unit, :].astype(f32)
            * factors[:unit, count8 + n : count8 + n + 1]
        )
        here = slice(n * unit, (n + 1) * unit)
        if mode == "final":
            outs[0][here, :] = merged.astype(bf16)
        elif mode == "all":
            outs[0][here, :] = merged
            outs[2][here, :] = merged.astype(bf16)
        elif n < half:
            outs[0][here, :] = merged
        else:
            outs[2][(n - half) * unit : (n - half + 1) * unit, :] = merged.astype(bf16)
    if mode == "all":
        outs[1][...] = jnp.concatenate([new_shift, new_total], axis=0)
        write_message(outs[2], rows, new_shift, new_total)
    elif mode == "half":
        half8 = round_up(half, 8)
        outs[1][...] = jnp.concatenate(
            [pad_rows(new_shift[:half], half8), pad_rows(new_total[:half], half8)], axis=0
        )
        write_message(
            outs[2],
            half * unit,
            pad_rows(new_shift[half:count], half8),
            pad_rows(new_total[half:count], half8),
        )


def merge(unit, mode, num, stats, message):
    rows = num.shape[0]
    if mode == "final":
        out_shape = jax.ShapeDtypeStruct((rows, LANES), bf16)
    else:
        rows = rows // 2 if mode == "half" else rows
        count = rows // unit
        out_shape = (
            jax.ShapeDtypeStruct((rows, LANES), f32),
            jax.ShapeDtypeStruct((2 * round_up(count, 8), LANES), f32),
            jax.ShapeDtypeStruct((rows + stat_rows(count), LANES), bf16),
        )
    return pl.pallas_call(
        functools.partial(merge_kernel, unit, mode),
        out_shape=out_shape,
        compiler_params=pltpu.CompilerParams(vmem_limit_bytes=VMEM_BYTES),
    )(num, stats, message)


def project_kernel(rel, split, n_head, *refs):
    sources = refs[: 2 * split]
    w_ref = refs[2 * split]
    outs = refs[2 * split + 1 : -2]
    rows_ref, lhs_ref = refs[-2:]
    seq, head = lax.axis_index("seq"), lax.axis_index("head")
    chip = lax.div(seq, split)
    core = lax.rem(seq, split)
    heads_kv = rows_ref.shape[0]
    units, heads, unit, _ = sources[0].shape
    chips = 2 * units
    piece = unit // split
    first = head * (chips // n_head) if n_head == 2 else 0
    for side in range(split):
        owner = core if side == 0 else 1 - core
        for part in range(2):
            x_ref = sources[2 * side + part]
            for n in range(units):
                place = lax.rem(jnp.bitwise_xor(chip, rel[part][n]) - first + chips, chips)
                for part_of in range(split):
                    row = place * unit + (owner if part_of == 0 else 1 - owner) * piece
                    for h in range(heads):
                        rows_ref[owner * heads + h, pl.ds(pl.multiple_of(row, 16), piece), :] = (
                            x_ref[n, h, part_of * piece : (part_of + 1) * piece].astype(f32)
                        )
    rows = lhs_ref.shape[0]
    for kv in range(heads_kv):
        for g in range(GROUP):
            lanes = slice((kv * GROUP + g) * HD, (kv * GROUP + g + 1) * HD)
            lhs_ref[:, lanes] = rows_ref[kv, pl.ds(g, rows, stride=GROUP), :].astype(bf16)
    result = jnp.dot(lhs_ref[...], w_ref[...], preferred_element_type=f32)
    if n_head == 2:
        outs[0][...] = result[: rows // 2]
        outs[1][...] = result[rows // 2 :]
    else:
        outs[0][...] = result


def project(rel, split, n_head, sources, weight):
    units, heads, unit, _ = sources[0].shape
    heads_kv = heads * split
    rows = 2 * units * unit // GROUP
    columns = weight.shape[1]
    if n_head == 2:
        out_shape = (jax.ShapeDtypeStruct((rows // 2, columns), f32),) * 2
    else:
        out_shape = (jax.ShapeDtypeStruct((rows, columns), f32),)
    return pl.pallas_call(
        functools.partial(project_kernel, rel, split, n_head),
        in_specs=[pl.BlockSpec(memory_space=pltpu.VMEM)] * (2 * split + 1),
        out_shape=out_shape,
        scratch_shapes=[
            pltpu.VMEM((heads_kv, 2 * units * unit, LANES), f32),
            pltpu.VMEM((rows, heads_kv * GROUP * HD), bf16),
        ],
        compiler_params=pltpu.CompilerParams(vmem_limit_bytes=VMEM_BYTES),
    )(*sources, weight)


def append_kernel(rel, split, unit_rows, len_ref, acc_ref, ck_ref, cv_ref, mine_ref, other_ref, *rest):
    nk_ref, nv_ref = rest[-2:]
    rows, width = ck_ref.shape
    chips, heads, both, _ = mine_ref.shape
    local_rows = unit_rows // split
    seq = lax.axis_index("seq")
    chip, core = lax.div(seq, split), lax.rem(seq, split)
    length, accepted = len_ref[0], acc_ref[0]
    first = (seq * pl.num_programs(0) + pl.program_id(0)) * rows - length
    touched = (first < accepted) & (first + rows > 0)

    @pl.when(jnp.logical_not(touched))
    def _():
        nk_ref[...] = ck_ref[...]
        nv_ref[...] = cv_ref[...]

    @pl.when(touched)
    def _():
        place = first + lax.broadcasted_iota(jnp.int32, (rows, both), 0)
        lane = lax.broadcasted_iota(jnp.int32, (rows, both), 1)
        inside = (place >= 0) & (place < accepted)
        chosen = first + lax.broadcasted_iota(jnp.int32, (rows, HD), 0)
        chosen = (chosen >= 0) & (chosen < accepted)
        for side in range(split):
            drafts = mine_ref if side == 0 else other_ref
            source_core = core if side == 0 else 1 - core
            for cache_ref, new_ref, start in ((ck_ref, nk_ref, 0), (cv_ref, nv_ref, unit_rows)):
                sums = [jnp.zeros((rows, HD), f32)] * heads
                here = (lane >= start) & (lane < start + unit_rows) & inside
                row = row_of(lane - start, local_rows, source_core)
                for n in range(chips):
                    source = jnp.bitwise_xor(chip, rel[n]) * unit_rows + row
                    pick = jnp.where(here & (source == place), 1.0, 0.0).astype(bf16)
                    for h in range(heads):
                        sums[h] = sums[h] + jnp.dot(
                            pick, drafts[n, h], preferred_element_type=f32
                        )
                for h in range(heads):
                    lanes = pl.ds(pl.multiple_of((source_core * heads + h) * HD, HD), HD)
                    new_ref[:, lanes] = jnp.where(
                        chosen, sums[h], cache_ref[:, lanes].astype(f32)
                    ).astype(bf16)


def append(rel, split, unit_rows, length, accepted, ck, cv, drafts, after):
    rows = ck.shape[0]
    block = rows // 4 if rows % 64 == 0 else rows
    cache_spec = pl.BlockSpec((block, ck.shape[1]), lambda i: (i, 0))
    mine, other = drafts[0], drafts[-1]
    draft_spec = pl.BlockSpec(mine.shape, lambda i: (0, 0, 0, 0))
    shape = jax.ShapeDtypeStruct(ck.shape, bf16)
    return pl.pallas_call(
        functools.partial(append_kernel, rel, split, unit_rows),
        grid=(rows // block,),
        in_specs=[pl.BlockSpec(memory_space=pltpu.SMEM)] * 2
        + [cache_spec, cache_spec, draft_spec, draft_spec]
        + [pl.BlockSpec(memory_space=pl.ANY)] * len(after),
        out_specs=(cache_spec, cache_spec),
        out_shape=(shape, shape),
        compiler_params=pltpu.CompilerParams(vmem_limit_bytes=VMEM_BYTES),
        cost_estimate=pl.CostEstimate(flops=0, bytes_accessed=8 * ck.size, transcendentals=0),
    )(length, accepted, ck, cv, mine, other, *after)


def one_request(n_seq, n_head, dq, dk, dv, ck, cv, accepted, length, weight):
    seq = lax.axis_index("seq")
    local_rows = dq.shape[0]
    heads_kv = dk.shape[1] // HD
    split = 2 if heads_kv % 2 == 0 else 1
    heads = heads_kv // split
    unit_rows = local_rows * split
    unit = unit_rows * GROUP
    n_bits = n_seq.bit_length() - 1
    bits = list(range(n_bits - 1, split - 2, -1))

    def swap(x, bit):
        return lax.ppermute(x, "seq", [(i, i ^ (1 << bit)) for i in range(n_seq)])

    core = seq % split

    q4 = dq.reshape(local_rows, heads_kv, GROUP, LANES).transpose(1, 0, 2, 3)
    q4 = q4.reshape(heads_kv, local_rows * GROUP, LANES)
    dk4 = dk.reshape(local_rows, heads_kv, HD).transpose(1, 0, 2)
    dv4 = dv.reshape(local_rows, heads_kv, HD).transpose(1, 0, 2)
    pack = jnp.concatenate([q4, dk4, dv4], axis=1)
    parts, caches = [pack], [ck, cv]
    if split == 2:
        mine = lax.dynamic_slice_in_dim(pack, core * heads, heads, 0)
        parts = [mine, swap(lax.dynamic_slice_in_dim(pack, (1 - core) * heads, heads, 0), 0)]
    cut = local_rows * GROUP
    second = cut + local_rows
    pieces = [p[:, :cut] for p in parts]
    pieces += [p[:, cut : cut + local_rows] for p in parts]
    pieces += [p[:, second : second + local_rows] for p in parts]
    q = jnp.concatenate(pieces, axis=1)
    d_key, d_value = q[:, unit : unit + unit_rows], q[:, unit + unit_rows :]
    spare = ((0, 0), (0, LANES - unit_rows), (0, 0))
    drafts = jnp.concatenate([jnp.pad(d_key, spare), jnp.pad(d_value, spare)], axis=1)
    q = q[None]
    if split == 2:
        q, ck_late, cv_late = lax.optimization_barrier((q, ck, cv))
        caches += [swap(ck_late, 0), swap(cv_late, 0)]

    rel = [0]
    for bit in bits[:-1]:
        q = jnp.concatenate([q, swap(q, bit)], axis=0)
        if split == 2 and bit == bits[0]:
            q, *own = lax.optimization_barrier((q, ck, cv))
            caches[:2] = [
                lax.dynamic_slice_in_dim(c, core * heads * HD, heads * HD, 1) for c in own
            ]
        rel = rel + [r | (1 << bit) // split for r in rel]
    q, dkv = q[:, :, :unit], q[:, :, unit:]
    near = bits[-1]
    rel_far = [r | (1 << near) // split for r in rel]
    q_far = swap(q, near)

    run = functools.partial(attend, length)
    (message,) = run(q, rel, unit_rows, split, caches, drafts, True)
    num, stats = run(q_far, rel_far, unit_rows, split, caches, drafts, False, (message,))
    message = swap(message, near)

    dkv = jnp.concatenate([dkv, swap(dkv, near)], axis=0)

    for bit in reversed(bits[:-1]):
        mode = "all" if bit == bits[0] else "half"
        num, stats, message = merge(unit, mode, num, stats, message)
        message = swap(message, bit)

    att = merge(unit, "final", num, stats, message).reshape(-1, heads, unit, LANES)
    att, dkv = lax.optimization_barrier((att, dkv))
    every = [dkv, swap(dkv, 0)] if split == 2 else [dkv]
    for bit in bits[1:-1]:
        att = jnp.concatenate([att, swap(att, bit)], axis=0)
    att, every = lax.optimization_barrier((att, every))
    att_near = swap(att, near)
    sources = [att, att_near]
    if split == 2:
        sources += [swap(att, 0), swap(att_near, 0)]
    result = project((rel_far, rel), split, n_head, sources, weight)
    if n_head == 2:
        keep, send = result
        projected = keep + lax.ppermute(send, "head", [(0, 1), (1, 0)])
    else:
        projected = lax.psum_scatter(result[0], "head", scatter_dimension=0, tiled=True)
    new_key, new_value = append(
        rel + rel_far, split, unit_rows, length, accepted, ck, cv, every, (result[-1],)
    )
    return projected.astype(bf16), new_key, new_value


def on_device(n_seq, n_head, dq, dk, dv, ck, cv, accepted, cache_len, weight):
    results = [
        one_request(
            n_seq, n_head, dq[r], dk[r], dv[r], ck[r], cv[r], accepted[r : r + 1], cache_len[r : r + 1], weight
        )
        for r in range(dq.shape[0])
    ]
    return tuple(jnp.stack(parts) for parts in zip(*results))


def solution(mesh):
    in_specs = (
        P(None, "seq", "head"),
        P(None, "seq", "head"),
        P(None, "seq", "head"),
        P(None, "seq", "head"),
        P(None, "seq", "head"),
        P(),
        P(),
        P("head", "seq"),
    )
    out_specs = (P(None, "head", "seq"), P(None, "seq", "head"), P(None, "seq", "head"))
    return jax.shard_map(
        functools.partial(on_device, mesh.shape["seq"], mesh.shape["head"]),
        mesh=mesh,
        in_specs=in_specs,
        out_specs=out_specs,
        check_vma=False,
    )
```

time: 64.2 us -> 60.7 us (0.945)
  waiting for transfers between devices: 21.7 us -> 27.4 us
  matrix products: 3.81 us -> 0 us
  starting transfers between devices: 20.1 us -> 16.8 us
  other arithmetic: 2.78 us -> 1.43 us
  Pallas kernels: 11 us -> 10.3 us
    ppermute x16 -> x15, waiting for transfers between devices: 19.9 us -> 26.6 us  [swap(): return lax.ppermute(x, 'seq', [(i, i ^ 1 << bit) for i in range(n_seq)])]
    dot_general x2 -> x0, matrix products: 3.81 us -> none  [append(): jnp.dot(pick.astype(bf16), rows, preferred_element_type=f32).astype(bf16)]
    ppermute x16 -> x15, starting transfers between devices: 18.5 us -> 15.2 us  [swap(): return lax.ppermute(x, 'seq', [(i, i ^ 1 << bit) for i in range(n_seq)])]
    pallas_call x2, Pallas kernels: 8.46 us -> 6.46 us  [attend(): pl.pallas_call(functools.partial(attend_kernel, rel, unit_rows, split, as...]
    pallas_call x0 -> x1, Pallas kernels: none -> 1.87 us  [append(): pl.pallas_call(functools.partial(append_kernel, rel, split, unit_rows), g...]
    concatenate x6 -> x2, other arithmetic: 1.1 us -> 0.02 us  [the longest x1 0.01 us: one_request(): q = jnp.concatenate(pieces, axis=1)]
    ppermute x1, waiting for transfers between devices: 1.76 us -> 0.78 us  [one_request(): projected = keep + lax.ppermute(send, 'head', [(0, 1), (1, 0)])]
  transfers between devices with their start and end apart: 17 -> 16, of which waited for: 8 -> 11; matrix products, arithmetic and copies ran while one was open for 10% -> 2% of each run, Pallas kernels for 15% -> 14%
where the time goes in v2:
time: 60.7 us; the launch traced here: 60.4 us
  waiting for transfers between devices  27.4 us (45%)
  starting transfers between devices  16.8 us (28%)
  Pallas kernels  10.3 us (17%)
  local copies, waits for them, and re-layouts  2.45 us (4%)
  between operations  2.1 us (3%)
  other arithmetic  1.43 us (2%)
    ppermute x15, waiting for transfers between devices, swap(): return lax.ppermute(x, 'seq', [(i, i ^ 1 << bit) for i in range(n_seq)])  26.6 us
    ppermute x15, starting transfers between devices, swap(): return lax.ppermute(x, 'seq', [(i, i ^ 1 << bit) for i in range(n_seq)])  15.2 us
    pallas_call x2, Pallas kernels, attend(): pl.pallas_call(functools.partial(attend_kernel, rel, unit_rows, split, as...  6.46 us
    pallas_call x1, Pallas kernels, append(): pl.pallas_call(functools.partial(append_kernel, rel, split, unit_rows), g...  1.87 us
    ppermute x1, starting transfers between devices, one_request(): projected = keep + lax.ppermute(send, 'head', [(0, 1), (1, 0)])  1.58 us
    dynamic_slice x1, local copies, waits for them, and re-layouts, one_request(): lax.dynamic_slice_in_dim(c, core * heads * HD, heads * HD, 1)  1.27 us
  transfers between devices with their start and end apart: 16, of which 11 were waited for; matrix products, arithmetic and copies ran while one was open for 2% of the time, Pallas kernels for 14%

profile of v2, /device:TPU:0, one launch (start us, length us, event | category | flops | bytes accessed | tf_op | source)
XLA Modules:
  0.0 60.4 jit_solution(11541067994428162227)
XLA Ops:
  0.6 0.8 %copy_bitcast_fusion.1 = bf16[4,48,128]{2,1,0:T(8,128)(2,1)S(1)} fusion(bf16[1,6,32,128]{3,1,2,0:T(8,128)(2,1)} %bitcast.34), kind=kLoop, calls=%fused_computation.15 | loop fusion | bytes 98304 | tf_op jit(solution)/shard_map/reshape | solution.py:399
  2.8 0.8 %collective-permute-done = bf16[2,60,128]{2,1,0:T(8,128)(2,1)S(1)} collective-permute-done((bf16[2,60,128]{2,1,0:T(8,128)(2,1)S(1)}, bf16[2,60,128]{2,1,0:T(8,128)(2,1)S(1)}, u32[]{:S(2)}, u32[]{:S(2)}) %collective-permute-start) | collective-permute-done | bytes 30752 | tf_op jit(solution)/shard_map/ppermute | solution.py:394
  5.1 4.0 %collective-permute-start.1 = (bf16[1,2,120,128]{3,2,1,0:T(8,128)(2,1)S(1)}, bf16[1,2,120,128]{3,2,1,0:T(8,128)(2,1)S(1)}, u32[]{:S(2)}, u32[]{:S(2)}) collective-permute-start(bf16[1,2,120,128]{3,2,1,0:T(8,128)(2,1)S(1)} %bitcast.32), channel_id=1, source_target_pairs={{0,16},{2,18},{4,20},{6,22},{8,24},{10,26},{12,28},{14,30},{16,0},... | collective-permute-start | bytes 184328 | tf_op jit(solution)/shard_map/ppermute | solution.py:394
  9.1 3.6 %collective-permute-done.1 = bf16[1,2,120,128]{3,2,1,0:T(8,128)(2,1)S(1)} collective-permute-done((bf16[1,2,120,128]{3,2,1,0:T(8,128)(2,1)S(1)}, bf16[1,2,120,128]{3,2,1,0:T(8,128)(2,1)S(1)}, u32[]{:S(2)}, u32[]{:S(2)}) %collective-permute-start.1) | collective-permute-done | bytes 61472 | tf_op jit(solution)/shard_map/ppermute | solution.py:394
  12.8 0.8 %collective-permute-start.2 = (bf16[2,2,120,128]{3,2,1,0:T(8,128)(2,1)S(1)}, bf16[2,2,120,128]{3,2,1,0:T(8,128)(2,1)S(1)}, u32[]{:S(2)}, u32[]{:S(2)}) collective-permute-start(bf16[2,2,120,128]{3,2,1,0:T(8,128)(2,1)S(1)} %pad_maximum_fusion.2), channel_id=1, source_target_pairs={{0,8},{2,10},{4,12},{6,14},{8,0},{10,2},{12,4},{14,6},{16,24},{18,... | collective-permute-start | bytes 368648 | tf_op jit(solution)/shard_map/ppermute | solution.py:394
  13.5 1.3 %constant_dynamic-slice_fusion.2 = (bf16[1024,256]{1,0:T(8,128)(2,1)S(1)}, bf16[1024,256]{1,0:T(8,128)(2,1)S(1)}) fusion(bf16[1024,512]{1,0:T(8,128)(2,1)} %bitcast.25, s32[]{:T(128)S(6)} %select_n.20, bf16[1024,512]{1,0:T(8,128)(2,1)} %bitcast.28), kind=kLoop, calls=%fused_computation.20 | loop fusion | bytes 2097156 | tf_op jit(solution)/shard_map/dynamic_slice | solution.py:427
  14.8 2.9 %collective-permute-done.2 = bf16[2,2,120,128]{3,2,1,0:T(8,128)(2,1)S(1)} collective-permute-done((bf16[2,2,120,128]{3,2,1,0:T(8,128)(2,1)S(1)}, bf16[2,2,120,128]{3,2,1,0:T(8,128)(2,1)S(1)}, u32[]{:S(2)}, u32[]{:S(2)}) %collective-permute-start.2) | collective-permute-done | bytes 122912 | tf_op jit(solution)/shard_map/ppermute | solution.py:394
  17.8 1.8 %collective-permute-start.3 = (bf16[4,2,96,128]{3,2,1,0:T(8,128)(2,1)S(1)}, bf16[4,2,96,128]{3,2,1,0:T(8,128)(2,1)S(1)}, u32[]{:S(2)}, u32[]{:S(2)}) collective-permute-start(bf16[4,2,96,128]{3,2,1,0:T(8,128)(2,1)S(1)} %slice.39.q_ref), channel_id=1, source_target_pairs={{0,4},{2,6},{4,0},{6,2},{8,12},{10,14},{12,8},{14,10},{16,20},{18,... | collective-permute-start | bytes 589832 | tf_op jit(solution)/shard_map/ppermute | solution.py:394
  19.5 3.2 %shard_map.103.rest_5_ = bf16[800,128]{1,0:T(8,128)(2,1)S(1)} custom-call(s32[1]{0:T(128)S(6)} %copy.18.len_ref, bf16[4,2,96,128]{3,2,1,0:T(8,128)(2,1)S(1)} %slice.39.q_ref, bf16[1024,256]{1,0:T(8,128)(2,1)S(1)} %get-tuple-element.56.rest_0_, bf16[1024,256]{1,0:T(8,128)(2,1)S(1)} %get-tuple-element.55.rest_1_, ...), custom_call_target="tpu_custom_call" | custom-call | flops 855638016 | bytes 2097152 | tf_op jit(solution)/shard_map/pallas_call | solution.py:170
  23.1 1.5 %collective-permute-done.3.q_ref = bf16[4,2,96,128]{3,2,1,0:T(8,128)(2,1)S(1)} collective-permute-done((bf16[4,2,96,128]{3,2,1,0:T(8,128)(2,1)S(1)}, bf16[4,2,96,128]{3,2,1,0:T(8,128)(2,1)S(1)}, u32[]{:S(2)}, u32[]{:S(2)}) %collective-permute-start.3) | collective-permute-done | bytes 196640 | tf_op jit(solution)/shard_map/ppermute | solution.py:394
  24.6 3.2 %shard_map.104 = (f32[768,128]{1,0:T(8,128)S(1)}, f32[16,128]{1,0:T(8,128)S(1)}) custom-call(s32[1]{0:T(128)S(6)} %copy.18.len_ref, bf16[4,2,96,128]{3,2,1,0:T(8,128)(2,1)S(1)} %collective-permute-done.3.q_ref, bf16[1024,256]{1,0:T(8,128)(2,1)S(1)} %get-tuple-element.56.rest_0_, bf16[1024,256]{1,0:T(8,128)(2,1)S(1)} %get-tuple-element.55.rest_1_, ...), custom_call_target="tpu_custom_call" | custom-call | flops 855638016 | bytes 2097152 | tf_op jit(solution)/shard_map/pallas_call | solution.py:170
  28.9 1.0 %collective-permute-start.7 = (bf16[416,128]{1,0:T(8,128)(2,1)S(1)}, bf16[416,128]{1,0:T(8,128)(2,1)S(1)}, u32[]{:S(2)}, u32[]{:S(2)}) collective-permute-start(bf16[416,128]{1,0:T(8,128)(2,1)S(1)} %get-tuple-element.36), channel_id=1, source_target_pairs={{0,8},{2,10},{4,12},{6,14},{8,0},{10,2},{12,4},{14,6},{16,24},{18,... | collective-permute-start | bytes 319496 | tf_op jit(solution)/shard_map/ppermute | solution.py:394
  29.9 1.2 %collective-permute-start.9 = (bf16[4,2,24,128]{3,2,1,0:T(8,128)(2,1)S(1)}, bf16[4,2,24,128]{3,2,1,0:T(8,128)(2,1)S(1)}, u32[]{:S(2)}, u32[]{:S(2)}) collective-permute-start(bf16[4,2,24,128]{3,2,1,0:T(8,128)(2,1)S(1)} %slice.40), channel_id=1, source_target_pairs={{0,4},{2,6},{4,0},{6,2},{8,12},{10,14},{12,8},{14,10},{16,20},{18,... | collective-permute-start | bytes 147464 | tf_op jit(solution)/shard_map/ppermute | solution.py:394
  31.1 2.6 %collective-permute-done.7.msg_ref = bf16[416,128]{1,0:T(8,128)(2,1)S(1)} collective-permute-done((bf16[416,128]{1,0:T(8,128)(2,1)S(1)}, bf16[416,128]{1,0:T(8,128)(2,1)S(1)}, u32[]{:S(2)}, u32[]{:S(2)}) %collective-permute-start.7) | collective-permute-done | bytes 106528 | tf_op jit(solution)/shard_map/ppermute | solution.py:394
  34.0 3.8 %collective-permute-start.8 = (bf16[416,128]{1,0:T(8,128)(2,1)S(1)}, bf16[416,128]{1,0:T(8,128)(2,1)S(1)}, u32[]{:S(2)}, u32[]{:S(2)}) collective-permute-start(bf16[416,128]{1,0:T(8,128)(2,1)S(1)} %get-tuple-element.39), channel_id=1, source_target_pairs={{0,16},{2,18},{4,20},{6,22},{8,24},{10,26},{12,28},{14,30},{16,0},... | collective-permute-start | bytes 319496 | tf_op jit(solution)/shard_map/ppermute | solution.py:394
  37.8 3.9 %collective-permute-done.8.msg_ref = bf16[416,128]{1,0:T(8,128)(2,1)S(1)} collective-permute-done((bf16[416,128]{1,0:T(8,128)(2,1)S(1)}, bf16[416,128]{1,0:T(8,128)(2,1)S(1)}, u32[]{:S(2)}, u32[]{:S(2)}) %collective-permute-start.8) | collective-permute-done | bytes 106528 | tf_op jit(solution)/shard_map/ppermute | solution.py:394
  42.2 4.5 %collective-permute-done.10 = bf16[2,2,96,128]{3,2,1,0:T(8,128)(2,1)S(1)} collective-permute-done((bf16[2,2,96,128]{3,2,1,0:T(8,128)(2,1)S(1)}, bf16[2,2,96,128]{3,2,1,0:T(8,128)(2,1)S(1)}, u32[]{:S(2)}, u32[]{:S(2)}) %collective-permute-start.10) | collective-permute-done | bytes 98336 | tf_op jit(solution)/shard_map/ppermute | solution.py:394
  46.8 1.1 %collective-permute-start.12 = (bf16[4,2,96,128]{3,2,1,0:T(8,128)(2,1)S(1)}, bf16[4,2,96,128]{3,2,1,0:T(8,128)(2,1)S(1)}, u32[]{:S(2)}, u32[]{:S(2)}) collective-permute-start(bf16[4,2,96,128]{3,2,1,0:T(8,128)(2,1)S(1)} %pad_maximum_fusion.refs_0_), channel_id=1, source_target_pairs={{0,4},{2,6},{4,0},{6,2},{8,12},{10,14},{12,8},{14,10},{16,20},{18,... | collective-permute-start | bytes 589832 | tf_op jit(solution)/shard_map/ppermute | solution.py:394
  47.8 4.7 %collective-permute-done.12.refs_1_ = bf16[4,2,96,128]{3,2,1,0:T(8,128)(2,1)S(1)} collective-permute-done((bf16[4,2,96,128]{3,2,1,0:T(8,128)(2,1)S(1)}, bf16[4,2,96,128]{3,2,1,0:T(8,128)(2,1)S(1)}, u32[]{:S(2)}, u32[]{:S(2)}) %collective-permute-start.12) | collective-permute-done | bytes 196640 | tf_op jit(solution)/shard_map/ppermute | solution.py:394
  52.5 1.4 %collective-permute-done.14.refs_3_ = bf16[4,2,96,128]{3,2,1,0:T(8,128)(2,1)S(1)} collective-permute-done((bf16[4,2,96,128]{3,2,1,0:T(8,128)(2,1)S(1)}, bf16[4,2,96,128]{3,2,1,0:T(8,128)(2,1)S(1)}, u32[]{:S(2)}, u32[]{:S(2)}) %collective-permute-start.14) | collective-permute-done | bytes 196640 | tf_op jit(solution)/shard_map/ppermute | solution.py:394
  53.9 0.9 %shard_map.108 = (f32[48,512]{1,0:T(8,128)S(1)}, f32[48,512]{1,0:T(8,128)S(1)}) custom-call(bf16[4,2,96,128]{3,2,1,0:T(8,128)(2,1)S(1)} %pad_maximum_fusion.refs_0_, bf16[4,2,96,128]{3,2,1,0:T(8,128)(2,1)S(1)} %collective-permute-done.12.refs_1_, bf16[4,2,96,128]{3,2,1,0:T(8,128)(2,1)S(1)} %collective-permute-done.13.refs_2_, ...), custom_call_target="tpu_custom_call" | custom-call | tf_op jit(solution)/shard_map/pallas_call | solution.py:306
  54.9 1.6 %collective-permute-start.15 = (f32[48,512]{1,0:T(8,128)S(1)}, f32[48,512]{1,0:T(8,128)S(1)}, u32[]{:S(2)}, u32[]{:S(2)}) collective-permute-start(f32[48,512]{1,0:T(8,128)S(1)} %get-tuple-element.44.rest_0_), channel_id=1, source_target_pairs={{0,1},{1,0},{2,3},{3,2},{4,5},{5,4},{6,7},{7,6},{8,9},{9,8},{10,11... | collective-permute-start | bytes 294920 | tf_op jit(solution)/shard_map/ppermute | solution.py:460
  57.1 1.9 %shard_map.109 = (bf16[1024,512]{1,0:T(8,128)(2,1)}, bf16[1024,512]{1,0:T(8,128)(2,1)}) custom-call(s32[1]{0:T(128)S(6)} %copy.18.len_ref, s32[1]{0:T(128)S(6)} %copy.17.acc_ref, bf16[1024,512]{1,0:T(8,128)(2,1)S(1)} %bitcast.29, bf16[1024,512]{1,0:T(8,128)(2,1)S(1)} %bitcast.26, bf16[8,2,24,128]{3,2,1,0:T(8,128)(2,1)S(1)} %pad_maximum_fusion.3.mine_ref, ...), custom_call_target="tpu_custom_call" | custom-call | bytes 4194304 | tf_op jit(solution)/shard_map/pallas_call | solution.py:369
  59.0 0.8 %collective-permute-done.15 = f32[48,512]{1,0:T(8,128)S(1)} collective-permute-done((f32[48,512]{1,0:T(8,128)S(1)}, f32[48,512]{1,0:T(8,128)S(1)}, u32[]{:S(2)}, u32[]{:S(2)}) %collective-permute-start.15) | collective-permute-done | bytes 98336 | tf_op jit(solution)/shard_map/ppermute | solution.py:460
  (40 shorter events, 5.0 us)
Async XLA Ops:
  2.2 1.4 %collective-permute-start = (bf16[2,60,128]{2,1,0:T(8,128)(2,1)S(1)}, bf16[2,60,128]{2,1,0:T(8,128)(2,1)S(1)}, u32[]{:S(2)}, u32[]{:S(2)}) collective-permute-start(bf16[2,60,128]{2,1,0:T(8,128)(2,1)S(1)} %constant_dynamic-slice_fusion.4), channel_id=1, source_target_pairs={{0,2},{2,0},{4,6},{6,4},{8,10},{10,8},{12,14},{14,12},{16,18},{18,... | collective-permute-start | bytes 92168 | tf_op jit(solution)/shard_map/ppermute | solution.py:394
  3.9 15.6 %collective-permute-start.4 = (bf16[1024,512]{1,0:T(8,128)(2,1)}, bf16[1024,512]{1,0:T(8,128)(2,1)S(1)}, u32[]{:S(2)}, u32[]{:S(2)}) collective-permute-start(bf16[1024,512]{1,0:T(8,128)(2,1)} %bitcast.27), channel_id=1, source_target_pairs={{0,2},{2,0},{4,6},{6,4},{8,10},{10,8},{12,14},{14,12},{16,18},{18,... | collective-permute-start | bytes 3145736 | tf_op jit(solution)/shard_map/ppermute | solution.py:394
  4.3 15.2 %collective-permute-start.5 = (bf16[1024,512]{1,0:T(8,128)(2,1)}, bf16[1024,512]{1,0:T(8,128)(2,1)S(1)}, u32[]{:S(2)}, u32[]{:S(2)}) collective-permute-start(bf16[1024,512]{1,0:T(8,128)(2,1)} %bitcast.24), channel_id=1, source_target_pairs={{0,2},{2,0},{4,6},{6,4},{8,10},{10,8},{12,14},{14,12},{16,18},{18,... | collective-permute-start | bytes 3145736 | tf_op jit(solution)/shard_map/ppermute | solution.py:394
  5.1 7.6 %collective-permute-start.1 = (bf16[1,2,120,128]{3,2,1,0:T(8,128)(2,1)S(1)}, bf16[1,2,120,128]{3,2,1,0:T(8,128)(2,1)S(1)}, u32[]{:S(2)}, u32[]{:S(2)}) collective-permute-start(bf16[1,2,120,128]{3,2,1,0:T(8,128)(2,1)S(1)} %bitcast.32), channel_id=1, source_target_pairs={{0,16},{2,18},{4,20},{6,22},{8,24},{10,26},{12,28},{14,30},{16,0},... | collective-permute-start | bytes 184328 | tf_op jit(solution)/shard_map/ppermute | solution.py:394
  12.8 4.9 %collective-permute-start.2 = (bf16[2,2,120,128]{3,2,1,0:T(8,128)(2,1)S(1)}, bf16[2,2,120,128]{3,2,1,0:T(8,128)(2,1)S(1)}, u32[]{:S(2)}, u32[]{:S(2)}) collective-permute-start(bf16[2,2,120,128]{3,2,1,0:T(8,128)(2,1)S(1)} %pad_maximum_fusion.2), channel_id=1, source_target_pairs={{0,8},{2,10},{4,12},{6,14},{8,0},{10,2},{12,4},{14,6},{16,24},{18,... | collective-permute-start | bytes 368648 | tf_op jit(solution)/shard_map/ppermute | solution.py:394
  17.8 6.9 %collective-permute-start.3 = (bf16[4,2,96,128]{3,2,1,0:T(8,128)(2,1)S(1)}, bf16[4,2,96,128]{3,2,1,0:T(8,128)(2,1)S(1)}, u32[]{:S(2)}, u32[]{:S(2)}) collective-permute-start(bf16[4,2,96,128]{3,2,1,0:T(8,128)(2,1)S(1)} %slice.39.q_ref), channel_id=1, source_target_pairs={{0,4},{2,6},{4,0},{6,2},{8,12},{10,14},{12,8},{14,10},{16,20},{18,... | collective-permute-start | bytes 589832 | tf_op jit(solution)/shard_map/ppermute | solution.py:394
  19.5 34.4 %copy-start = (bf16[4096,512]{1,0:T(8,128)(2,1)S(1)}, bf16[4096,512]{1,0:T(8,128)(2,1)}, u32[]{:S(2)}) copy-start(bf16[4096,512]{1,0:T(8,128)(2,1)} %refs_4_.1) | copy-start | bytes 12582916
  22.7 5.8 %collective-permute-start.6 = (bf16[800,128]{1,0:T(8,128)(2,1)S(1)}, bf16[800,128]{1,0:T(8,128)(2,1)S(1)}, u32[]{:S(2)}, u32[]{:S(2)}) collective-permute-start(bf16[800,128]{1,0:T(8,128)(2,1)S(1)} %shard_map.103.rest_5_), channel_id=1, source_target_pairs={{0,4},{2,6},{4,0},{6,2},{8,12},{10,14},{12,8},{14,10},{16,20},{18,... | collective-permute-start | bytes 614408 | tf_op jit(solution)/shard_map/ppermute | solution.py:394
  27.9 29.3 %copy-start.1 = (bf16[1,1024,512]{2,1,0:T(8,128)(2,1)S(1)}, bf16[1,1024,512]{2,1,0:T(8,128)(2,1)}, u32[]{:S(2)}) copy-start(bf16[1,1024,512]{2,1,0:T(8,128)(2,1)} %param.12) | copy-start | bytes 3145732
  27.9 29.3 %copy-start.2 = (bf16[1,1024,512]{2,1,0:T(8,128)(2,1)S(1)}, bf16[1,1024,512]{2,1,0:T(8,128)(2,1)}, u32[]{:S(2)}) copy-start(bf16[1,1024,512]{2,1,0:T(8,128)(2,1)} %param.11) | copy-start | bytes 3145732
  28.9 4.8 %collective-permute-start.7 = (bf16[416,128]{1,0:T(8,128)(2,1)S(1)}, bf16[416,128]{1,0:T(8,128)(2,1)S(1)}, u32[]{:S(2)}, u32[]{:S(2)}) collective-permute-start(bf16[416,128]{1,0:T(8,128)(2,1)S(1)} %get-tuple-element.36), channel_id=1, source_target_pairs={{0,8},{2,10},{4,12},{6,14},{8,0},{10,2},{12,4},{14,6},{16,24},{18,... | collective-permute-start | bytes 319496 | tf_op jit(solution)/shard_map/ppermute | solution.py:394
  29.9 7.9 %collective-permute-start.9 = (bf16[4,2,24,128]{3,2,1,0:T(8,128)(2,1)S(1)}, bf16[4,2,24,128]{3,2,1,0:T(8,128)(2,1)S(1)}, u32[]{:S(2)}, u32[]{:S(2)}) collective-permute-start(bf16[4,2,24,128]{3,2,1,0:T(8,128)(2,1)S(1)} %slice.40), channel_id=1, source_target_pairs={{0,4},{2,6},{4,0},{6,2},{8,12},{10,14},{12,8},{14,10},{16,20},{18,... | collective-permute-start | bytes 147464 | tf_op jit(solution)/shard_map/ppermute | solution.py:394
  34.0 7.7 %collective-permute-start.8 = (bf16[416,128]{1,0:T(8,128)(2,1)S(1)}, bf16[416,128]{1,0:T(8,128)(2,1)S(1)}, u32[]{:S(2)}, u32[]{:S(2)}) collective-permute-start(bf16[416,128]{1,0:T(8,128)(2,1)S(1)} %get-tuple-element.39), channel_id=1, source_target_pairs={{0,16},{2,18},{4,20},{6,22},{8,24},{10,26},{12,28},{14,30},{16,0},... | collective-permute-start | bytes 319496 | tf_op jit(solution)/shard_map/ppermute | solution.py:394
  42.0 4.7 %collective-permute-start.10 = (bf16[2,2,96,128]{3,2,1,0:T(8,128)(2,1)S(1)}, bf16[2,2,96,128]{3,2,1,0:T(8,128)(2,1)S(1)}, u32[]{:S(2)}, u32[]{:S(2)}) collective-permute-start(bf16[2,2,96,128]{3,2,1,0:T(8,128)(2,1)S(1)} %bitcast.30), channel_id=1, source_target_pairs={{0,8},{2,10},{4,12},{6,14},{8,0},{10,2},{12,4},{14,6},{16,24},{18,... | collective-permute-start | bytes 294920 | tf_op jit(solution)/shard_map/ppermute | solution.py:394
  42.1 4.6 %collective-permute-start.11 = (bf16[8,2,24,128]{3,2,1,0:T(8,128)(2,1)S(1)}, bf16[8,2,24,128]{3,2,1,0:T(8,128)(2,1)S(1)}, u32[]{:S(2)}, u32[]{:S(2)}) collective-permute-start(bf16[8,2,24,128]{3,2,1,0:T(8,128)(2,1)S(1)} %pad_maximum_fusion.3.mine_ref), channel_id=1, source_target_pairs={{0,2},{2,0},{4,6},{6,4},{8,10},{10,8},{12,14},{14,12},{16,18},{18,... | collective-permute-start | bytes 294920 | tf_op jit(solution)/shard_map/ppermute | solution.py:394
  46.8 5.7 %collective-permute-start.12 = (bf16[4,2,96,128]{3,2,1,0:T(8,128)(2,1)S(1)}, bf16[4,2,96,128]{3,2,1,0:T(8,128)(2,1)S(1)}, u32[]{:S(2)}, u32[]{:S(2)}) collective-permute-start(bf16[4,2,96,128]{3,2,1,0:T(8,128)(2,1)S(1)} %pad_maximum_fusion.refs_0_), channel_id=1, source_target_pairs={{0,4},{2,6},{4,0},{6,2},{8,12},{10,14},{12,8},{14,10},{16,20},{18,... | collective-permute-start | bytes 589832 | tf_op jit(solution)/shard_map/ppermute | solution.py:394
  47.8 4.7 %collective-permute-start.13 = (bf16[4,2,96,128]{3,2,1,0:T(8,128)(2,1)S(1)}, bf16[4,2,96,128]{3,2,1,0:T(8,128)(2,1)S(1)}, u32[]{:S(2)}, u32[]{:S(2)}) collective-permute-start(bf16[4,2,96,128]{3,2,1,0:T(8,128)(2,1)S(1)} %pad_maximum_fusion.refs_0_), channel_id=1, source_target_pairs={{0,2},{2,0},{4,6},{6,4},{8,10},{10,8},{12,14},{14,12},{16,18},{18,... | collective-permute-start | bytes 589832 | tf_op jit(solution)/shard_map/ppermute | solution.py:394
  52.5 1.4 %collective-permute-start.14 = (bf16[4,2,96,128]{3,2,1,0:T(8,128)(2,1)S(1)}, bf16[4,2,96,128]{3,2,1,0:T(8,128)(2,1)S(1)}, u32[]{:S(2)}, u32[]{:S(2)}) collective-permute-start(bf16[4,2,96,128]{3,2,1,0:T(8,128)(2,1)S(1)} %collective-permute-done.12.refs_1_), channel_id=1, source_target_pairs={{0,2},{2,0},{4,6},{6,4},{8,10},{10,8},{12,14},{14,12},{16,18},{18,... | collective-permute-start | bytes 589832 | tf_op jit(solution)/shard_map/ppermute | solution.py:394
  54.9 4.9 %collective-permute-start.15 = (f32[48,512]{1,0:T(8,128)S(1)}, f32[48,512]{1,0:T(8,128)S(1)}, u32[]{:S(2)}, u32[]{:S(2)}) collective-permute-start(f32[48,512]{1,0:T(8,128)S(1)} %get-tuple-element.44.rest_0_), channel_id=1, source_target_pairs={{0,1},{1,0},{2,3},{3,2},{4,5},{5,4},{6,7},{7,6},{8,9},{9,8},{10,11... | collective-permute-start | bytes 294920 | tf_op jit(solution)/shard_map/ppermute | solution.py:460

commit v3 on v2

--- a/solution.py
+++ b/solution.py
@@ -62,14 +62,14 @@
     return place + jnp.where(place < local_rows, core, -core) * local_rows
 
 
-def attend_kernel(rel, unit_rows, split, as_message, n_after, len_ref, q_ref, *rest):
+def attend_kernel(rel, unit_rows, split, as_message, n_after, scal, q_ref, *rest):
     caches = rest[: 2 * split]
     d_ref = rest[2 * split]
     outs = rest[2 * split + 1 + n_after :]
     units, heads = q_ref.shape[:2]
     unit = unit_rows * GROUP
     keys = caches[0].shape[0]
-    seq, length = lax.axis_index("seq"), len_ref[0]
+    seq, length = lax.axis_index("seq"), scal[0:1, 0:1]
     chip = lax.div(seq, split)
     count = units * heads
     count8 = round_up(count, 8)
@@ -146,7 +146,7 @@
         outs[1][...] = stats[: 2 * count8]
 
 
-def attend(length, q, rel, unit_rows, split, caches, drafts, as_message, after=()):
+def attend(scal, q, rel, unit_rows, split, caches, drafts, as_message, after=()):
     units, heads = q.shape[:2]
     unit = unit_rows * GROUP
     keys = caches[0].shape[0]
@@ -158,29 +158,27 @@
             jax.ShapeDtypeStruct((count * unit, LANES), f32),
             jax.ShapeDtypeStruct((2 * round_up(count, 8), LANES), f32),
         )
-    cache_spec = pl.BlockSpec((keys, heads * HD), lambda i, s: (0, 0))
+    whole = pl.BlockSpec(memory_space=pltpu.VMEM)
+    cache_spec = pl.BlockSpec((keys, heads * HD), lambda i: (0, 0))
     other_spec = pl.BlockSpec(
-        (keys, heads * HD), lambda i, s: (0, lax.rem(lax.axis_index("seq"), split))
-    )
-    in_specs = [pl.BlockSpec(q.shape, lambda i, s: (0, 0, 0, 0))]
+        (keys, heads * HD), lambda i: (0, lax.rem(lax.axis_index("seq"), split))
+    )
+    in_specs = [whole, pl.BlockSpec(q.shape, lambda i: (0, 0, 0, 0))]
     in_specs += [cache_spec] * 2 + [other_spec] * (len(caches) - 2)
-    in_specs += [pl.BlockSpec(drafts.shape, lambda i, s: (0, 0, 0))]
+    in_specs += [pl.BlockSpec(drafts.shape, lambda i: (0, 0, 0))]
     in_specs += [pl.BlockSpec(memory_space=pl.ANY)] * len(after)
     scores = count * unit * (split * keys + LANES)
     return pl.pallas_call(
         functools.partial(attend_kernel, rel, unit_rows, split, as_message, len(after)),
-        grid_spec=pltpu.PrefetchScalarGridSpec(
-            num_scalar_prefetch=1,
-            grid=(1,),
-            in_specs=in_specs,
-            out_specs=tuple(pl.BlockSpec(o.shape, lambda i, s: (0, 0)) for o in out_shape),
-        ),
+        grid=(1,),
+        in_specs=in_specs,
+        out_specs=tuple(pl.BlockSpec(o.shape, lambda i: (0, 0)) for o in out_shape),
         out_shape=out_shape,
         compiler_params=pltpu.CompilerParams(vmem_limit_bytes=VMEM_BYTES),
         cost_estimate=pl.CostEstimate(
             flops=4 * scores * HD, bytes_accessed=4 * split * keys * heads * HD, transcendentals=scores
         ),
-    )(length, q, *caches, drafts, *after)
+    )(scal, q, *caches, drafts, *after)
 
 
 def merge_kernel(unit, mode, num_ref, stat_ref, msg_ref, *outs):
@@ -289,7 +287,7 @@
     result = jnp.dot(lhs_ref[...], w_ref[...], preferred_element_type=f32)
     if n_head == 2:
         outs[0][...] = result[: rows // 2]
-        outs[1][...] = result[rows // 2 :]
+        outs[1][...] = result[rows // 2 :].astype(bf16)
     else:
         outs[0][...] = result
 
@@ -300,7 +298,7 @@
     rows = 2 * units * unit // GROUP
     columns = weight.shape[1]
     if n_head == 2:
-        out_shape = (jax.ShapeDtypeStruct((rows // 2, columns), f32),) * 2
+        out_shape = tuple(jax.ShapeDtypeStruct((rows // 2, columns), t) for t in (f32, bf16))
     else:
         out_shape = (jax.ShapeDtypeStruct((rows, columns), f32),)
     return pl.pallas_call(
@@ -315,14 +313,14 @@
     )(*sources, weight)
 
 
-def append_kernel(rel, split, unit_rows, len_ref, acc_ref, ck_ref, cv_ref, mine_ref, other_ref, *rest):
+def append_kernel(rel, split, unit_rows, scal, ck_ref, cv_ref, mine_ref, other_ref, *rest):
     nk_ref, nv_ref = rest[-2:]
     rows, width = ck_ref.shape
     chips, heads, both, _ = mine_ref.shape
     local_rows = unit_rows // split
     seq = lax.axis_index("seq")
     chip, core = lax.div(seq, split), lax.rem(seq, split)
-    length, accepted = len_ref[0], acc_ref[0]
+    length, accepted = jnp.max(scal[0:1]), jnp.max(scal[1:2])
     first = (seq * pl.num_programs(0) + pl.program_id(0)) * rows - length
     touched = (first < accepted) & (first + rows > 0)
 
@@ -359,7 +357,7 @@
                     ).astype(bf16)
 
 
-def append(rel, split, unit_rows, length, accepted, ck, cv, drafts, after):
+def append(rel, split, unit_rows, scal, ck, cv, drafts, after):
     rows = ck.shape[0]
     block = rows // 4 if rows % 64 == 0 else rows
     cache_spec = pl.BlockSpec((block, ck.shape[1]), lambda i: (i, 0))
@@ -369,14 +367,14 @@
     return pl.pallas_call(
         functools.partial(append_kernel, rel, split, unit_rows),
         grid=(rows // block,),
-        in_specs=[pl.BlockSpec(memory_space=pltpu.SMEM)] * 2
+        in_specs=[pl.BlockSpec(memory_space=pltpu.VMEM)]
         + [cache_spec, cache_spec, draft_spec, draft_spec]
         + [pl.BlockSpec(memory_space=pl.ANY)] * len(after),
         out_specs=(cache_spec, cache_spec),
         out_shape=(shape, shape),
         compiler_params=pltpu.CompilerParams(vmem_limit_bytes=VMEM_BYTES),
         cost_estimate=pl.CostEstimate(flops=0, bytes_accessed=8 * ck.size, transcendentals=0),
-    )(length, accepted, ck, cv, mine, other, *after)
+    )(scal, ck, cv, mine, other, *after)
 
 
 def one_request(n_seq, n_head, dq, dk, dv, ck, cv, accepted, length, weight):
@@ -413,14 +411,17 @@
     d_key, d_value = q[:, unit : unit + unit_rows], q[:, unit + unit_rows :]
     spare = ((0, 0), (0, LANES - unit_rows), (0, 0))
     drafts = jnp.concatenate([jnp.pad(d_key, spare), jnp.pad(d_value, spare)], axis=1)
-    q = q[None]
+    q, scal = lax.optimization_barrier(
+        (q[None], jnp.broadcast_to(jnp.stack([length, accepted]), (2, LANES)))
+    )
     if split == 2:
         q, ck_late, cv_late = lax.optimization_barrier((q, ck, cv))
         caches += [swap(ck_late, 0), swap(cv_late, 0)]
 
-    rel = [0]
+    rel, near = [0], bits[-1]
     for bit in bits[:-1]:
-        q = jnp.concatenate([q, swap(q, bit)], axis=0)
+        new = swap(q, bit)
+        q = jnp.concatenate([q, new], axis=0)
         if split == 2 and bit == bits[0]:
             q, *own = lax.optimization_barrier((q, ck, cv))
             caches[:2] = [
@@ -428,11 +429,10 @@
             ]
         rel = rel + [r | (1 << bit) // split for r in rel]
     q, dkv = q[:, :, :unit], q[:, :, unit:]
-    near = bits[-1]
     rel_far = [r | (1 << near) // split for r in rel]
     q_far = swap(q, near)
 
-    run = functools.partial(attend, length)
+    run = functools.partial(attend, scal)
     (message,) = run(q, rel, unit_rows, split, caches, drafts, True)
     num, stats = run(q_far, rel_far, unit_rows, split, caches, drafts, False, (message,))
     message = swap(message, near)
@@ -457,11 +457,11 @@
     result = project((rel_far, rel), split, n_head, sources, weight)
     if n_head == 2:
         keep, send = result
-        projected = keep + lax.ppermute(send, "head", [(0, 1), (1, 0)])
+        projected = keep + lax.ppermute(send, "head", [(0, 1), (1, 0)]).astype(f32)
     else:
         projected = lax.psum_scatter(result[0], "head", scatter_dimension=0, tiled=True)
     new_key, new_value = append(
-        rel + rel_far, split, unit_rows, length, accepted, ck, cv, every, (result[-1],)
+        rel + rel_far, split, unit_rows, scal, ck, cv, every, (result[-1],)
     )
     return projected.astype(bf16), new_key, new_value
 

time: 60.7 us -> 59.8 us (0.985)
  waiting for transfers between devices: 27.4 us -> 26.2 us
    ppermute x15, waiting for transfers between devices: 26.6 us -> 25.9 us  [swap(): return lax.ppermute(x, 'seq', [(i, i ^ 1 << bit) for i in range(n_seq)])]
  transfers between devices with their start and end apart: 16 -> 16, of which waited for: 11 -> 10; matrix products, arithmetic and copies ran while one was open for 2% -> 3% of each run, Pallas kernels for 14% -> 15%
where the time goes in v3:
time: 59.8 us; the launch traced here: 59.5 us
  waiting for transfers between devices  26.2 us (44%)
  starting transfers between devices  16.4 us (27%)
  Pallas kernels  10.8 us (18%)
  local copies, waits for them, and re-layouts  2.54 us (4%)
  between operations  2.1 us (4%)
  other arithmetic  1.5 us (3%)
    ppermute x15, waiting for transfers between devices, swap(): return lax.ppermute(x, 'seq', [(i, i ^ 1 << bit) for i in range(n_seq)])  25.9 us
    ppermute x15, starting transfers between devices, swap(): return lax.ppermute(x, 'seq', [(i, i ^ 1 << bit) for i in range(n_seq)])  14.8 us
    pallas_call x2, Pallas kernels, attend(): pl.pallas_call(functools.partial(attend_kernel, rel, unit_rows, split, as...  6.58 us
    pallas_call x1, Pallas kernels, append(): pl.pallas_call(functools.partial(append_kernel, rel, split, unit_rows), g...  2.31 us
    ppermute x1, starting transfers between devices, one_request(): projected = keep + lax.ppermute(send, 'head', [(0, 1), (1, 0)]).astype(f32)  1.59 us
    dynamic_slice x1, local copies, waits for them, and re-layouts, one_request(): lax.dynamic_slice_in_dim(c, core * heads * HD, heads * HD, 1)  1.27 us
  transfers between devices with their start and end apart: 16, of which 10 were waited for; matrix products, arithmetic and copies ran while one was open for 3% of the time, Pallas kernels for 15%

profile of v3, /device:TPU:0, one launch (start us, length us, event | category | flops | bytes accessed | tf_op | source)
XLA Modules:
  0.0 59.5 jit_solution(11848751561995255603)
XLA Ops:
  0.6 0.8 %copy_bitcast_fusion.1 = bf16[4,48,128]{2,1,0:T(8,128)(2,1)S(1)} fusion(bf16[1,6,32,128]{3,1,2,0:T(8,128)(2,1)} %bitcast.40), kind=kLoop, calls=%fused_computation.15 | loop fusion | bytes 98304 | tf_op jit(solution)/shard_map/reshape | solution.py:397
  1.5 0.7 %pad_maximum_fusion.4 = bf16[4,60,128]{2,1,0:T(8,128)(2,1)S(1)} fusion(bf16[4,6,128]{2,1,0:T(8,128)(2,1)} %bitcast.41, bf16[4,6,128]{2,1,0:T(8,128)(2,1)} %bitcast.42, bf16[4,48,128]{2,1,0:T(8,128)(2,1)S(1)} %copy_bitcast_fusion.1), kind=kLoop, calls=%fused_computation.12 | loop fusion | flops 184320 | bytes 122880 | tf_op jit(solution)/shard_map/concatenate | solution.py:400
  5.0 3.7 %collective-permute-start.1 = (bf16[1,2,120,128]{3,2,1,0:T(8,128)(2,1)S(1)}, bf16[1,2,120,128]{3,2,1,0:T(8,128)(2,1)S(1)}, u32[]{:S(2)}, u32[]{:S(2)}) collective-permute-start(bf16[1,2,120,128]{3,2,1,0:T(8,128)(2,1)S(1)} %bitcast.38), channel_id=1, source_target_pairs={{0,16},{2,18},{4,20},{6,22},{8,24},{10,26},{12,28},{14,30},{16,0},... | collective-permute-start | bytes 184328 | tf_op jit(solution)/shard_map/ppermute | solution.py:392
  8.7 3.9 %collective-permute-done.1 = bf16[1,2,120,128]{3,2,1,0:T(8,128)(2,1)S(1)} collective-permute-done((bf16[1,2,120,128]{3,2,1,0:T(8,128)(2,1)S(1)}, bf16[1,2,120,128]{3,2,1,0:T(8,128)(2,1)S(1)}, u32[]{:S(2)}, u32[]{:S(2)}) %collective-permute-start.1) | collective-permute-done | bytes 61472 | tf_op jit(solution)/shard_map/ppermute | solution.py:392
  12.6 0.8 %collective-permute-start.2 = (bf16[2,2,120,128]{3,2,1,0:T(8,128)(2,1)S(1)}, bf16[2,2,120,128]{3,2,1,0:T(8,128)(2,1)S(1)}, u32[]{:S(2)}, u32[]{:S(2)}) collective-permute-start(bf16[2,2,120,128]{3,2,1,0:T(8,128)(2,1)S(1)} %pad_maximum_fusion.2), channel_id=1, source_target_pairs={{0,8},{2,10},{4,12},{6,14},{8,0},{10,2},{12,4},{14,6},{16,24},{18,... | collective-permute-start | bytes 368648 | tf_op jit(solution)/shard_map/ppermute | solution.py:392
  13.4 1.3 %constant_dynamic-slice_fusion.2 = (bf16[1024,256]{1,0:T(8,128)(2,1)S(1)}, bf16[1024,256]{1,0:T(8,128)(2,1)S(1)}) fusion(bf16[1024,512]{1,0:T(8,128)(2,1)} %bitcast.31, s32[]{:T(128)S(6)} %select_n.20, bf16[1024,512]{1,0:T(8,128)(2,1)} %bitcast.34), kind=kLoop, calls=%fused_computation.20 | loop fusion | bytes 2097156 | tf_op jit(solution)/shard_map/dynamic_slice | solution.py:428
  14.7 2.8 %collective-permute-done.2 = bf16[2,2,120,128]{3,2,1,0:T(8,128)(2,1)S(1)} collective-permute-done((bf16[2,2,120,128]{3,2,1,0:T(8,128)(2,1)S(1)}, bf16[2,2,120,128]{3,2,1,0:T(8,128)(2,1)S(1)}, u32[]{:S(2)}, u32[]{:S(2)}) %collective-permute-start.2) | collective-permute-done | bytes 122912 | tf_op jit(solution)/shard_map/ppermute | solution.py:392
  17.6 1.6 %collective-permute-start.3 = (bf16[4,2,96,128]{3,2,1,0:T(8,128)(2,1)S(1)}, bf16[4,2,96,128]{3,2,1,0:T(8,128)(2,1)S(1)}, u32[]{:S(2)}, u32[]{:S(2)}) collective-permute-start(bf16[4,2,96,128]{3,2,1,0:T(8,128)(2,1)S(1)} %slice.39.q_ref), channel_id=1, source_target_pairs={{0,4},{2,6},{4,0},{6,2},{8,12},{10,14},{12,8},{14,10},{16,20},{18,... | collective-permute-start | bytes 589832 | tf_op jit(solution)/shard_map/ppermute | solution.py:392
  19.3 3.3 %shard_map.103.rest_5_ = bf16[800,128]{1,0:T(8,128)(2,1)S(1)} custom-call(s32[2,128]{1,0:T(2,128)S(1)} %broadcast_in_dim.12.scal, bf16[4,2,96,128]{3,2,1,0:T(8,128)(2,1)S(1)} %slice.39.q_ref, bf16[1024,256]{1,0:T(8,128)(2,1)S(1)} %get-tuple-element.60.rest_0_, bf16[1024,256]{1,0:T(8,128)(2,1)S(1)} %get-tuple-element.59.rest_1_, ...), custom_call_target="tpu_custom_call" | custom-call | flops 855638016 | bytes 2097152 | tf_op jit(solution)/shard_map/pallas_call | solution.py:171
  23.0 1.1 %collective-permute-done.3.q_ref = bf16[4,2,96,128]{3,2,1,0:T(8,128)(2,1)S(1)} collective-permute-done((bf16[4,2,96,128]{3,2,1,0:T(8,128)(2,1)S(1)}, bf16[4,2,96,128]{3,2,1,0:T(8,128)(2,1)S(1)}, u32[]{:S(2)}, u32[]{:S(2)}) %collective-permute-start.3) | collective-permute-done | bytes 196640 | tf_op jit(solution)/shard_map/ppermute | solution.py:392
  24.1 3.3 %shard_map.104 = (f32[768,128]{1,0:T(8,128)S(1)}, f32[16,128]{1,0:T(8,128)S(1)}) custom-call(s32[2,128]{1,0:T(2,128)S(1)} %broadcast_in_dim.12.scal, bf16[4,2,96,128]{3,2,1,0:T(8,128)(2,1)S(1)} %collective-permute-done.3.q_ref, bf16[1024,256]{1,0:T(8,128)(2,1)S(1)} %get-tuple-element.60.rest_0_, bf16[1024,256]{1,0:T(8,128)(2,1)S(1)} %get-tuple-element.59.rest_1_, ...), custom_call_target="tpu_custom_call" | custom-call | flops 855638016 | bytes 2097152 | tf_op jit(solution)/shard_map/pallas_call | solution.py:171
  27.4 0.9 %collective-permute-done.6.msg_ref = bf16[800,128]{1,0:T(8,128)(2,1)S(1)} collective-permute-done((bf16[800,128]{1,0:T(8,128)(2,1)S(1)}, bf16[800,128]{1,0:T(8,128)(2,1)S(1)}, u32[]{:S(2)}, u32[]{:S(2)}) %collective-permute-start.6) | collective-permute-done | bytes 204832 | tf_op jit(solution)/shard_map/ppermute | solution.py:392
  28.7 1.3 %collective-permute-start.7 = (bf16[416,128]{1,0:T(8,128)(2,1)S(1)}, bf16[416,128]{1,0:T(8,128)(2,1)S(1)}, u32[]{:S(2)}, u32[]{:S(2)}) collective-permute-start(bf16[416,128]{1,0:T(8,128)(2,1)S(1)} %get-tuple-element.40), channel_id=1, source_target_pairs={{0,8},{2,10},{4,12},{6,14},{8,0},{10,2},{12,4},{14,6},{16,24},{18,... | collective-permute-start | bytes 319496 | tf_op jit(solution)/shard_map/ppermute | solution.py:392
  30.1 1.1 %collective-permute-start.9 = (bf16[4,2,24,128]{3,2,1,0:T(8,128)(2,1)S(1)}, bf16[4,2,24,128]{3,2,1,0:T(8,128)(2,1)S(1)}, u32[]{:S(2)}, u32[]{:S(2)}) collective-permute-start(bf16[4,2,24,128]{3,2,1,0:T(8,128)(2,1)S(1)} %slice.40), channel_id=1, source_target_pairs={{0,4},{2,6},{4,0},{6,2},{8,12},{10,14},{12,8},{14,10},{16,20},{18,... | collective-permute-start | bytes 147464 | tf_op jit(solution)/shard_map/ppermute | solution.py:392
  31.2 2.3 %collective-permute-done.7.msg_ref = bf16[416,128]{1,0:T(8,128)(2,1)S(1)} collective-permute-done((bf16[416,128]{1,0:T(8,128)(2,1)S(1)}, bf16[416,128]{1,0:T(8,128)(2,1)S(1)}, u32[]{:S(2)}, u32[]{:S(2)}) %collective-permute-start.7) | collective-permute-done | bytes 106528 | tf_op jit(solution)/shard_map/ppermute | solution.py:392
  33.8 3.8 %collective-permute-start.8 = (bf16[416,128]{1,0:T(8,128)(2,1)S(1)}, bf16[416,128]{1,0:T(8,128)(2,1)S(1)}, u32[]{:S(2)}, u32[]{:S(2)}) collective-permute-start(bf16[416,128]{1,0:T(8,128)(2,1)S(1)} %get-tuple-element.43), channel_id=1, source_target_pairs={{0,16},{2,18},{4,20},{6,22},{8,24},{10,26},{12,28},{14,30},{16,0},... | collective-permute-start | bytes 319496 | tf_op jit(solution)/shard_map/ppermute | solution.py:392
  37.6 3.9 %collective-permute-done.8.msg_ref = bf16[416,128]{1,0:T(8,128)(2,1)S(1)} collective-permute-done((bf16[416,128]{1,0:T(8,128)(2,1)S(1)}, bf16[416,128]{1,0:T(8,128)(2,1)S(1)}, u32[]{:S(2)}, u32[]{:S(2)}) %collective-permute-start.8) | collective-permute-done | bytes 106528 | tf_op jit(solution)/shard_map/ppermute | solution.py:392
  42.0 4.5 %collective-permute-done.10 = bf16[2,2,96,128]{3,2,1,0:T(8,128)(2,1)S(1)} collective-permute-done((bf16[2,2,96,128]{3,2,1,0:T(8,128)(2,1)S(1)}, bf16[2,2,96,128]{3,2,1,0:T(8,128)(2,1)S(1)}, u32[]{:S(2)}, u32[]{:S(2)}) %collective-permute-start.10) | collective-permute-done | bytes 98336 | tf_op jit(solution)/shard_map/ppermute | solution.py:392
  46.6 0.7 %collective-permute-start.12 = (bf16[4,2,96,128]{3,2,1,0:T(8,128)(2,1)S(1)}, bf16[4,2,96,128]{3,2,1,0:T(8,128)(2,1)S(1)}, u32[]{:S(2)}, u32[]{:S(2)}) collective-permute-start(bf16[4,2,96,128]{3,2,1,0:T(8,128)(2,1)S(1)} %pad_maximum_fusion.refs_0_), channel_id=1, source_target_pairs={{0,4},{2,6},{4,0},{6,2},{8,12},{10,14},{12,8},{14,10},{16,20},{18,... | collective-permute-start | bytes 589832 | tf_op jit(solution)/shard_map/ppermute | solution.py:392
  47.3 5.0 %collective-permute-done.12.refs_1_ = bf16[4,2,96,128]{3,2,1,0:T(8,128)(2,1)S(1)} collective-permute-done((bf16[4,2,96,128]{3,2,1,0:T(8,128)(2,1)S(1)}, bf16[4,2,96,128]{3,2,1,0:T(8,128)(2,1)S(1)}, u32[]{:S(2)}, u32[]{:S(2)}) %collective-permute-start.12) | collective-permute-done | bytes 196640 | tf_op jit(solution)/shard_map/ppermute | solution.py:392
  52.3 1.4 %collective-permute-done.14.refs_3_ = bf16[4,2,96,128]{3,2,1,0:T(8,128)(2,1)S(1)} collective-permute-done((bf16[4,2,96,128]{3,2,1,0:T(8,128)(2,1)S(1)}, bf16[4,2,96,128]{3,2,1,0:T(8,128)(2,1)S(1)}, u32[]{:S(2)}, u32[]{:S(2)}) %collective-permute-start.14) | collective-permute-done | bytes 196640 | tf_op jit(solution)/shard_map/ppermute | solution.py:392
  53.8 0.9 %shard_map.108 = (f32[48,512]{1,0:T(8,128)S(1)}, bf16[48,512]{1,0:T(8,128)(2,1)S(1)}) custom-call(bf16[4,2,96,128]{3,2,1,0:T(8,128)(2,1)S(1)} %pad_maximum_fusion.refs_0_, bf16[4,2,96,128]{3,2,1,0:T(8,128)(2,1)S(1)} %collective-permute-done.12.refs_1_, bf16[4,2,96,128]{3,2,1,0:T(8,128)(2,1)S(1)} %collective-permute-done.13.refs_2_, ...), custom_call_target="tpu_custom_call" | custom-call | tf_op jit(solution)/shard_map/pallas_call | solution.py:304
  54.7 1.6 %collective-permute-start.15 = (bf16[48,512]{1,0:T(8,128)(2,1)S(1)}, bf16[48,512]{1,0:T(8,128)(2,1)S(1)}, u32[]{:S(2)}, u32[]{:S(2)}) collective-permute-start(bf16[48,512]{1,0:T(8,128)(2,1)S(1)} %get-tuple-element.48.rest_0_), channel_id=1, source_target_pairs={{0,1},{1,0},{2,3},{3,2},{4,5},{5,4},{6,7},{7,6},{8,9},{9,8},{10,11... | collective-permute-start | bytes 147464 | tf_op jit(solution)/shard_map/ppermute | solution.py:460
  56.3 2.3 %shard_map.109 = (bf16[1024,512]{1,0:T(8,128)(2,1)}, bf16[1024,512]{1,0:T(8,128)(2,1)}) custom-call(s32[2,128]{1,0:T(2,128)S(1)} %broadcast_in_dim.12.scal, bf16[1024,512]{1,0:T(8,128)(2,1)S(1)} %bitcast.35, bf16[1024,512]{1,0:T(8,128)(2,1)S(1)} %bitcast.32, bf16[8,2,24,128]{3,2,1,0:T(8,128)(2,1)S(1)} %pad_maximum_fusion.3.mine_ref, ...), custom_call_target="tpu_custom_call" | custom-call | bytes 4194304 | tf_op jit(solution)/shard_map/pallas_call | solution.py:367
  (42 shorter events, 4.1 us)
Async XLA Ops:
  2.2 1.9 %collective-permute-start = (bf16[2,60,128]{2,1,0:T(8,128)(2,1)S(1)}, bf16[2,60,128]{2,1,0:T(8,128)(2,1)S(1)}, u32[]{:S(2)}, u32[]{:S(2)}) collective-permute-start(bf16[2,60,128]{2,1,0:T(8,128)(2,1)S(1)} %constant_dynamic-slice_fusion.4), channel_id=1, source_target_pairs={{0,2},{2,0},{4,6},{6,4},{8,10},{10,8},{12,14},{14,12},{16,18},{18,... | collective-permute-start | bytes 92168 | tf_op jit(solution)/shard_map/ppermute | solution.py:392
  4.5 14.7 %collective-permute-start.4 = (bf16[1024,512]{1,0:T(8,128)(2,1)}, bf16[1024,512]{1,0:T(8,128)(2,1)S(1)}, u32[]{:S(2)}, u32[]{:S(2)}) collective-permute-start(bf16[1024,512]{1,0:T(8,128)(2,1)} %bitcast.33), channel_id=1, source_target_pairs={{0,2},{2,0},{4,6},{6,4},{8,10},{10,8},{12,14},{14,12},{16,18},{18,... | collective-permute-start | bytes 3145736 | tf_op jit(solution)/shard_map/ppermute | solution.py:392
  4.6 14.7 %collective-permute-start.5 = (bf16[1024,512]{1,0:T(8,128)(2,1)}, bf16[1024,512]{1,0:T(8,128)(2,1)S(1)}, u32[]{:S(2)}, u32[]{:S(2)}) collective-permute-start(bf16[1024,512]{1,0:T(8,128)(2,1)} %bitcast.30), channel_id=1, source_target_pairs={{0,2},{2,0},{4,6},{6,4},{8,10},{10,8},{12,14},{14,12},{16,18},{18,... | collective-permute-start | bytes 3145736 | tf_op jit(solution)/shard_map/ppermute | solution.py:392
  5.0 7.6 %collective-permute-start.1 = (bf16[1,2,120,128]{3,2,1,0:T(8,128)(2,1)S(1)}, bf16[1,2,120,128]{3,2,1,0:T(8,128)(2,1)S(1)}, u32[]{:S(2)}, u32[]{:S(2)}) collective-permute-start(bf16[1,2,120,128]{3,2,1,0:T(8,128)(2,1)S(1)} %bitcast.38), channel_id=1, source_target_pairs={{0,16},{2,18},{4,20},{6,22},{8,24},{10,26},{12,28},{14,30},{16,0},... | collective-permute-start | bytes 184328 | tf_op jit(solution)/shard_map/ppermute | solution.py:392
  12.6 4.9 %collective-permute-start.2 = (bf16[2,2,120,128]{3,2,1,0:T(8,128)(2,1)S(1)}, bf16[2,2,120,128]{3,2,1,0:T(8,128)(2,1)S(1)}, u32[]{:S(2)}, u32[]{:S(2)}) collective-permute-start(bf16[2,2,120,128]{3,2,1,0:T(8,128)(2,1)S(1)} %pad_maximum_fusion.2), channel_id=1, source_target_pairs={{0,8},{2,10},{4,12},{6,14},{8,0},{10,2},{12,4},{14,6},{16,24},{18,... | collective-permute-start | bytes 368648 | tf_op jit(solution)/shard_map/ppermute | solution.py:392
  17.6 6.5 %collective-permute-start.3 = (bf16[4,2,96,128]{3,2,1,0:T(8,128)(2,1)S(1)}, bf16[4,2,96,128]{3,2,1,0:T(8,128)(2,1)S(1)}, u32[]{:S(2)}, u32[]{:S(2)}) collective-permute-start(bf16[4,2,96,128]{3,2,1,0:T(8,128)(2,1)S(1)} %slice.39.q_ref), channel_id=1, source_target_pairs={{0,4},{2,6},{4,0},{6,2},{8,12},{10,14},{12,8},{14,10},{16,20},{18,... | collective-permute-start | bytes 589832 | tf_op jit(solution)/shard_map/ppermute | solution.py:392
  19.2 34.5 %copy-start = (bf16[4096,512]{1,0:T(8,128)(2,1)S(1)}, bf16[4096,512]{1,0:T(8,128)(2,1)}, u32[]{:S(2)}) copy-start(bf16[4096,512]{1,0:T(8,128)(2,1)} %refs_4_.1) | copy-start | bytes 12582916
  22.5 5.8 %collective-permute-start.6 = (bf16[800,128]{1,0:T(8,128)(2,1)S(1)}, bf16[800,128]{1,0:T(8,128)(2,1)S(1)}, u32[]{:S(2)}, u32[]{:S(2)}) collective-permute-start(bf16[800,128]{1,0:T(8,128)(2,1)S(1)} %shard_map.103.rest_5_), channel_id=1, source_target_pairs={{0,4},{2,6},{4,0},{6,2},{8,12},{10,14},{12,8},{14,10},{16,20},{18,... | collective-permute-start | bytes 614408 | tf_op jit(solution)/shard_map/ppermute | solution.py:392
  27.4 28.9 %copy-start.1 = (bf16[1,1024,512]{2,1,0:T(8,128)(2,1)S(1)}, bf16[1,1024,512]{2,1,0:T(8,128)(2,1)}, u32[]{:S(2)}) copy-start(bf16[1,1024,512]{2,1,0:T(8,128)(2,1)} %param.12) | copy-start | bytes 3145732
  27.4 28.9 %copy-start.2 = (bf16[1,1024,512]{2,1,0:T(8,128)(2,1)S(1)}, bf16[1,1024,512]{2,1,0:T(8,128)(2,1)}, u32[]{:S(2)}) copy-start(bf16[1,1024,512]{2,1,0:T(8,128)(2,1)} %param.11) | copy-start | bytes 3145732
  28.7 4.8 %collective-permute-start.7 = (bf16[416,128]{1,0:T(8,128)(2,1)S(1)}, bf16[416,128]{1,0:T(8,128)(2,1)S(1)}, u32[]{:S(2)}, u32[]{:S(2)}) collective-permute-start(bf16[416,128]{1,0:T(8,128)(2,1)S(1)} %get-tuple-element.40), channel_id=1, source_target_pairs={{0,8},{2,10},{4,12},{6,14},{8,0},{10,2},{12,4},{14,6},{16,24},{18,... | collective-permute-start | bytes 319496 | tf_op jit(solution)/shard_map/ppermute | solution.py:392
  30.1 7.6 %collective-permute-start.9 = (bf16[4,2,24,128]{3,2,1,0:T(8,128)(2,1)S(1)}, bf16[4,2,24,128]{3,2,1,0:T(8,128)(2,1)S(1)}, u32[]{:S(2)}, u32[]{:S(2)}) collective-permute-start(bf16[4,2,24,128]{3,2,1,0:T(8,128)(2,1)S(1)} %slice.40), channel_id=1, source_target_pairs={{0,4},{2,6},{4,0},{6,2},{8,12},{10,14},{12,8},{14,10},{16,20},{18,... | collective-permute-start | bytes 147464 | tf_op jit(solution)/shard_map/ppermute | solution.py:392
  33.8 7.7 %collective-permute-start.8 = (bf16[416,128]{1,0:T(8,128)(2,1)S(1)}, bf16[416,128]{1,0:T(8,128)(2,1)S(1)}, u32[]{:S(2)}, u32[]{:S(2)}) collective-permute-start(bf16[416,128]{1,0:T(8,128)(2,1)S(1)} %get-tuple-element.43), channel_id=1, source_target_pairs={{0,16},{2,18},{4,20},{6,22},{8,24},{10,26},{12,28},{14,30},{16,0},... | collective-permute-start | bytes 319496 | tf_op jit(solution)/shard_map/ppermute | solution.py:392
  41.9 4.7 %collective-permute-start.10 = (bf16[2,2,96,128]{3,2,1,0:T(8,128)(2,1)S(1)}, bf16[2,2,96,128]{3,2,1,0:T(8,128)(2,1)S(1)}, u32[]{:S(2)}, u32[]{:S(2)}) collective-permute-start(bf16[2,2,96,128]{3,2,1,0:T(8,128)(2,1)S(1)} %bitcast.36), channel_id=1, source_target_pairs={{0,8},{2,10},{4,12},{6,14},{8,0},{10,2},{12,4},{14,6},{16,24},{18,... | collective-permute-start | bytes 294920 | tf_op jit(solution)/shard_map/ppermute | solution.py:392
  42.0 4.6 %collective-permute-start.11 = (bf16[8,2,24,128]{3,2,1,0:T(8,128)(2,1)S(1)}, bf16[8,2,24,128]{3,2,1,0:T(8,128)(2,1)S(1)}, u32[]{:S(2)}, u32[]{:S(2)}) collective-permute-start(bf16[8,2,24,128]{3,2,1,0:T(8,128)(2,1)S(1)} %pad_maximum_fusion.3.mine_ref), channel_id=1, source_target_pairs={{0,2},{2,0},{4,6},{6,4},{8,10},{10,8},{12,14},{14,12},{16,18},{18,... | collective-permute-start | bytes 294920 | tf_op jit(solution)/shard_map/ppermute | solution.py:392
  46.6 5.7 %collective-permute-start.12 = (bf16[4,2,96,128]{3,2,1,0:T(8,128)(2,1)S(1)}, bf16[4,2,96,128]{3,2,1,0:T(8,128)(2,1)S(1)}, u32[]{:S(2)}, u32[]{:S(2)}) collective-permute-start(bf16[4,2,96,128]{3,2,1,0:T(8,128)(2,1)S(1)} %pad_maximum_fusion.refs_0_), channel_id=1, source_target_pairs={{0,4},{2,6},{4,0},{6,2},{8,12},{10,14},{12,8},{14,10},{16,20},{18,... | collective-permute-start | bytes 589832 | tf_op jit(solution)/shard_map/ppermute | solution.py:392
  47.3 5.0 %collective-permute-start.13 = (bf16[4,2,96,128]{3,2,1,0:T(8,128)(2,1)S(1)}, bf16[4,2,96,128]{3,2,1,0:T(8,128)(2,1)S(1)}, u32[]{:S(2)}, u32[]{:S(2)}) collective-permute-start(bf16[4,2,96,128]{3,2,1,0:T(8,128)(2,1)S(1)} %pad_maximum_fusion.refs_0_), channel_id=1, source_target_pairs={{0,2},{2,0},{4,6},{6,4},{8,10},{10,8},{12,14},{14,12},{16,18},{18,... | collective-permute-start | bytes 589832 | tf_op jit(solution)/shard_map/ppermute | solution.py:392
  52.3 1.4 %collective-permute-start.14 = (bf16[4,2,96,128]{3,2,1,0:T(8,128)(2,1)S(1)}, bf16[4,2,96,128]{3,2,1,0:T(8,128)(2,1)S(1)}, u32[]{:S(2)}, u32[]{:S(2)}) collective-permute-start(bf16[4,2,96,128]{3,2,1,0:T(8,128)(2,1)S(1)} %collective-permute-done.12.refs_1_), channel_id=1, source_target_pairs={{0,2},{2,0},{4,6},{6,4},{8,10},{10,8},{12,14},{14,12},{16,18},{18,... | collective-permute-start | bytes 589832 | tf_op jit(solution)/shard_map/ppermute | solution.py:392
  54.7 4.2 %collective-permute-start.15 = (bf16[48,512]{1,0:T(8,128)(2,1)S(1)}, bf16[48,512]{1,0:T(8,128)(2,1)S(1)}, u32[]{:S(2)}, u32[]{:S(2)}) collective-permute-start(bf16[48,512]{1,0:T(8,128)(2,1)S(1)} %get-tuple-element.48.rest_0_), channel_id=1, source_target_pairs={{0,1},{1,0},{2,3},{3,2},{4,5},{5,4},{6,7},{7,6},{8,9},{9,8},{10,11... | collective-permute-start | bytes 147464 | tf_op jit(solution)/shard_map/ppermute | solution.py:460

commit v4 on v3

--- a/solution.py
+++ b/solution.py
@@ -87,12 +87,32 @@
         local_rows,
         core,
     )
-    for head in range(heads):
-        lanes = slice(head * HD, (head + 1) * HD)
+    def lanes_of(head, side):
+        if side == 0:
+            return slice(head * HD, (head + 1) * HD)
+        return pl.ds(pl.multiple_of((core * heads + head) * HD, HD), HD)
+
+    def score_of(chunk):
+        head, start, side = chunk
+        queries = q_ref[start : start + step, head].reshape(step * unit, HD)
+        return lax.dot_general(
+            queries, caches[2 * side][:, lanes_of(head, side)], (((1,), (1,)), ((), ())), preferred_element_type=f32
+        )
+
+    chunks = [
+        (head, start, side)
+        for head in range(heads)
+        for start in range(0, units, step)
+        for side in range(split)
+    ]
+    tops, sums = [], []
+    following = score_of(chunks[0])
+    for at, (head, start, side) in enumerate(chunks):
+        raw = following
+        if at + 1 < len(chunks):
+            following = score_of(chunks[at + 1])
         draft_values = jnp.concatenate([d_ref[head, LANES:], ones[:LANES]], axis=1)
-        for start in range(0, units, step):
-            rows = step * unit
-            queries = q_ref[start : start + step, head].reshape(rows, HD)
+        if side == 0:
             time = jnp.concatenate(
                 [
                     unit_row + unit_rows * jnp.bitwise_xor(chip, rel[start + n])
@@ -101,44 +121,42 @@
                 axis=0,
             )
             draft_scores = lax.dot_general(
-                queries, d_ref[head, :LANES], (((1,), (1,)), ((), ())), preferred_element_type=f32
+                q_ref[start : start + step, head].reshape(step * unit, HD),
+                d_ref[head, :LANES],
+                (((1,), (1,)), ((), ())),
+                preferred_element_type=f32,
             )
             draft_scores = jnp.where(draft_row <= time, draft_scores * LOG2_SCALE, DEAD)
-            tops, sums = [], []
-            for side in range(split):
-                k_ref, v_ref = caches[2 * side : 2 * side + 2]
-                block = seq if side == 0 else seq + 1 - 2 * core
-                score = lax.dot_general(
-                    queries, k_ref[:, lanes], (((1,), (1,)), ((), ())), preferred_element_type=f32
-                )
-                score = jnp.where(key_index + block * keys < length, score * LOG2_SCALE, DEAD)
-                inside = (draft >= side * local_rows) & (draft < (side + 1) * local_rows)
-                own_drafts = jnp.where(inside, draft_scores, DEAD)
-                top = jnp.maximum(
-                    jnp.max(score, axis=1, keepdims=True), jnp.max(own_drafts, axis=1, keepdims=True)
-                )
-                top = jnp.maximum(top, FLOOR)
-                tops.append(top)
-                values_ones = jnp.concatenate([v_ref[:, lanes], ones], axis=1)
-                sums.append(
-                    jnp.dot(
-                        jnp.exp2(score - top).astype(bf16), values_ones, preferred_element_type=f32
-                    )
-                    + jnp.dot(
-                        jnp.exp2(own_drafts - top).astype(bf16),
-                        draft_values,
-                        preferred_element_type=f32,
-                    )
-                )
-            shift = functools.reduce(jnp.maximum, tops).astype(bf16).astype(f32)
-            both = sum(part * jnp.exp2(top - shift) for part, top in zip(sums, tops))
-            weighted, total = both[:, :HD], both[:, HD : HD + 1]
-            for n in range(step):
-                place = (start + n) * heads + head
-                part = slice(n * unit, (n + 1) * unit)
-                out_ref[place * unit : (place + 1) * unit, :] = weighted[part].astype(out_ref.dtype)
-                columns.append((place, shift[part]))
-                columns.append((count8 + place, total[part]))
+        block = seq if side == 0 else seq + 1 - 2 * core
+        score = jnp.where(key_index + block * keys < length, raw * LOG2_SCALE, DEAD)
+        inside = (draft >= side * local_rows) & (draft < (side + 1) * local_rows)
+        own_drafts = jnp.where(inside, draft_scores, DEAD)
+        top = jnp.maximum(
+            jnp.max(score, axis=1, keepdims=True), jnp.max(own_drafts, axis=1, keepdims=True)
+        )
+        top = jnp.maximum(top, FLOOR)
+        tops.append(top)
+        values_ones = jnp.concatenate(
+            [caches[2 * side + 1][:, lanes_of(head, side)], ones], axis=1
+        )
+        sums.append(
+            jnp.dot(jnp.exp2(score - top).astype(bf16), values_ones, preferred_element_type=f32)
+            + jnp.dot(
+                jnp.exp2(own_drafts - top).astype(bf16), draft_values, preferred_element_type=f32
+            )
+        )
+        if side + 1 < split:
+            continue
+        shift = functools.reduce(jnp.maximum, tops).astype(bf16).astype(f32)
+        both = sum(part * jnp.exp2(top - shift) for part, top in zip(sums, tops))
+        weighted, total = both[:, :HD], both[:, HD : HD + 1]
+        for n in range(step):
+            place = (start + n) * heads + head
+            part = slice(n * unit, (n + 1) * unit)
+            out_ref[place * unit : (place + 1) * unit, :] = weighted[part].astype(out_ref.dtype)
+            columns.append((place, shift[part]))
+            columns.append((count8 + place, total[part]))
+        tops, sums = [], []
     stats = columns_to_rows(columns, unit)
     if as_message:
         write_message(out_ref, count * unit, stats[:count8], stats[count8 : 2 * count8])
@@ -159,20 +177,13 @@
             jax.ShapeDtypeStruct((2 * round_up(count, 8), LANES), f32),
         )
     whole = pl.BlockSpec(memory_space=pltpu.VMEM)
-    cache_spec = pl.BlockSpec((keys, heads * HD), lambda i: (0, 0))
-    other_spec = pl.BlockSpec(
-        (keys, heads * HD), lambda i: (0, lax.rem(lax.axis_index("seq"), split))
-    )
-    in_specs = [whole, pl.BlockSpec(q.shape, lambda i: (0, 0, 0, 0))]
-    in_specs += [cache_spec] * 2 + [other_spec] * (len(caches) - 2)
-    in_specs += [pl.BlockSpec(drafts.shape, lambda i: (0, 0, 0))]
+    in_specs = [whole] * (3 + len(caches))
     in_specs += [pl.BlockSpec(memory_space=pl.ANY)] * len(after)
     scores = count * unit * (split * keys + LANES)
     return pl.pallas_call(
         functools.partial(attend_kernel, rel, unit_rows, split, as_message, len(after)),
-        grid=(1,),
         in_specs=in_specs,
-        out_specs=tuple(pl.BlockSpec(o.shape, lambda i: (0, 0)) for o in out_shape),
+        out_specs=(whole,) * len(out_shape),
         out_shape=out_shape,
         compiler_params=pltpu.CompilerParams(vmem_limit_bytes=VMEM_BYTES),
         cost_estimate=pl.CostEstimate(
@@ -254,63 +265,74 @@
     )(num, stats, message)
 
 
-def project_kernel(rel, split, n_head, *refs):
-    sources = refs[: 2 * split]
-    w_ref = refs[2 * split]
-    outs = refs[2 * split + 1 : -2]
-    rows_ref, lhs_ref = refs[-2:]
+def project_kernel(rel, split, n_head, parts, n_partial, *refs):
+    sources, w_ref = refs[: len(parts)], refs[len(parts)]
+    partial = refs[len(parts) + 1 : len(parts) + 1 + n_partial]
+    outs, (rows_ref, lhs_ref) = refs[len(parts) + 1 + n_partial : -2], refs[-2:]
     seq, head = lax.axis_index("seq"), lax.axis_index("head")
     chip = lax.div(seq, split)
     core = lax.rem(seq, split)
-    heads_kv = rows_ref.shape[0]
     units, heads, unit, _ = sources[0].shape
     chips = 2 * units
     piece = unit // split
     first = head * (chips // n_head) if n_head == 2 else 0
-    for side in range(split):
+    slots = rows_ref.shape[0] // heads
+    if len(parts) < 2 * slots:
+        rows_ref[...] = jnp.zeros_like(rows_ref)
+    for (side, part), x_ref in zip(parts, sources):
         owner = core if side == 0 else 1 - core
-        for part in range(2):
-            x_ref = sources[2 * side + part]
-            for n in range(units):
-                place = lax.rem(jnp.bitwise_xor(chip, rel[part][n]) - first + chips, chips)
-                for part_of in range(split):
-                    row = place * unit + (owner if part_of == 0 else 1 - owner) * piece
-                    for h in range(heads):
-                        rows_ref[owner * heads + h, pl.ds(pl.multiple_of(row, 16), piece), :] = (
-                            x_ref[n, h, part_of * piece : (part_of + 1) * piece].astype(f32)
-                        )
-    rows = lhs_ref.shape[0]
-    for kv in range(heads_kv):
+        slot = owner if slots == split else 0
+        for n in range(units):
+            place = lax.rem(jnp.bitwise_xor(chip, rel[part][n]) - first + chips, chips)
+            for part_of in range(split):
+                row = place * unit + (owner if part_of == 0 else 1 - owner) * piece
+                for h in range(heads):
+                    rows_ref[slot * heads + h, pl.ds(pl.multiple_of(row, 16), piece), :] = x_ref[
+                        n, h, part_of * piece : (part_of + 1) * piece
+                    ].astype(f32)
+    rows, depth = lhs_ref.shape
+    for kv in range(rows_ref.shape[0]):
         for g in range(GROUP):
             lanes = slice((kv * GROUP + g) * HD, (kv * GROUP + g + 1) * HD)
             lhs_ref[:, lanes] = rows_ref[kv, pl.ds(g, rows, stride=GROUP), :].astype(bf16)
-    result = jnp.dot(lhs_ref[...], w_ref[...], preferred_element_type=f32)
-    if n_head == 2:
+    if slots == split:
+        weight = w_ref[...]
+    else:
+        weight = w_ref[pl.ds(pl.multiple_of((1 - core) * depth, LANES), depth), :]
+    result = jnp.dot(lhs_ref[...], weight, preferred_element_type=f32)
+    for ref in partial:
+        result = result + ref[...]
+    if len(outs) == 2:
         outs[0][...] = result[: rows // 2]
         outs[1][...] = result[rows // 2 :].astype(bf16)
     else:
         outs[0][...] = result
 
 
-def project(rel, split, n_head, sources, weight):
+def project(rel, split, n_head, parts, sources, weight, partial=(), whole=False):
     units, heads, unit, _ = sources[0].shape
-    heads_kv = heads * split
+    slots = 1 if partial else split
     rows = 2 * units * unit // GROUP
     columns = weight.shape[1]
-    if n_head == 2:
+    if n_head == 2 and whole:
         out_shape = tuple(jax.ShapeDtypeStruct((rows // 2, columns), t) for t in (f32, bf16))
     else:
         out_shape = (jax.ShapeDtypeStruct((rows, columns), f32),)
     return pl.pallas_call(
-        functools.partial(project_kernel, rel, split, n_head),
-        in_specs=[pl.BlockSpec(memory_space=pltpu.VMEM)] * (2 * split + 1),
+        functools.partial(project_kernel, rel, split, n_head, parts, len(partial)),
+        in_specs=[pl.BlockSpec(memory_space=pltpu.VMEM)] * (len(sources) + 1 + len(partial)),
         out_shape=out_shape,
         scratch_shapes=[
-            pltpu.VMEM((heads_kv, 2 * units * unit, LANES), f32),
-            pltpu.VMEM((rows, heads_kv * GROUP * HD), bf16),
+            pltpu.VMEM((heads * slots, 2 * units * unit, LANES), f32),
+            pltpu.VMEM((rows, heads * slots * GROUP * HD), bf16),
         ],
         compiler_params=pltpu.CompilerParams(vmem_limit_bytes=VMEM_BYTES),
-    )(*sources, weight)
+        cost_estimate=pl.CostEstimate(
+            flops=2 * rows * columns * heads * slots * GROUP * HD,
+            bytes_accessed=2 * columns * heads * slots * GROUP * HD,
+            transcendentals=0,
+        ),
+    )(*sources, weight, *partial)
 
 
 def append_kernel(rel, split, unit_rows, scal, ck_ref, cv_ref, mine_ref, other_ref, *rest):
@@ -451,10 +473,23 @@
         att = jnp.concatenate([att, swap(att, bit)], axis=0)
     att, every = lax.optimization_barrier((att, every))
     att_near = swap(att, near)
-    sources = [att, att_near]
+    halves = (rel_far, rel)
     if split == 2:
-        sources += [swap(att, 0), swap(att_near, 0)]
-    result = project((rel_far, rel), split, n_head, sources, weight)
+        begun = project(
+            halves,
+            split,
+            n_head,
+            ((0, 0), (0, 1), (1, 0)),
+            [att, att_near, swap(att, 0)],
+            weight,
+        )
+        result = project(
+            halves, split, n_head, ((1, 1),), [swap(att_near, 0)], weight, begun, True
+        )
+    else:
+        result = project(
+            halves, split, n_head, ((0, 0), (0, 1)), [att, att_near], weight, (), True
+        )
     if n_head == 2:
         keep, send = result
         projected = keep + lax.ppermute(send, "head", [(0, 1), (1, 0)]).astype(f32)

time: 59.8 us -> 59.1 us (0.988)
  waiting for transfers between devices: 26.2 us -> 24.9 us
    ppermute x15, waiting for transfers between devices: 25.9 us -> 24.7 us  [swap(): return lax.ppermute(x, 'seq', [(i, i ^ 1 << bit) for i in range(n_seq)])]
    pallas_call x1 -> x2, Pallas kernels: 0.94 us -> 1.58 us  [project(): pl.pallas_call(functools.partial(project_kernel, rel, split, n_head, part...]
    pallas_call x2, Pallas kernels: 6.58 us -> 5.95 us  [attend(): pl.pallas_call(functools.partial(attend_kernel, rel, unit_rows, split, as...]
  transfers between devices with their start and end apart: 16 -> 16, of which waited for: 10 -> 10; matrix products, arithmetic and copies ran while one was open for 3% -> 3% of each run, Pallas kernels for 15% -> 16%
where the time goes in v4:
time: 59.1 us; the launch traced here: 58.8 us
  waiting for transfers between devices  24.9 us (42%)
  starting transfers between devices  16.9 us (29%)
  Pallas kernels  10.9 us (18%)
  local copies, waits for them, and re-layouts  2.55 us (4%)
  between operations  2.13 us (4%)
  other arithmetic  1.5 us (3%)
    ppermute x15, waiting for transfers between devices, swap(): return lax.ppermute(x, 'seq', [(i, i ^ 1 << bit) for i in range(n_seq)])  24.7 us
    ppermute x15, starting transfers between devices, swap(): return lax.ppermute(x, 'seq', [(i, i ^ 1 << bit) for i in range(n_seq)])  15.3 us
    pallas_call x2, Pallas kernels, attend(): pl.pallas_call(functools.partial(attend_kernel, rel, unit_rows, split, as...  5.95 us
    pallas_call x1, Pallas kernels, append(): pl.pallas_call(functools.partial(append_kernel, rel, split, unit_rows), g...  2.31 us
    ppermute x1, starting transfers between devices, one_request(): projected = keep + lax.ppermute(send, 'head', [(0, 1), (1, 0)]).astype(f32)  1.59 us
    pallas_call x2, Pallas kernels, project(): pl.pallas_call(functools.partial(project_kernel, rel, split, n_head, part...  1.58 us
    dynamic_slice x1, local copies, waits for them, and re-layouts, one_request(): lax.dynamic_slice_in_dim(c, core * heads * HD, heads * HD, 1)  1.27 us
  transfers between devices with their start and end apart: 16, of which 10 were waited for; matrix products, arithmetic and copies ran while one was open for 3% of the time, Pallas kernels for 16%

profile of v4, /device:TPU:0, one launch (start us, length us, event | category | flops | bytes accessed | tf_op | source)
XLA Modules:
  0.0 58.8 jit_solution(7508510815509423559)
XLA Ops:
  0.6 0.8 %copy_bitcast_fusion.1 = bf16[4,48,128]{2,1,0:T(8,128)(2,1)S(1)} fusion(bf16[1,6,32,128]{3,1,2,0:T(8,128)(2,1)} %bitcast.40), kind=kLoop, calls=%fused_computation.15 | loop fusion | bytes 98304 | tf_op jit(solution)/shard_map/reshape | solution.py:419
  1.5 0.7 %pad_maximum_fusion.4 = bf16[4,60,128]{2,1,0:T(8,128)(2,1)S(1)} fusion(bf16[4,6,128]{2,1,0:T(8,128)(2,1)} %bitcast.41, bf16[4,6,128]{2,1,0:T(8,128)(2,1)} %bitcast.42, bf16[4,48,128]{2,1,0:T(8,128)(2,1)S(1)} %copy_bitcast_fusion.1), kind=kLoop, calls=%fused_computation.12 | loop fusion | flops 184320 | bytes 122880 | tf_op jit(solution)/shard_map/concatenate | solution.py:422
  5.0 3.7 %collective-permute-start.1 = (bf16[1,2,120,128]{3,2,1,0:T(8,128)(2,1)S(1)}, bf16[1,2,120,128]{3,2,1,0:T(8,128)(2,1)S(1)}, u32[]{:S(2)}, u32[]{:S(2)}) collective-permute-start(bf16[1,2,120,128]{3,2,1,0:T(8,128)(2,1)S(1)} %bitcast.38), channel_id=1, source_target_pairs={{0,16},{2,18},{4,20},{6,22},{8,24},{10,26},{12,28},{14,30},{16,0},... | collective-permute-start | bytes 184328 | tf_op jit(solution)/shard_map/ppermute | solution.py:414
  8.7 3.9 %collective-permute-done.1 = bf16[1,2,120,128]{3,2,1,0:T(8,128)(2,1)S(1)} collective-permute-done((bf16[1,2,120,128]{3,2,1,0:T(8,128)(2,1)S(1)}, bf16[1,2,120,128]{3,2,1,0:T(8,128)(2,1)S(1)}, u32[]{:S(2)}, u32[]{:S(2)}) %collective-permute-start.1) | collective-permute-done | bytes 61472 | tf_op jit(solution)/shard_map/ppermute | solution.py:414
  12.6 0.8 %collective-permute-start.2 = (bf16[2,2,120,128]{3,2,1,0:T(8,128)(2,1)S(1)}, bf16[2,2,120,128]{3,2,1,0:T(8,128)(2,1)S(1)}, u32[]{:S(2)}, u32[]{:S(2)}) collective-permute-start(bf16[2,2,120,128]{3,2,1,0:T(8,128)(2,1)S(1)} %pad_maximum_fusion.2), channel_id=1, source_target_pairs={{0,8},{2,10},{4,12},{6,14},{8,0},{10,2},{12,4},{14,6},{16,24},{18,... | collective-permute-start | bytes 368648 | tf_op jit(solution)/shard_map/ppermute | solution.py:414
  13.4 1.3 %constant_dynamic-slice_fusion.2 = (bf16[1024,256]{1,0:T(8,128)(2,1)S(1)}, bf16[1024,256]{1,0:T(8,128)(2,1)S(1)}) fusion(bf16[1024,512]{1,0:T(8,128)(2,1)} %bitcast.31, s32[]{:T(128)S(6)} %select_n.20, bf16[1024,512]{1,0:T(8,128)(2,1)} %bitcast.34), kind=kLoop, calls=%fused_computation.20 | loop fusion | bytes 2097156 | tf_op jit(solution)/shard_map/dynamic_slice | solution.py:450
  14.7 2.8 %collective-permute-done.2 = bf16[2,2,120,128]{3,2,1,0:T(8,128)(2,1)S(1)} collective-permute-done((bf16[2,2,120,128]{3,2,1,0:T(8,128)(2,1)S(1)}, bf16[2,2,120,128]{3,2,1,0:T(8,128)(2,1)S(1)}, u32[]{:S(2)}, u32[]{:S(2)}) %collective-permute-start.2) | collective-permute-done | bytes 122912 | tf_op jit(solution)/shard_map/ppermute | solution.py:414
  17.6 1.6 %collective-permute-start.3 = (bf16[4,2,96,128]{3,2,1,0:T(8,128)(2,1)S(1)}, bf16[4,2,96,128]{3,2,1,0:T(8,128)(2,1)S(1)}, u32[]{:S(2)}, u32[]{:S(2)}) collective-permute-start(bf16[4,2,96,128]{3,2,1,0:T(8,128)(2,1)S(1)} %slice.39.q_ref), channel_id=1, source_target_pairs={{0,4},{2,6},{4,0},{6,2},{8,12},{10,14},{12,8},{14,10},{16,20},{18,... | collective-permute-start | bytes 589832 | tf_op jit(solution)/shard_map/ppermute | solution.py:414
  19.3 3.0 %shard_map.103.rest_5_ = bf16[800,128]{1,0:T(8,128)(2,1)S(1)} custom-call(s32[2,128]{1,0:T(2,128)S(1)} %broadcast_in_dim.12.scal, bf16[4,2,96,128]{3,2,1,0:T(8,128)(2,1)S(1)} %slice.39.q_ref, bf16[1024,256]{1,0:T(8,128)(2,1)S(1)} %get-tuple-element.60.rest_0_, bf16[1024,256]{1,0:T(8,128)(2,1)S(1)} %get-tuple-element.59.rest_1_, ...), custom_call_target="tpu_custom_call" | custom-call | flops 855638016 | bytes 2097152 | tf_op jit(solution)/shard_map/pallas_call | solution.py:183
  22.7 1.6 %collective-permute-done.3.q_ref = bf16[4,2,96,128]{3,2,1,0:T(8,128)(2,1)S(1)} collective-permute-done((bf16[4,2,96,128]{3,2,1,0:T(8,128)(2,1)S(1)}, bf16[4,2,96,128]{3,2,1,0:T(8,128)(2,1)S(1)}, u32[]{:S(2)}, u32[]{:S(2)}) %collective-permute-start.3) | collective-permute-done | bytes 196640 | tf_op jit(solution)/shard_map/ppermute | solution.py:414
  24.4 3.0 %shard_map.104 = (f32[768,128]{1,0:T(8,128)S(1)}, f32[16,128]{1,0:T(8,128)S(1)}) custom-call(s32[2,128]{1,0:T(2,128)S(1)} %broadcast_in_dim.12.scal, bf16[4,2,96,128]{3,2,1,0:T(8,128)(2,1)S(1)} %collective-permute-done.3.q_ref, bf16[1024,256]{1,0:T(8,128)(2,1)S(1)} %get-tuple-element.60.rest_0_, bf16[1024,256]{1,0:T(8,128)(2,1)S(1)} %get-tuple-element.59.rest_1_, ...), custom_call_target="tpu_custom_call" | custom-call | flops 855638016 | bytes 2097152 | tf_op jit(solution)/shard_map/pallas_call | solution.py:183
  27.3 0.7 %collective-permute-done.6.msg_ref = bf16[800,128]{1,0:T(8,128)(2,1)S(1)} collective-permute-done((bf16[800,128]{1,0:T(8,128)(2,1)S(1)}, bf16[800,128]{1,0:T(8,128)(2,1)S(1)}, u32[]{:S(2)}, u32[]{:S(2)}) %collective-permute-start.6) | collective-permute-done | bytes 204832 | tf_op jit(solution)/shard_map/ppermute | solution.py:414
  28.4 1.3 %collective-permute-start.7 = (bf16[416,128]{1,0:T(8,128)(2,1)S(1)}, bf16[416,128]{1,0:T(8,128)(2,1)S(1)}, u32[]{:S(2)}, u32[]{:S(2)}) collective-permute-start(bf16[416,128]{1,0:T(8,128)(2,1)S(1)} %get-tuple-element.40), channel_id=1, source_target_pairs={{0,8},{2,10},{4,12},{6,14},{8,0},{10,2},{12,4},{14,6},{16,24},{18,... | collective-permute-start | bytes 319496 | tf_op jit(solution)/shard_map/ppermute | solution.py:414
  29.8 1.4 %collective-permute-start.9 = (bf16[4,2,24,128]{3,2,1,0:T(8,128)(2,1)S(1)}, bf16[4,2,24,128]{3,2,1,0:T(8,128)(2,1)S(1)}, u32[]{:S(2)}, u32[]{:S(2)}) collective-permute-start(bf16[4,2,24,128]{3,2,1,0:T(8,128)(2,1)S(1)} %slice.40), channel_id=1, source_target_pairs={{0,4},{2,6},{4,0},{6,2},{8,12},{10,14},{12,8},{14,10},{16,20},{18,... | collective-permute-start | bytes 147464 | tf_op jit(solution)/shard_map/ppermute | solution.py:414
  31.2 2.0 %collective-permute-done.7.msg_ref = bf16[416,128]{1,0:T(8,128)(2,1)S(1)} collective-permute-done((bf16[416,128]{1,0:T(8,128)(2,1)S(1)}, bf16[416,128]{1,0:T(8,128)(2,1)S(1)}, u32[]{:S(2)}, u32[]{:S(2)}) %collective-permute-start.7) | collective-permute-done | bytes 106528 | tf_op jit(solution)/shard_map/ppermute | solution.py:414
  33.5 3.8 %collective-permute-start.8 = (bf16[416,128]{1,0:T(8,128)(2,1)S(1)}, bf16[416,128]{1,0:T(8,128)(2,1)S(1)}, u32[]{:S(2)}, u32[]{:S(2)}) collective-permute-start(bf16[416,128]{1,0:T(8,128)(2,1)S(1)} %get-tuple-element.43), channel_id=1, source_target_pairs={{0,16},{2,18},{4,20},{6,22},{8,24},{10,26},{12,28},{14,30},{16,0},... | collective-permute-start | bytes 319496 | tf_op jit(solution)/shard_map/ppermute | solution.py:414
  37.3 3.9 %collective-permute-done.8.msg_ref = bf16[416,128]{1,0:T(8,128)(2,1)S(1)} collective-permute-done((bf16[416,128]{1,0:T(8,128)(2,1)S(1)}, bf16[416,128]{1,0:T(8,128)(2,1)S(1)}, u32[]{:S(2)}, u32[]{:S(2)}) %collective-permute-start.8) | collective-permute-done | bytes 106528 | tf_op jit(solution)/shard_map/ppermute | solution.py:414
  41.7 4.5 %collective-permute-done.10 = bf16[2,2,96,128]{3,2,1,0:T(8,128)(2,1)S(1)} collective-permute-done((bf16[2,2,96,128]{3,2,1,0:T(8,128)(2,1)S(1)}, bf16[2,2,96,128]{3,2,1,0:T(8,128)(2,1)S(1)}, u32[]{:S(2)}, u32[]{:S(2)}) %collective-permute-start.10) | collective-permute-done | bytes 98336 | tf_op jit(solution)/shard_map/ppermute | solution.py:414
  46.3 0.9 %collective-permute-start.12 = (bf16[4,2,96,128]{3,2,1,0:T(8,128)(2,1)S(1)}, bf16[4,2,96,128]{3,2,1,0:T(8,128)(2,1)S(1)}, u32[]{:S(2)}, u32[]{:S(2)}) collective-permute-start(bf16[4,2,96,128]{3,2,1,0:T(8,128)(2,1)S(1)} %pad_maximum_fusion.refs_0_), channel_id=1, source_target_pairs={{0,4},{2,6},{4,0},{6,2},{8,12},{10,14},{12,8},{14,10},{16,20},{18,... | collective-permute-start | bytes 589832 | tf_op jit(solution)/shard_map/ppermute | solution.py:414
  47.2 4.8 %collective-permute-done.12.refs_1_ = bf16[4,2,96,128]{3,2,1,0:T(8,128)(2,1)S(1)} collective-permute-done((bf16[4,2,96,128]{3,2,1,0:T(8,128)(2,1)S(1)}, bf16[4,2,96,128]{3,2,1,0:T(8,128)(2,1)S(1)}, u32[]{:S(2)}, u32[]{:S(2)}) %collective-permute-start.12) | collective-permute-done | bytes 196640 | tf_op jit(solution)/shard_map/ppermute | solution.py:414
  52.0 1.0 %shard_map.108.refs_2_ = f32[96,512]{1,0:T(8,128)S(1)} custom-call(bf16[4,2,96,128]{3,2,1,0:T(8,128)(2,1)S(1)} %pad_maximum_fusion.refs_0_, bf16[4,2,96,128]{3,2,1,0:T(8,128)(2,1)S(1)} %collective-permute-done.12.refs_1_, bf16[4,2,96,128]{3,2,1,0:T(8,128)(2,1)S(1)} %collective-permute-done.14.refs_2_, bf16[4096,512]{1,0:T(8,128)(2,1)S(1)} %copy-done), custom_call_target="tpu_custom_call" | custom-call | flops 402653184 | bytes 4194304 | tf_op jit(solution)/shard_map/pallas_call | solution.py:321
  54.0 1.6 %collective-permute-start.15 = (bf16[48,512]{1,0:T(8,128)(2,1)S(1)}, bf16[48,512]{1,0:T(8,128)(2,1)S(1)}, u32[]{:S(2)}, u32[]{:S(2)}) collective-permute-start(bf16[48,512]{1,0:T(8,128)(2,1)S(1)} %get-tuple-element.48.rest_0_), channel_id=1, source_target_pairs={{0,1},{1,0},{2,3},{3,2},{4,5},{5,4},{6,7},{7,6},{8,9},{9,8},{10,11... | collective-permute-start | bytes 147464 | tf_op jit(solution)/shard_map/ppermute | solution.py:495
  55.6 2.3 %shard_map.110 = (bf16[1024,512]{1,0:T(8,128)(2,1)}, bf16[1024,512]{1,0:T(8,128)(2,1)}) custom-call(s32[2,128]{1,0:T(2,128)S(1)} %broadcast_in_dim.12.scal, bf16[1024,512]{1,0:T(8,128)(2,1)S(1)} %bitcast.35, bf16[1024,512]{1,0:T(8,128)(2,1)S(1)} %bitcast.32, bf16[8,2,24,128]{3,2,1,0:T(8,128)(2,1)S(1)} %pad_maximum_fusion.3.mine_ref, ...), custom_call_target="tpu_custom_call" | custom-call | bytes 4194304 | tf_op jit(solution)/shard_map/pallas_call | solution.py:389
  58.2 0.6 %fusion.6 = bf16[1,48,512]{2,1,0:T(8,128)(2,1)} fusion(f32[48,512]{1,0:T(8,128)S(1)} %get-tuple-element.47, bf16[48,512]{1,0:T(8,128)(2,1)S(1)} %collective-permute-done.15), kind=kLoop, calls=%fused_computation.13 | loop fusion | flops 73728 | bytes 196608 | tf_op jit(solution)/shard_map/stack | solution.py:511
  (43 shorter events, 4.5 us)
Async XLA Ops:
  2.2 1.9 %collective-permute-start = (bf16[2,60,128]{2,1,0:T(8,128)(2,1)S(1)}, bf16[2,60,128]{2,1,0:T(8,128)(2,1)S(1)}, u32[]{:S(2)}, u32[]{:S(2)}) collective-permute-start(bf16[2,60,128]{2,1,0:T(8,128)(2,1)S(1)} %constant_dynamic-slice_fusion.4), channel_id=1, source_target_pairs={{0,2},{2,0},{4,6},{6,4},{8,10},{10,8},{12,14},{14,12},{16,18},{18,... | collective-permute-start | bytes 92168 | tf_op jit(solution)/shard_map/ppermute | solution.py:414
  4.5 14.7 %collective-permute-start.4 = (bf16[1024,512]{1,0:T(8,128)(2,1)}, bf16[1024,512]{1,0:T(8,128)(2,1)S(1)}, u32[]{:S(2)}, u32[]{:S(2)}) collective-permute-start(bf16[1024,512]{1,0:T(8,128)(2,1)} %bitcast.33), channel_id=1, source_target_pairs={{0,2},{2,0},{4,6},{6,4},{8,10},{10,8},{12,14},{14,12},{16,18},{18,... | collective-permute-start | bytes 3145736 | tf_op jit(solution)/shard_map/ppermute | solution.py:414
  4.6 14.7 %collective-permute-start.5 = (bf16[1024,512]{1,0:T(8,128)(2,1)}, bf16[1024,512]{1,0:T(8,128)(2,1)S(1)}, u32[]{:S(2)}, u32[]{:S(2)}) collective-permute-start(bf16[1024,512]{1,0:T(8,128)(2,1)} %bitcast.30), channel_id=1, source_target_pairs={{0,2},{2,0},{4,6},{6,4},{8,10},{10,8},{12,14},{14,12},{16,18},{18,... | collective-permute-start | bytes 3145736 | tf_op jit(solution)/shard_map/ppermute | solution.py:414
  5.0 7.6 %collective-permute-start.1 = (bf16[1,2,120,128]{3,2,1,0:T(8,128)(2,1)S(1)}, bf16[1,2,120,128]{3,2,1,0:T(8,128)(2,1)S(1)}, u32[]{:S(2)}, u32[]{:S(2)}) collective-permute-start(bf16[1,2,120,128]{3,2,1,0:T(8,128)(2,1)S(1)} %bitcast.38), channel_id=1, source_target_pairs={{0,16},{2,18},{4,20},{6,22},{8,24},{10,26},{12,28},{14,30},{16,0},... | collective-permute-start | bytes 184328 | tf_op jit(solution)/shard_map/ppermute | solution.py:414
  12.6 4.9 %collective-permute-start.2 = (bf16[2,2,120,128]{3,2,1,0:T(8,128)(2,1)S(1)}, bf16[2,2,120,128]{3,2,1,0:T(8,128)(2,1)S(1)}, u32[]{:S(2)}, u32[]{:S(2)}) collective-permute-start(bf16[2,2,120,128]{3,2,1,0:T(8,128)(2,1)S(1)} %pad_maximum_fusion.2), channel_id=1, source_target_pairs={{0,8},{2,10},{4,12},{6,14},{8,0},{10,2},{12,4},{14,6},{16,24},{18,... | collective-permute-start | bytes 368648 | tf_op jit(solution)/shard_map/ppermute | solution.py:414
  17.6 6.7 %collective-permute-start.3 = (bf16[4,2,96,128]{3,2,1,0:T(8,128)(2,1)S(1)}, bf16[4,2,96,128]{3,2,1,0:T(8,128)(2,1)S(1)}, u32[]{:S(2)}, u32[]{:S(2)}) collective-permute-start(bf16[4,2,96,128]{3,2,1,0:T(8,128)(2,1)S(1)} %slice.39.q_ref), channel_id=1, source_target_pairs={{0,4},{2,6},{4,0},{6,2},{8,12},{10,14},{12,8},{14,10},{16,20},{18,... | collective-permute-start | bytes 589832 | tf_op jit(solution)/shard_map/ppermute | solution.py:414
  19.2 32.8 %copy-start = (bf16[4096,512]{1,0:T(8,128)(2,1)S(1)}, bf16[4096,512]{1,0:T(8,128)(2,1)}, u32[]{:S(2)}) copy-start(bf16[4096,512]{1,0:T(8,128)(2,1)} %refs_1_.1) | copy-start | bytes 12582916
  22.2 5.8 %collective-permute-start.6 = (bf16[800,128]{1,0:T(8,128)(2,1)S(1)}, bf16[800,128]{1,0:T(8,128)(2,1)S(1)}, u32[]{:S(2)}, u32[]{:S(2)}) collective-permute-start(bf16[800,128]{1,0:T(8,128)(2,1)S(1)} %shard_map.103.rest_5_), channel_id=1, source_target_pairs={{0,4},{2,6},{4,0},{6,2},{8,12},{10,14},{12,8},{14,10},{16,20},{18,... | collective-permute-start | bytes 614408 | tf_op jit(solution)/shard_map/ppermute | solution.py:414
  28.4 4.8 %collective-permute-start.7 = (bf16[416,128]{1,0:T(8,128)(2,1)S(1)}, bf16[416,128]{1,0:T(8,128)(2,1)S(1)}, u32[]{:S(2)}, u32[]{:S(2)}) collective-permute-start(bf16[416,128]{1,0:T(8,128)(2,1)S(1)} %get-tuple-element.40), channel_id=1, source_target_pairs={{0,8},{2,10},{4,12},{6,14},{8,0},{10,2},{12,4},{14,6},{16,24},{18,... | collective-permute-start | bytes 319496 | tf_op jit(solution)/shard_map/ppermute | solution.py:414
  29.8 7.5 %collective-permute-start.9 = (bf16[4,2,24,128]{3,2,1,0:T(8,128)(2,1)S(1)}, bf16[4,2,24,128]{3,2,1,0:T(8,128)(2,1)S(1)}, u32[]{:S(2)}, u32[]{:S(2)}) collective-permute-start(bf16[4,2,24,128]{3,2,1,0:T(8,128)(2,1)S(1)} %slice.40), channel_id=1, source_target_pairs={{0,4},{2,6},{4,0},{6,2},{8,12},{10,14},{12,8},{14,10},{16,20},{18,... | collective-permute-start | bytes 147464 | tf_op jit(solution)/shard_map/ppermute | solution.py:414
  33.5 7.7 %collective-permute-start.8 = (bf16[416,128]{1,0:T(8,128)(2,1)S(1)}, bf16[416,128]{1,0:T(8,128)(2,1)S(1)}, u32[]{:S(2)}, u32[]{:S(2)}) collective-permute-start(bf16[416,128]{1,0:T(8,128)(2,1)S(1)} %get-tuple-element.43), channel_id=1, source_target_pairs={{0,16},{2,18},{4,20},{6,22},{8,24},{10,26},{12,28},{14,30},{16,0},... | collective-permute-start | bytes 319496 | tf_op jit(solution)/shard_map/ppermute | solution.py:414
  41.6 4.7 %collective-permute-start.10 = (bf16[2,2,96,128]{3,2,1,0:T(8,128)(2,1)S(1)}, bf16[2,2,96,128]{3,2,1,0:T(8,128)(2,1)S(1)}, u32[]{:S(2)}, u32[]{:S(2)}) collective-permute-start(bf16[2,2,96,128]{3,2,1,0:T(8,128)(2,1)S(1)} %bitcast.36), channel_id=1, source_target_pairs={{0,8},{2,10},{4,12},{6,14},{8,0},{10,2},{12,4},{14,6},{16,24},{18,... | collective-permute-start | bytes 294920 | tf_op jit(solution)/shard_map/ppermute | solution.py:414
  41.6 4.7 %collective-permute-start.11 = (bf16[8,2,24,128]{3,2,1,0:T(8,128)(2,1)S(1)}, bf16[8,2,24,128]{3,2,1,0:T(8,128)(2,1)S(1)}, u32[]{:S(2)}, u32[]{:S(2)}) collective-permute-start(bf16[8,2,24,128]{3,2,1,0:T(8,128)(2,1)S(1)} %pad_maximum_fusion.3.mine_ref), channel_id=1, source_target_pairs={{0,2},{2,0},{4,6},{6,4},{8,10},{10,8},{12,14},{14,12},{16,18},{18,... | collective-permute-start | bytes 294920 | tf_op jit(solution)/shard_map/ppermute | solution.py:414
  46.3 9.4 %copy-start.1 = (bf16[1,1024,512]{2,1,0:T(8,128)(2,1)S(1)}, bf16[1,1024,512]{2,1,0:T(8,128)(2,1)}, u32[]{:S(2)}) copy-start(bf16[1,1024,512]{2,1,0:T(8,128)(2,1)} %param.12) | copy-start | bytes 3145732
  46.3 9.3 %copy-start.2 = (bf16[1,1024,512]{2,1,0:T(8,128)(2,1)S(1)}, bf16[1,1024,512]{2,1,0:T(8,128)(2,1)}, u32[]{:S(2)}) copy-start(bf16[1,1024,512]{2,1,0:T(8,128)(2,1)} %param.11) | copy-start | bytes 3145732
  46.3 5.7 %collective-permute-start.12 = (bf16[4,2,96,128]{3,2,1,0:T(8,128)(2,1)S(1)}, bf16[4,2,96,128]{3,2,1,0:T(8,128)(2,1)S(1)}, u32[]{:S(2)}, u32[]{:S(2)}) collective-permute-start(bf16[4,2,96,128]{3,2,1,0:T(8,128)(2,1)S(1)} %pad_maximum_fusion.refs_0_), channel_id=1, source_target_pairs={{0,4},{2,6},{4,0},{6,2},{8,12},{10,14},{12,8},{14,10},{16,20},{18,... | collective-permute-start | bytes 589832 | tf_op jit(solution)/shard_map/ppermute | solution.py:414
  47.2 4.8 %collective-permute-start.14 = (bf16[4,2,96,128]{3,2,1,0:T(8,128)(2,1)S(1)}, bf16[4,2,96,128]{3,2,1,0:T(8,128)(2,1)S(1)}, u32[]{:S(2)}, u32[]{:S(2)}) collective-permute-start(bf16[4,2,96,128]{3,2,1,0:T(8,128)(2,1)S(1)} %pad_maximum_fusion.refs_0_), channel_id=1, source_target_pairs={{0,2},{2,0},{4,6},{6,4},{8,10},{10,8},{12,14},{14,12},{16,18},{18,... | collective-permute-start | bytes 589832 | tf_op jit(solution)/shard_map/ppermute | solution.py:414
  52.0 1.4 %collective-permute-start.13 = (bf16[4,2,96,128]{3,2,1,0:T(8,128)(2,1)S(1)}, bf16[4,2,96,128]{3,2,1,0:T(8,128)(2,1)S(1)}, u32[]{:S(2)}, u32[]{:S(2)}) collective-permute-start(bf16[4,2,96,128]{3,2,1,0:T(8,128)(2,1)S(1)} %collective-permute-done.12.refs_1_), channel_id=1, source_target_pairs={{0,2},{2,0},{4,6},{6,4},{8,10},{10,8},{12,14},{14,12},{16,18},{18,... | collective-permute-start | bytes 589832 | tf_op jit(solution)/shard_map/ppermute | solution.py:414
  54.0 4.2 %collective-permute-start.15 = (bf16[48,512]{1,0:T(8,128)(2,1)S(1)}, bf16[48,512]{1,0:T(8,128)(2,1)S(1)}, u32[]{:S(2)}, u32[]{:S(2)}) collective-permute-start(bf16[48,512]{1,0:T(8,128)(2,1)S(1)} %get-tuple-element.48.rest_0_), channel_id=1, source_target_pairs={{0,1},{1,0},{2,3},{3,2},{4,5},{5,4},{6,7},{7,6},{8,9},{9,8},{10,11... | collective-permute-start | bytes 147464 | tf_op jit(solution)/shard_map/ppermute | solution.py:495

commit v5 on v4

--- a/solution.py
+++ b/solution.py
@@ -335,6 +335,45 @@
     )(*sources, weight, *partial)
 
 
+def drafts_kernel(split, own_ref, *rest):
+    others, (draft_ref, unit_ref, rows_ref) = rest[:-3], rest[-3:]
+    rows, width = own_ref.shape
+    heads = draft_ref.shape[0]
+    core = lax.rem(lax.axis_index("seq"), split)
+    rows_ref[...] = jnp.zeros_like(rows_ref)
+    for n, ref in enumerate((own_ref, *others)):
+        rows_ref[n * rows : (n + 1) * rows, :] = ref[...].astype(f32)
+    unit_rows = rows * (1 + len(others))
+    for h in range(heads):
+        for n in range(2):
+            lanes = pl.ds(pl.multiple_of(n * (width // 2) + (core * heads + h) * HD, HD), HD)
+            draft_ref[h, n * LANES : (n + 1) * LANES, :] = rows_ref[:, lanes].astype(bf16)
+        unit_ref[h] = jnp.concatenate(
+            [
+                rows_ref[
+                    :unit_rows,
+                    pl.ds(pl.multiple_of(n * (width // 2) + (core * heads + h) * HD, HD), HD),
+                ]
+                for n in range(2)
+            ],
+            axis=0,
+        ).astype(bf16)
+
+
+def chip_drafts(split, heads, own, others):
+    rows, width = own.shape
+    return pl.pallas_call(
+        functools.partial(drafts_kernel, split),
+        in_specs=[pl.BlockSpec(memory_space=pltpu.VMEM)] * (1 + len(others)),
+        out_shape=(
+            jax.ShapeDtypeStruct((heads, 2 * LANES, HD), bf16),
+            jax.ShapeDtypeStruct((heads, 2 * rows * split, HD), bf16),
+        ),
+        scratch_shapes=[pltpu.VMEM((LANES, width), f32)],
+        compiler_params=pltpu.CompilerParams(vmem_limit_bytes=VMEM_BYTES),
+    )(own, *others)
+
+
 def append_kernel(rel, split, unit_rows, scal, ck_ref, cv_ref, mine_ref, other_ref, *rest):
     nk_ref, nv_ref = rest[-2:]
     rows, width = ck_ref.shape
@@ -417,40 +456,34 @@
 
     q4 = dq.reshape(local_rows, heads_kv, GROUP, LANES).transpose(1, 0, 2, 3)
     q4 = q4.reshape(heads_kv, local_rows * GROUP, LANES)
-    dk4 = dk.reshape(local_rows, heads_kv, HD).transpose(1, 0, 2)
-    dv4 = dv.reshape(local_rows, heads_kv, HD).transpose(1, 0, 2)
-    pack = jnp.concatenate([q4, dk4, dv4], axis=1)
-    parts, caches = [pack], [ck, cv]
+    drafts_own = jnp.concatenate([dk, dv], axis=1)
+    caches, drafts_other = [ck, cv], []
+    q = q4
     if split == 2:
-        mine = lax.dynamic_slice_in_dim(pack, core * heads, heads, 0)
-        parts = [mine, swap(lax.dynamic_slice_in_dim(pack, (1 - core) * heads, heads, 0), 0)]
-    cut = local_rows * GROUP
-    second = cut + local_rows
-    pieces = [p[:, :cut] for p in parts]
-    pieces += [p[:, cut : cut + local_rows] for p in parts]
-    pieces += [p[:, second : second + local_rows] for p in parts]
-    q = jnp.concatenate(pieces, axis=1)
-    d_key, d_value = q[:, unit : unit + unit_rows], q[:, unit + unit_rows :]
-    spare = ((0, 0), (0, LANES - unit_rows), (0, 0))
-    drafts = jnp.concatenate([jnp.pad(d_key, spare), jnp.pad(d_value, spare)], axis=1)
+        mine = lax.dynamic_slice_in_dim(q4, core * heads, heads, 0)
+        sent = lax.dynamic_slice_in_dim(q4, (1 - core) * heads, heads, 0)
+        q = jnp.concatenate([mine, swap(sent, 0)], axis=1)
     q, scal = lax.optimization_barrier(
         (q[None], jnp.broadcast_to(jnp.stack([length, accepted]), (2, LANES)))
     )
     if split == 2:
-        q, ck_late, cv_late = lax.optimization_barrier((q, ck, cv))
-        caches += [swap(ck_late, 0), swap(cv_late, 0)]
+        q, drafts_own, *late = lax.optimization_barrier((q, drafts_own, ck, cv))
+        drafts_other = [swap(drafts_own, 0)]
+        caches += [swap(c, 0) for c in late]
 
     rel, near = [0], bits[-1]
     for bit in bits[:-1]:
         new = swap(q, bit)
         q = jnp.concatenate([q, new], axis=0)
         if split == 2 and bit == bits[0]:
-            q, *own = lax.optimization_barrier((q, ck, cv))
+            q, drafts_own, drafts_other, *own = lax.optimization_barrier(
+                (q, drafts_own, drafts_other, ck, cv)
+            )
             caches[:2] = [
                 lax.dynamic_slice_in_dim(c, core * heads * HD, heads * HD, 1) for c in own
             ]
         rel = rel + [r | (1 << bit) // split for r in rel]
-    q, dkv = q[:, :, :unit], q[:, :, unit:]
+    drafts, chip_rows = chip_drafts(split, heads, drafts_own, drafts_other)
     rel_far = [r | (1 << near) // split for r in rel]
     q_far = swap(q, near)
 
@@ -459,20 +492,25 @@
     num, stats = run(q_far, rel_far, unit_rows, split, caches, drafts, False, (message,))
     message = swap(message, near)
 
-    dkv = jnp.concatenate([dkv, swap(dkv, near)], axis=0)
+    dkv, order = chip_rows[None], [0]
 
     for bit in reversed(bits[:-1]):
         mode = "all" if bit == bits[0] else "half"
         num, stats, message = merge(unit, mode, num, stats, message)
+        if bit in (bits[-2], bits[0]):
+            num, dkv = lax.optimization_barrier((num, dkv))
+            for late in bits[-2:-1] if bit == bits[-2] else bits[:-2]:
+                dkv = jnp.concatenate([dkv, swap(dkv, late)], axis=0)
+                order = order + [r ^ (1 << late) // split for r in order]
         message = swap(message, bit)
 
     att = merge(unit, "final", num, stats, message).reshape(-1, heads, unit, LANES)
-    att, dkv = lax.optimization_barrier((att, dkv))
-    every = [dkv, swap(dkv, 0)] if split == 2 else [dkv]
     for bit in bits[1:-1]:
         att = jnp.concatenate([att, swap(att, bit)], axis=0)
-    att, every = lax.optimization_barrier((att, every))
+    att, dkv = lax.optimization_barrier((att, dkv))
     att_near = swap(att, near)
+    dkv = jnp.concatenate([dkv, swap(dkv, near)], axis=0)
+    order = order + [r ^ (1 << near) // split for r in order]
     halves = (rel_far, rel)
     if split == 2:
         begun = project(
@@ -483,6 +521,7 @@
             [att, att_near, swap(att, 0)],
             weight,
         )
+        begun, dkv = lax.optimization_barrier((begun, dkv))
         result = project(
             halves, split, n_head, ((1, 1),), [swap(att_near, 0)], weight, begun, True
         )
@@ -495,8 +534,9 @@
         projected = keep + lax.ppermute(send, "head", [(0, 1), (1, 0)]).astype(f32)
     else:
         projected = lax.psum_scatter(result[0], "head", scatter_dimension=0, tiled=True)
+    every = [dkv, swap(dkv, 0)] if split == 2 else [dkv]
     new_key, new_value = append(
-        rel + rel_far, split, unit_rows, scal, ck, cv, every, (result[-1],)
+        order, split, unit_rows, scal, ck, cv, every, (result[-1],)
     )
     return projected.astype(bf16), new_key, new_value
 

time: 59.1 us -> 58.5 us (0.990)
  waiting for transfers between devices: 24.9 us -> 22.3 us
  starting transfers between devices: 16.9 us -> 19.1 us
    ppermute x15 -> x18, waiting for transfers between devices: 24.7 us -> 22.1 us  [swap(): return lax.ppermute(x, 'seq', [(i, i ^ 1 << bit) for i in range(n_seq)])]
    ppermute x15 -> x18, starting transfers between devices: 15.3 us -> 17.5 us  [swap(): return lax.ppermute(x, 'seq', [(i, i ^ 1 << bit) for i in range(n_seq)])]
  transfers between devices with their start and end apart: 16 -> 19, of which waited for: 10 -> 11; matrix products, arithmetic and copies ran while one was open for 3% -> 4% of each run, Pallas kernels for 16% -> 18%
where the time goes in v5:
time: 58.5 us; the launch traced here: 58.3 us
  waiting for transfers between devices  22.3 us (38%)
  starting transfers between devices  19.1 us (33%)
  Pallas kernels  11 us (19%)
  local copies, waits for them, and re-layouts  2.24 us (4%)
  between operations  2.11 us (4%)
  other arithmetic  1.48 us (3%)
    ppermute x18, waiting for transfers between devices, swap(): return lax.ppermute(x, 'seq', [(i, i ^ 1 << bit) for i in range(n_seq)])  22.1 us
    ppermute x18, starting transfers between devices, swap(): return lax.ppermute(x, 'seq', [(i, i ^ 1 << bit) for i in range(n_seq)])  17.5 us
    pallas_call x2, Pallas kernels, attend(): pl.pallas_call(functools.partial(attend_kernel, rel, unit_rows, split, as...  5.96 us
    pallas_call x1, Pallas kernels, append(): pl.pallas_call(functools.partial(append_kernel, rel, split, unit_rows), g...  2.34 us
    pallas_call x2, Pallas kernels, project(): pl.pallas_call(functools.partial(project_kernel, rel, split, n_head, part...  1.59 us
    ppermute x1, starting transfers between devices, one_request(): projected = keep + lax.ppermute(send, 'head', [(0, 1), (1, 0)]).astype(f32)  1.57 us
    dynamic_slice x1, local copies, waits for them, and re-layouts, one_request(): lax.dynamic_slice_in_dim(c, core * heads * HD, heads * HD, 1)  1.28 us
  transfers between devices with their start and end apart: 19, of which 11 were waited for; matrix products, arithmetic and copies ran while one was open for 4% of the time, Pallas kernels for 18%

profile of v5, /device:TPU:0, one launch (start us, length us, event | category | flops | bytes accessed | tf_op | source)
XLA Modules:
  0.0 58.3 jit_solution(10953657272278118117)
XLA Ops:
  0.6 0.8 %copy_bitcast_fusion.1 = bf16[4,48,128]{2,1,0:T(8,128)(2,1)S(1)} fusion(bf16[1,6,32,128]{3,1,2,0:T(8,128)(2,1)} %bitcast.38), kind=kLoop, calls=%fused_computation.8 | loop fusion | bytes 98304 | tf_op jit(solution)/shard_map/reshape | solution.py:458
  3.3 0.7 %pad_maximum_fusion.5.own_ref = bf16[6,1024]{1,0:T(8,128)(2,1)S(1)} fusion(bf16[6,512]{1,0:T(8,128)(2,1)} %bitcast.39, bf16[6,512]{1,0:T(8,128)(2,1)} %bitcast.40), kind=kLoop, calls=%fused_computation.10 | loop fusion | flops 24576 | bytes 24576 | tf_op jit(solution)/shard_map/concatenate | solution.py:459
  4.7 3.7 %collective-permute-start.1 = (bf16[1,2,96,128]{3,2,1,0:T(8,128)(2,1)S(1)}, bf16[1,2,96,128]{3,2,1,0:T(8,128)(2,1)S(1)}, u32[]{:S(2)}, u32[]{:S(2)}) collective-permute-start(bf16[1,2,96,128]{3,2,1,0:T(8,128)(2,1)S(1)} %maximum_bitcast_fusion), channel_id=1, source_target_pairs={{0,16},{2,18},{4,20},{6,22},{8,24},{10,26},{12,28},{14,30},{16,0},... | collective-permute-start | bytes 147464 | tf_op jit(solution)/shard_map/ppermute | solution.py:453
  8.5 2.2 %collective-permute-done.1 = bf16[1,2,96,128]{3,2,1,0:T(8,128)(2,1)S(1)} collective-permute-done((bf16[1,2,96,128]{3,2,1,0:T(8,128)(2,1)S(1)}, bf16[1,2,96,128]{3,2,1,0:T(8,128)(2,1)S(1)}, u32[]{:S(2)}, u32[]{:S(2)}) %collective-permute-start.1) | collective-permute-done | bytes 49184 | tf_op jit(solution)/shard_map/ppermute | solution.py:453
  10.7 1.9 %collective-permute-start.3 = (bf16[2,2,96,128]{3,2,1,0:T(8,128)(2,1)S(1)}, bf16[2,2,96,128]{3,2,1,0:T(8,128)(2,1)S(1)}, u32[]{:S(2)}, u32[]{:S(2)}) collective-permute-start(bf16[2,2,96,128]{3,2,1,0:T(8,128)(2,1)S(1)} %pad_maximum_fusion.1), channel_id=1, source_target_pairs={{0,8},{2,10},{4,12},{6,14},{8,0},{10,2},{12,4},{14,6},{16,24},{18,... | collective-permute-start | bytes 294920 | tf_op jit(solution)/shard_map/ppermute | solution.py:453
  12.7 1.3 %constant_dynamic-slice_fusion = (bf16[1024,256]{1,0:T(8,128)(2,1)S(1)}, bf16[1024,256]{1,0:T(8,128)(2,1)S(1)}) fusion(bf16[1024,512]{1,0:T(8,128)(2,1)} %bitcast.29, s32[]{:T(128)S(6)} %select_n.20, bf16[1024,512]{1,0:T(8,128)(2,1)} %bitcast.32), kind=kLoop, calls=%fused_computation.13 | loop fusion | bytes 2097156 | tf_op jit(solution)/shard_map/dynamic_slice | solution.py:483
  14.0 1.6 %collective-permute-done.3 = bf16[2,2,96,128]{3,2,1,0:T(8,128)(2,1)S(1)} collective-permute-done((bf16[2,2,96,128]{3,2,1,0:T(8,128)(2,1)S(1)}, bf16[2,2,96,128]{3,2,1,0:T(8,128)(2,1)S(1)}, u32[]{:S(2)}, u32[]{:S(2)}) %collective-permute-start.3) | collective-permute-done | bytes 98336 | tf_op jit(solution)/shard_map/ppermute | solution.py:453
  15.6 1.6 %collective-permute-start.4 = (bf16[4,2,96,128]{3,2,1,0:T(8,128)(2,1)S(1)}, bf16[4,2,96,128]{3,2,1,0:T(8,128)(2,1)S(1)}, u32[]{:S(2)}, u32[]{:S(2)}) collective-permute-start(bf16[4,2,96,128]{3,2,1,0:T(8,128)(2,1)S(1)} %constant_dynamic-update-slice_fusion.q_ref), channel_id=1, source_target_pairs={{0,4},{2,6},{4,0},{6,2},{8,12},{10,14},{12,8},{14,10},{16,20},{18,... | collective-permute-start | bytes 589832 | tf_op jit(solution)/shard_map/ppermute | solution.py:453
  17.2 3.0 %shard_map.104.rest_5_ = bf16[800,128]{1,0:T(8,128)(2,1)S(1)} custom-call(s32[2,128]{1,0:T(2,128)S(1)} %broadcast_in_dim.15.scal, bf16[4,2,96,128]{3,2,1,0:T(8,128)(2,1)S(1)} %constant_dynamic-update-slice_fusion.q_ref, bf16[1024,256]{1,0:T(8,128)(2,1)S(1)} %get-tuple-element.72.rest_0_, bf16[1024,256]{1,0:T(8,128)(2,1)S(1)} %get-tuple-element.71.rest_1_, ...), custom_call_target="tpu_custom_call" | custom-call | flops 855638016 | bytes 2097152 | tf_op jit(solution)/shard_map/pallas_call | solution.py:183
  20.8 1.0 %collective-permute-done.4.q_ref = bf16[4,2,96,128]{3,2,1,0:T(8,128)(2,1)S(1)} collective-permute-done((bf16[4,2,96,128]{3,2,1,0:T(8,128)(2,1)S(1)}, bf16[4,2,96,128]{3,2,1,0:T(8,128)(2,1)S(1)}, u32[]{:S(2)}, u32[]{:S(2)}) %collective-permute-start.4) | collective-permute-done | bytes 196640 | tf_op jit(solution)/shard_map/ppermute | solution.py:453
  21.8 3.0 %shard_map.105 = (f32[768,128]{1,0:T(8,128)S(1)}, f32[16,128]{1,0:T(8,128)S(1)}) custom-call(s32[2,128]{1,0:T(2,128)S(1)} %broadcast_in_dim.15.scal, bf16[4,2,96,128]{3,2,1,0:T(8,128)(2,1)S(1)} %collective-permute-done.4.q_ref, bf16[1024,256]{1,0:T(8,128)(2,1)S(1)} %get-tuple-element.72.rest_0_, bf16[1024,256]{1,0:T(8,128)(2,1)S(1)} %get-tuple-element.71.rest_1_, ...), custom_call_target="tpu_custom_call" | custom-call | flops 855638016 | bytes 2097152 | tf_op jit(solution)/shard_map/pallas_call | solution.py:183
  24.8 1.4 %collective-permute-done.7.msg_ref = bf16[800,128]{1,0:T(8,128)(2,1)S(1)} collective-permute-done((bf16[800,128]{1,0:T(8,128)(2,1)S(1)}, bf16[800,128]{1,0:T(8,128)(2,1)S(1)}, u32[]{:S(2)}, u32[]{:S(2)}) %collective-permute-start.7) | collective-permute-done | bytes 204832 | tf_op jit(solution)/shard_map/ppermute | solution.py:453
  26.6 1.8 %collective-permute-start.8 = (bf16[416,128]{1,0:T(8,128)(2,1)S(1)}, bf16[416,128]{1,0:T(8,128)(2,1)S(1)}, u32[]{:S(2)}, u32[]{:S(2)}) collective-permute-start(bf16[416,128]{1,0:T(8,128)(2,1)S(1)} %get-tuple-element.54), channel_id=1, source_target_pairs={{0,8},{2,10},{4,12},{6,14},{8,0},{10,2},{12,4},{14,6},{16,24},{18,... | collective-permute-start | bytes 319496 | tf_op jit(solution)/shard_map/ppermute | solution.py:453
  28.7 2.7 %collective-permute-done.8.msg_ref = bf16[416,128]{1,0:T(8,128)(2,1)S(1)} collective-permute-done((bf16[416,128]{1,0:T(8,128)(2,1)S(1)}, bf16[416,128]{1,0:T(8,128)(2,1)S(1)}, u32[]{:S(2)}, u32[]{:S(2)}) %collective-permute-start.8) | collective-permute-done | bytes 106528 | tf_op jit(solution)/shard_map/ppermute | solution.py:453
  31.7 4.3 %collective-permute-start.10 = (bf16[416,128]{1,0:T(8,128)(2,1)S(1)}, bf16[416,128]{1,0:T(8,128)(2,1)S(1)}, u32[]{:S(2)}, u32[]{:S(2)}) collective-permute-start(bf16[416,128]{1,0:T(8,128)(2,1)S(1)} %get-tuple-element.59), channel_id=1, source_target_pairs={{0,16},{2,18},{4,20},{6,22},{8,24},{10,26},{12,28},{14,30},{16,0},... | collective-permute-start | bytes 319496 | tf_op jit(solution)/shard_map/ppermute | solution.py:453
  36.0 3.8 %collective-permute-done.10.msg_ref = bf16[416,128]{1,0:T(8,128)(2,1)S(1)} collective-permute-done((bf16[416,128]{1,0:T(8,128)(2,1)S(1)}, bf16[416,128]{1,0:T(8,128)(2,1)S(1)}, u32[]{:S(2)}, u32[]{:S(2)}) %collective-permute-start.10) | collective-permute-done | bytes 106528 | tf_op jit(solution)/shard_map/ppermute | solution.py:453
  40.7 4.2 %collective-permute-done.11 = bf16[2,2,96,128]{3,2,1,0:T(8,128)(2,1)S(1)} collective-permute-done((bf16[2,2,96,128]{3,2,1,0:T(8,128)(2,1)S(1)}, bf16[2,2,96,128]{3,2,1,0:T(8,128)(2,1)S(1)}, u32[]{:S(2)}, u32[]{:S(2)}) %collective-permute-start.11) | collective-permute-done | bytes 98336 | tf_op jit(solution)/shard_map/ppermute | solution.py:453
  44.9 1.2 %collective-permute-start.13 = (bf16[4,2,96,128]{3,2,1,0:T(8,128)(2,1)S(1)}, bf16[4,2,96,128]{3,2,1,0:T(8,128)(2,1)S(1)}, u32[]{:S(2)}, u32[]{:S(2)}) collective-permute-start(bf16[4,2,96,128]{3,2,1,0:T(8,128)(2,1)S(1)} %pad_maximum_fusion.refs_0_), channel_id=1, source_target_pairs={{0,4},{2,6},{4,0},{6,2},{8,12},{10,14},{12,8},{14,10},{16,20},{18,... | collective-permute-start | bytes 589832 | tf_op jit(solution)/shard_map/ppermute | solution.py:453
  46.1 0.9 %collective-permute-start.16 = (bf16[4,2,24,128]{3,2,1,0:T(8,128)(2,1)S(1)}, bf16[4,2,24,128]{3,2,1,0:T(8,128)(2,1)S(1)}, u32[]{:S(2)}, u32[]{:S(2)}) collective-permute-start(bf16[4,2,24,128]{3,2,1,0:T(8,128)(2,1)S(1)} %pad_maximum_fusion.3), channel_id=1, source_target_pairs={{0,4},{2,6},{4,0},{6,2},{8,12},{10,14},{12,8},{14,10},{16,20},{18,... | collective-permute-start | bytes 147464 | tf_op jit(solution)/shard_map/ppermute | solution.py:453
  47.0 4.2 %collective-permute-done.13.refs_1_ = bf16[4,2,96,128]{3,2,1,0:T(8,128)(2,1)S(1)} collective-permute-done((bf16[4,2,96,128]{3,2,1,0:T(8,128)(2,1)S(1)}, bf16[4,2,96,128]{3,2,1,0:T(8,128)(2,1)S(1)}, u32[]{:S(2)}, u32[]{:S(2)}) %collective-permute-start.13) | collective-permute-done | bytes 196640 | tf_op jit(solution)/shard_map/ppermute | solution.py:453
  51.7 1.0 %shard_map.109.refs_2_ = f32[96,512]{1,0:T(8,128)S(1)} custom-call(bf16[4,2,96,128]{3,2,1,0:T(8,128)(2,1)S(1)} %pad_maximum_fusion.refs_0_, bf16[4,2,96,128]{3,2,1,0:T(8,128)(2,1)S(1)} %collective-permute-done.13.refs_1_, bf16[4,2,96,128]{3,2,1,0:T(8,128)(2,1)S(1)} %collective-permute-done.15.refs_2_, bf16[4096,512]{1,0:T(8,128)(2,1)S(1)} %copy-done), custom_call_target="tpu_custom_call" | custom-call | flops 402653184 | bytes 4194304 | tf_op jit(solution)/shard_map/pallas_call | solution.py:321
  53.4 1.6 %collective-permute-start.17 = (bf16[48,512]{1,0:T(8,128)(2,1)S(1)}, bf16[48,512]{1,0:T(8,128)(2,1)S(1)}, u32[]{:S(2)}, u32[]{:S(2)}) collective-permute-start(bf16[48,512]{1,0:T(8,128)(2,1)S(1)} %get-tuple-element.65.rest_0_), channel_id=1, source_target_pairs={{0,1},{1,0},{2,3},{3,2},{4,5},{5,4},{6,7},{7,6},{8,9},{9,8},{10,11... | collective-permute-start | bytes 147464 | tf_op jit(solution)/shard_map/ppermute | solution.py:534
  55.0 2.3 %shard_map.111 = (bf16[1024,512]{1,0:T(8,128)(2,1)}, bf16[1024,512]{1,0:T(8,128)(2,1)}) custom-call(s32[2,128]{1,0:T(2,128)S(1)} %broadcast_in_dim.15.scal, bf16[1024,512]{1,0:T(8,128)(2,1)S(1)} %bitcast.33, bf16[1024,512]{1,0:T(8,128)(2,1)S(1)} %bitcast.30, bf16[8,2,24,128]{3,2,1,0:T(8,128)(2,1)S(1)} %pad_maximum_fusion.2.mine_ref, ...), custom_call_target="tpu_custom_call" | custom-call | bytes 4194304 | tf_op jit(solution)/shard_map/pallas_call | solution.py:428
  57.6 0.6 %fusion = bf16[1,48,512]{2,1,0:T(8,128)(2,1)} fusion(f32[48,512]{1,0:T(8,128)S(1)} %get-tuple-element.64, bf16[48,512]{1,0:T(8,128)(2,1)S(1)} %collective-permute-done.17), kind=kLoop, calls=%fused_computation.4 | loop fusion | flops 73728 | bytes 196608 | tf_op jit(solution)/shard_map/stack | solution.py:551
  (44 shorter events, 5.4 us)
Async XLA Ops:
  1.5 2.6 %collective-permute-start = (bf16[2,48,128]{2,1,0:T(8,128)(2,1)S(1)}, bf16[2,48,128]{2,1,0:T(8,128)(2,1)S(1)}, u32[]{:S(2)}, u32[]{:S(2)}) collective-permute-start(bf16[2,48,128]{2,1,0:T(8,128)(2,1)S(1)} %get-tuple-element.70), channel_id=1, source_target_pairs={{0,2},{2,0},{4,6},{6,4},{8,10},{10,8},{12,14},{14,12},{16,18},{18,... | collective-permute-start | bytes 73736 | tf_op jit(solution)/shard_map/ppermute | solution.py:453
  4.2 13.0 %collective-permute-start.5 = (bf16[1024,512]{1,0:T(8,128)(2,1)}, bf16[1024,512]{1,0:T(8,128)(2,1)S(1)}, u32[]{:S(2)}, u32[]{:S(2)}) collective-permute-start(bf16[1024,512]{1,0:T(8,128)(2,1)} %bitcast.31), channel_id=1, source_target_pairs={{0,2},{2,0},{4,6},{6,4},{8,10},{10,8},{12,14},{14,12},{16,18},{18,... | collective-permute-start | bytes 3145736 | tf_op jit(solution)/shard_map/ppermute | solution.py:453
  4.3 12.9 %collective-permute-start.6 = (bf16[1024,512]{1,0:T(8,128)(2,1)}, bf16[1024,512]{1,0:T(8,128)(2,1)S(1)}, u32[]{:S(2)}, u32[]{:S(2)}) collective-permute-start(bf16[1024,512]{1,0:T(8,128)(2,1)} %bitcast.28), channel_id=1, source_target_pairs={{0,2},{2,0},{4,6},{6,4},{8,10},{10,8},{12,14},{14,12},{16,18},{18,... | collective-permute-start | bytes 3145736 | tf_op jit(solution)/shard_map/ppermute | solution.py:453
  4.7 6.0 %collective-permute-start.1 = (bf16[1,2,96,128]{3,2,1,0:T(8,128)(2,1)S(1)}, bf16[1,2,96,128]{3,2,1,0:T(8,128)(2,1)S(1)}, u32[]{:S(2)}, u32[]{:S(2)}) collective-permute-start(bf16[1,2,96,128]{3,2,1,0:T(8,128)(2,1)S(1)} %maximum_bitcast_fusion), channel_id=1, source_target_pairs={{0,16},{2,18},{4,20},{6,22},{8,24},{10,26},{12,28},{14,30},{16,0},... | collective-permute-start | bytes 147464 | tf_op jit(solution)/shard_map/ppermute | solution.py:453
  8.4 2.4 %collective-permute-start.2 = (bf16[6,1024]{1,0:T(8,128)(2,1)S(1)}, bf16[6,1024]{1,0:T(8,128)(2,1)S(1)}, u32[]{:S(2)}, u32[]{:S(2)}) collective-permute-start(bf16[6,1024]{1,0:T(8,128)(2,1)S(1)} %pad_maximum_fusion.5.own_ref), channel_id=1, source_target_pairs={{0,2},{2,0},{4,6},{6,4},{8,10},{10,8},{12,14},{14,12},{16,18},{18,... | collective-permute-start | bytes 36872 | tf_op jit(solution)/shard_map/ppermute | solution.py:453
  10.7 4.9 %collective-permute-start.3 = (bf16[2,2,96,128]{3,2,1,0:T(8,128)(2,1)S(1)}, bf16[2,2,96,128]{3,2,1,0:T(8,128)(2,1)S(1)}, u32[]{:S(2)}, u32[]{:S(2)}) collective-permute-start(bf16[2,2,96,128]{3,2,1,0:T(8,128)(2,1)S(1)} %pad_maximum_fusion.1), channel_id=1, source_target_pairs={{0,8},{2,10},{4,12},{6,14},{8,0},{10,2},{12,4},{14,6},{16,24},{18,... | collective-permute-start | bytes 294920 | tf_op jit(solution)/shard_map/ppermute | solution.py:453
  15.6 6.2 %collective-permute-start.4 = (bf16[4,2,96,128]{3,2,1,0:T(8,128)(2,1)S(1)}, bf16[4,2,96,128]{3,2,1,0:T(8,128)(2,1)S(1)}, u32[]{:S(2)}, u32[]{:S(2)}) collective-permute-start(bf16[4,2,96,128]{3,2,1,0:T(8,128)(2,1)S(1)} %constant_dynamic-update-slice_fusion.q_ref), channel_id=1, source_target_pairs={{0,4},{2,6},{4,0},{6,2},{8,12},{10,14},{12,8},{14,10},{16,20},{18,... | collective-permute-start | bytes 589832 | tf_op jit(solution)/shard_map/ppermute | solution.py:453
  17.2 34.5 %copy-start = (bf16[4096,512]{1,0:T(8,128)(2,1)S(1)}, bf16[4096,512]{1,0:T(8,128)(2,1)}, u32[]{:S(2)}) copy-start(bf16[4096,512]{1,0:T(8,128)(2,1)} %refs_1_.1) | copy-start | bytes 12582916
  20.2 6.0 %collective-permute-start.7 = (bf16[800,128]{1,0:T(8,128)(2,1)S(1)}, bf16[800,128]{1,0:T(8,128)(2,1)S(1)}, u32[]{:S(2)}, u32[]{:S(2)}) collective-permute-start(bf16[800,128]{1,0:T(8,128)(2,1)S(1)} %shard_map.104.rest_5_), channel_id=1, source_target_pairs={{0,4},{2,6},{4,0},{6,2},{8,12},{10,14},{12,8},{14,10},{16,20},{18,... | collective-permute-start | bytes 614408 | tf_op jit(solution)/shard_map/ppermute | solution.py:453
  26.6 4.8 %collective-permute-start.8 = (bf16[416,128]{1,0:T(8,128)(2,1)S(1)}, bf16[416,128]{1,0:T(8,128)(2,1)S(1)}, u32[]{:S(2)}, u32[]{:S(2)}) collective-permute-start(bf16[416,128]{1,0:T(8,128)(2,1)S(1)} %get-tuple-element.54), channel_id=1, source_target_pairs={{0,8},{2,10},{4,12},{6,14},{8,0},{10,2},{12,4},{14,6},{16,24},{18,... | collective-permute-start | bytes 319496 | tf_op jit(solution)/shard_map/ppermute | solution.py:453
  28.4 7.6 %collective-permute-start.9 = (bf16[1,2,24,128]{3,2,1,0:T(8,128)(2,1)S(1)}, bf16[1,2,24,128]{3,2,1,0:T(8,128)(2,1)S(1)}, u32[]{:S(2)}, u32[]{:S(2)}) collective-permute-start(bf16[1,2,24,128]{3,2,1,0:T(8,128)(2,1)S(1)} %bitcast.36), channel_id=1, source_target_pairs={{0,8},{2,10},{4,12},{6,14},{8,0},{10,2},{12,4},{14,6},{16,24},{18,... | collective-permute-start | bytes 36872 | tf_op jit(solution)/shard_map/ppermute | solution.py:453
  31.7 8.2 %collective-permute-start.10 = (bf16[416,128]{1,0:T(8,128)(2,1)S(1)}, bf16[416,128]{1,0:T(8,128)(2,1)S(1)}, u32[]{:S(2)}, u32[]{:S(2)}) collective-permute-start(bf16[416,128]{1,0:T(8,128)(2,1)S(1)} %get-tuple-element.59), channel_id=1, source_target_pairs={{0,16},{2,18},{4,20},{6,22},{8,24},{10,26},{12,28},{14,30},{16,0},... | collective-permute-start | bytes 319496 | tf_op jit(solution)/shard_map/ppermute | solution.py:453
  35.9 4.7 %collective-permute-start.12 = (bf16[2,2,24,128]{3,2,1,0:T(8,128)(2,1)S(1)}, bf16[2,2,24,128]{3,2,1,0:T(8,128)(2,1)S(1)}, u32[]{:S(2)}, u32[]{:S(2)}) collective-permute-start(bf16[2,2,24,128]{3,2,1,0:T(8,128)(2,1)S(1)} %pad_maximum_fusion.4), channel_id=1, source_target_pairs={{0,16},{2,18},{4,20},{6,22},{8,24},{10,26},{12,28},{14,30},{16,0},... | collective-permute-start | bytes 73736 | tf_op jit(solution)/shard_map/ppermute | solution.py:453
  40.2 4.7 %collective-permute-start.11 = (bf16[2,2,96,128]{3,2,1,0:T(8,128)(2,1)S(1)}, bf16[2,2,96,128]{3,2,1,0:T(8,128)(2,1)S(1)}, u32[]{:S(2)}, u32[]{:S(2)}) collective-permute-start(bf16[2,2,96,128]{3,2,1,0:T(8,128)(2,1)S(1)} %bitcast.34), channel_id=1, source_target_pairs={{0,8},{2,10},{4,12},{6,14},{8,0},{10,2},{12,4},{14,6},{16,24},{18,... | collective-permute-start | bytes 294920 | tf_op jit(solution)/shard_map/ppermute | solution.py:453
  44.9 6.3 %collective-permute-start.13 = (bf16[4,2,96,128]{3,2,1,0:T(8,128)(2,1)S(1)}, bf16[4,2,96,128]{3,2,1,0:T(8,128)(2,1)S(1)}, u32[]{:S(2)}, u32[]{:S(2)}) collective-permute-start(bf16[4,2,96,128]{3,2,1,0:T(8,128)(2,1)S(1)} %pad_maximum_fusion.refs_0_), channel_id=1, source_target_pairs={{0,4},{2,6},{4,0},{6,2},{8,12},{10,14},{12,8},{14,10},{16,20},{18,... | collective-permute-start | bytes 589832 | tf_op jit(solution)/shard_map/ppermute | solution.py:453
  46.1 5.6 %collective-permute-start.15 = (bf16[4,2,96,128]{3,2,1,0:T(8,128)(2,1)S(1)}, bf16[4,2,96,128]{3,2,1,0:T(8,128)(2,1)S(1)}, u32[]{:S(2)}, u32[]{:S(2)}) collective-permute-start(bf16[4,2,96,128]{3,2,1,0:T(8,128)(2,1)S(1)} %pad_maximum_fusion.refs_0_), channel_id=1, source_target_pairs={{0,2},{2,0},{4,6},{6,4},{8,10},{10,8},{12,14},{14,12},{16,18},{18,... | collective-permute-start | bytes 589832 | tf_op jit(solution)/shard_map/ppermute | solution.py:453
  46.1 5.6 %collective-permute-start.16 = (bf16[4,2,24,128]{3,2,1,0:T(8,128)(2,1)S(1)}, bf16[4,2,24,128]{3,2,1,0:T(8,128)(2,1)S(1)}, u32[]{:S(2)}, u32[]{:S(2)}) collective-permute-start(bf16[4,2,24,128]{3,2,1,0:T(8,128)(2,1)S(1)} %pad_maximum_fusion.3), channel_id=1, source_target_pairs={{0,4},{2,6},{4,0},{6,2},{8,12},{10,14},{12,8},{14,10},{16,20},{18,... | collective-permute-start | bytes 147464 | tf_op jit(solution)/shard_map/ppermute | solution.py:453
  51.1 1.7 %collective-permute-start.14 = (bf16[4,2,96,128]{3,2,1,0:T(8,128)(2,1)S(1)}, bf16[4,2,96,128]{3,2,1,0:T(8,128)(2,1)S(1)}, u32[]{:S(2)}, u32[]{:S(2)}) collective-permute-start(bf16[4,2,96,128]{3,2,1,0:T(8,128)(2,1)S(1)} %collective-permute-done.13.refs_1_), channel_id=1, source_target_pairs={{0,2},{2,0},{4,6},{6,4},{8,10},{10,8},{12,14},{14,12},{16,18},{18,... | collective-permute-start | bytes 589832 | tf_op jit(solution)/shard_map/ppermute | solution.py:453
  51.7 3.3 %copy-start.1 = (bf16[1,1024,512]{2,1,0:T(8,128)(2,1)S(1)}, bf16[1,1024,512]{2,1,0:T(8,128)(2,1)}, u32[]{:S(2)}) copy-start(bf16[1,1024,512]{2,1,0:T(8,128)(2,1)} %param.12) | copy-start | bytes 3145732
  51.7 3.3 %copy-start.2 = (bf16[1,1024,512]{2,1,0:T(8,128)(2,1)S(1)}, bf16[1,1024,512]{2,1,0:T(8,128)(2,1)}, u32[]{:S(2)}) copy-start(bf16[1,1024,512]{2,1,0:T(8,128)(2,1)} %param.11) | copy-start | bytes 3145732
  52.8 2.2 %collective-permute-start.18 = (bf16[8,2,24,128]{3,2,1,0:T(8,128)(2,1)S(1)}, bf16[8,2,24,128]{3,2,1,0:T(8,128)(2,1)S(1)}, u32[]{:S(2)}, u32[]{:S(2)}) collective-permute-start(bf16[8,2,24,128]{3,2,1,0:T(8,128)(2,1)S(1)} %pad_maximum_fusion.2.mine_ref), channel_id=1, source_target_pairs={{0,2},{2,0},{4,6},{6,4},{8,10},{10,8},{12,14},{14,12},{16,18},{18,... | collective-permute-start | bytes 294920 | tf_op jit(solution)/shard_map/ppermute | solution.py:453
  53.4 4.2 %collective-permute-start.17 = (bf16[48,512]{1,0:T(8,128)(2,1)S(1)}, bf16[48,512]{1,0:T(8,128)(2,1)S(1)}, u32[]{:S(2)}, u32[]{:S(2)}) collective-permute-start(bf16[48,512]{1,0:T(8,128)(2,1)S(1)} %get-tuple-element.65.rest_0_), channel_id=1, source_target_pairs={{0,1},{1,0},{2,3},{3,2},{4,5},{5,4},{6,7},{7,6},{8,9},{9,8},{10,11... | collective-permute-start | bytes 147464 | tf_op jit(solution)/shard_map/ppermute | solution.py:534

commit v6 on v5

--- a/solution.py
+++ b/solution.py
@@ -348,7 +348,7 @@
         for n in range(2):
             lanes = pl.ds(pl.multiple_of(n * (width // 2) + (core * heads + h) * HD, HD), HD)
             draft_ref[h, n * LANES : (n + 1) * LANES, :] = rows_ref[:, lanes].astype(bf16)
-        unit_ref[h] = jnp.concatenate(
+        chip_rows = jnp.concatenate(
             [
                 rows_ref[
                     :unit_rows,
@@ -357,7 +357,8 @@
                 for n in range(2)
             ],
             axis=0,
-        ).astype(bf16)
+        )
+        unit_ref[h] = pad_rows(chip_rows, unit_ref.shape[1]).astype(bf16)
 
 
 def chip_drafts(split, heads, own, others):
@@ -367,7 +368,7 @@
         in_specs=[pl.BlockSpec(memory_space=pltpu.VMEM)] * (1 + len(others)),
         out_shape=(
             jax.ShapeDtypeStruct((heads, 2 * LANES, HD), bf16),
-            jax.ShapeDtypeStruct((heads, 2 * rows * split, HD), bf16),
+            jax.ShapeDtypeStruct((heads, round_up(2 * rows * split, 8), HD), bf16),
         ),
         scratch_shapes=[pltpu.VMEM((LANES, width), f32)],
         compiler_params=pltpu.CompilerParams(vmem_limit_bytes=VMEM_BYTES),
@@ -392,29 +393,32 @@
 
     @pl.when(touched)
     def _():
-        place = first + lax.broadcasted_iota(jnp.int32, (rows, both), 0)
-        lane = lax.broadcasted_iota(jnp.int32, (rows, both), 1)
-        inside = (place >= 0) & (place < accepted)
+        depth = chips * both
+        place = first + lax.broadcasted_iota(jnp.int32, (rows, depth), 0)
+        lane = lax.broadcasted_iota(jnp.int32, (1, depth), 1)
+        base = jnp.zeros((1, depth), jnp.int32)
+        row = lane
+        for n in range(chips):
+            here = (lane >= n * both) & (lane < (n + 1) * both)
+            base = jnp.where(here, jnp.bitwise_xor(chip, rel[n]) * unit_rows, base)
+            row = jnp.where(here, lane - n * both, row)
         chosen = first + lax.broadcasted_iota(jnp.int32, (rows, HD), 0)
         chosen = (chosen >= 0) & (chosen < accepted)
         for side in range(split):
             drafts = mine_ref if side == 0 else other_ref
             source_core = core if side == 0 else 1 - core
+            values = [
+                drafts[:, h].astype(f32).reshape(depth, HD).astype(bf16) for h in range(heads)
+            ]
             for cache_ref, new_ref, start in ((ck_ref, nk_ref, 0), (cv_ref, nv_ref, unit_rows)):
-                sums = [jnp.zeros((rows, HD), f32)] * heads
-                here = (lane >= start) & (lane < start + unit_rows) & inside
-                row = row_of(lane - start, local_rows, source_core)
-                for n in range(chips):
-                    source = jnp.bitwise_xor(chip, rel[n]) * unit_rows + row
-                    pick = jnp.where(here & (source == place), 1.0, 0.0).astype(bf16)
-                    for h in range(heads):
-                        sums[h] = sums[h] + jnp.dot(
-                            pick, drafts[n, h], preferred_element_type=f32
-                        )
+                source = base + row_of(row - start, local_rows, source_core)
+                source = jnp.where((row >= start) & (row < start + unit_rows), source, -(1 << 24))
+                pick = jnp.where(source == place, 1.0, 0.0).astype(bf16)
                 for h in range(heads):
                     lanes = pl.ds(pl.multiple_of((source_core * heads + h) * HD, HD), HD)
+                    moved = jnp.dot(pick, values[h], preferred_element_type=f32)
                     new_ref[:, lanes] = jnp.where(
-                        chosen, sums[h], cache_ref[:, lanes].astype(f32)
+                        chosen, moved, cache_ref[:, lanes].astype(f32)
                     ).astype(bf16)
 
 

time: 58.5 us -> 58.5 us (level)
  no operation moved by 1% of the time
where the time goes in v6:
time: 58.5 us; the launch traced here: 58.3 us
  waiting for transfers between devices  22.3 us (38%)
  starting transfers between devices  19.1 us (33%)
  Pallas kernels  11 us (19%)
  local copies, waits for them, and re-layouts  2.24 us (4%)
  between operations  2.11 us (4%)
  other arithmetic  1.48 us (3%)
    ppermute x18, waiting for transfers between devices, swap(): return lax.ppermute(x, 'seq', [(i, i ^ 1 << bit) for i in range(n_seq)])  22.1 us
    ppermute x18, starting transfers between devices, swap(): return lax.ppermute(x, 'seq', [(i, i ^ 1 << bit) for i in range(n_seq)])  17.5 us
    pallas_call x2, Pallas kernels, attend(): pl.pallas_call(functools.partial(attend_kernel, rel, unit_rows, split, as...  5.96 us
    pallas_call x1, Pallas kernels, append(): pl.pallas_call(functools.partial(append_kernel, rel, split, unit_rows), g...  2.35 us
    pallas_call x2, Pallas kernels, project(): pl.pallas_call(functools.partial(project_kernel, rel, split, n_head, part...  1.59 us
    ppermute x1, starting transfers between devices, one_request(): projected = keep + lax.ppermute(send, 'head', [(0, 1), (1, 0)]).astype(f32)  1.57 us
    dynamic_slice x1, local copies, waits for them, and re-layouts, one_request(): lax.dynamic_slice_in_dim(c, core * heads * HD, heads * HD, 1)  1.28 us
  transfers between devices with their start and end apart: 19, of which 11 were waited for; matrix products, arithmetic and copies ran while one was open for 4% of the time, Pallas kernels for 18%

profile of v6, /device:TPU:0, one launch (start us, length us, event | category | flops | bytes accessed | tf_op | source)
XLA Modules:
  0.0 58.3 jit_solution(12139697427151271444)
XLA Ops:
  0.6 0.8 %copy_bitcast_fusion.1 = bf16[4,48,128]{2,1,0:T(8,128)(2,1)S(1)} fusion(bf16[1,6,32,128]{3,1,2,0:T(8,128)(2,1)} %bitcast.38), kind=kLoop, calls=%fused_computation.8 | loop fusion | bytes 98304 | tf_op jit(solution)/shard_map/reshape | solution.py:462
  3.3 0.7 %pad_maximum_fusion.5.own_ref = bf16[6,1024]{1,0:T(8,128)(2,1)S(1)} fusion(bf16[6,512]{1,0:T(8,128)(2,1)} %bitcast.39, bf16[6,512]{1,0:T(8,128)(2,1)} %bitcast.40), kind=kLoop, calls=%fused_computation.10 | loop fusion | flops 24576 | bytes 24576 | tf_op jit(solution)/shard_map/concatenate | solution.py:463
  4.7 3.7 %collective-permute-start.1 = (bf16[1,2,96,128]{3,2,1,0:T(8,128)(2,1)S(1)}, bf16[1,2,96,128]{3,2,1,0:T(8,128)(2,1)S(1)}, u32[]{:S(2)}, u32[]{:S(2)}) collective-permute-start(bf16[1,2,96,128]{3,2,1,0:T(8,128)(2,1)S(1)} %maximum_bitcast_fusion), channel_id=1, source_target_pairs={{0,16},{2,18},{4,20},{6,22},{8,24},{10,26},{12,28},{14,30},{16,0},... | collective-permute-start | bytes 147464 | tf_op jit(solution)/shard_map/ppermute | solution.py:457
  8.5 2.2 %collective-permute-done.1 = bf16[1,2,96,128]{3,2,1,0:T(8,128)(2,1)S(1)} collective-permute-done((bf16[1,2,96,128]{3,2,1,0:T(8,128)(2,1)S(1)}, bf16[1,2,96,128]{3,2,1,0:T(8,128)(2,1)S(1)}, u32[]{:S(2)}, u32[]{:S(2)}) %collective-permute-start.1) | collective-permute-done | bytes 49184 | tf_op jit(solution)/shard_map/ppermute | solution.py:457
  10.7 1.9 %collective-permute-start.3 = (bf16[2,2,96,128]{3,2,1,0:T(8,128)(2,1)S(1)}, bf16[2,2,96,128]{3,2,1,0:T(8,128)(2,1)S(1)}, u32[]{:S(2)}, u32[]{:S(2)}) collective-permute-start(bf16[2,2,96,128]{3,2,1,0:T(8,128)(2,1)S(1)} %pad_maximum_fusion.1), channel_id=1, source_target_pairs={{0,8},{2,10},{4,12},{6,14},{8,0},{10,2},{12,4},{14,6},{16,24},{18,... | collective-permute-start | bytes 294920 | tf_op jit(solution)/shard_map/ppermute | solution.py:457
  12.7 1.3 %constant_dynamic-slice_fusion = (bf16[1024,256]{1,0:T(8,128)(2,1)S(1)}, bf16[1024,256]{1,0:T(8,128)(2,1)S(1)}) fusion(bf16[1024,512]{1,0:T(8,128)(2,1)} %bitcast.29, s32[]{:T(128)S(6)} %select_n.20, bf16[1024,512]{1,0:T(8,128)(2,1)} %bitcast.32), kind=kLoop, calls=%fused_computation.13 | loop fusion | bytes 2097156 | tf_op jit(solution)/shard_map/dynamic_slice | solution.py:487
  14.0 1.6 %collective-permute-done.3 = bf16[2,2,96,128]{3,2,1,0:T(8,128)(2,1)S(1)} collective-permute-done((bf16[2,2,96,128]{3,2,1,0:T(8,128)(2,1)S(1)}, bf16[2,2,96,128]{3,2,1,0:T(8,128)(2,1)S(1)}, u32[]{:S(2)}, u32[]{:S(2)}) %collective-permute-start.3) | collective-permute-done | bytes 98336 | tf_op jit(solution)/shard_map/ppermute | solution.py:457
  15.6 1.6 %collective-permute-start.4 = (bf16[4,2,96,128]{3,2,1,0:T(8,128)(2,1)S(1)}, bf16[4,2,96,128]{3,2,1,0:T(8,128)(2,1)S(1)}, u32[]{:S(2)}, u32[]{:S(2)}) collective-permute-start(bf16[4,2,96,128]{3,2,1,0:T(8,128)(2,1)S(1)} %constant_dynamic-update-slice_fusion.q_ref), channel_id=1, source_target_pairs={{0,4},{2,6},{4,0},{6,2},{8,12},{10,14},{12,8},{14,10},{16,20},{18,... | collective-permute-start | bytes 589832 | tf_op jit(solution)/shard_map/ppermute | solution.py:457
  17.2 3.0 %shard_map.104.rest_5_ = bf16[800,128]{1,0:T(8,128)(2,1)S(1)} custom-call(s32[2,128]{1,0:T(2,128)S(1)} %broadcast_in_dim.15.scal, bf16[4,2,96,128]{3,2,1,0:T(8,128)(2,1)S(1)} %constant_dynamic-update-slice_fusion.q_ref, bf16[1024,256]{1,0:T(8,128)(2,1)S(1)} %get-tuple-element.72.rest_0_, bf16[1024,256]{1,0:T(8,128)(2,1)S(1)} %get-tuple-element.71.rest_1_, ...), custom_call_target="tpu_custom_call" | custom-call | flops 855638016 | bytes 2097152 | tf_op jit(solution)/shard_map/pallas_call | solution.py:183
  20.8 1.0 %collective-permute-done.4.q_ref = bf16[4,2,96,128]{3,2,1,0:T(8,128)(2,1)S(1)} collective-permute-done((bf16[4,2,96,128]{3,2,1,0:T(8,128)(2,1)S(1)}, bf16[4,2,96,128]{3,2,1,0:T(8,128)(2,1)S(1)}, u32[]{:S(2)}, u32[]{:S(2)}) %collective-permute-start.4) | collective-permute-done | bytes 196640 | tf_op jit(solution)/shard_map/ppermute | solution.py:457
  21.8 3.0 %shard_map.105 = (f32[768,128]{1,0:T(8,128)S(1)}, f32[16,128]{1,0:T(8,128)S(1)}) custom-call(s32[2,128]{1,0:T(2,128)S(1)} %broadcast_in_dim.15.scal, bf16[4,2,96,128]{3,2,1,0:T(8,128)(2,1)S(1)} %collective-permute-done.4.q_ref, bf16[1024,256]{1,0:T(8,128)(2,1)S(1)} %get-tuple-element.72.rest_0_, bf16[1024,256]{1,0:T(8,128)(2,1)S(1)} %get-tuple-element.71.rest_1_, ...), custom_call_target="tpu_custom_call" | custom-call | flops 855638016 | bytes 2097152 | tf_op jit(solution)/shard_map/pallas_call | solution.py:183
  24.8 1.4 %collective-permute-done.7.msg_ref = bf16[800,128]{1,0:T(8,128)(2,1)S(1)} collective-permute-done((bf16[800,128]{1,0:T(8,128)(2,1)S(1)}, bf16[800,128]{1,0:T(8,128)(2,1)S(1)}, u32[]{:S(2)}, u32[]{:S(2)}) %collective-permute-start.7) | collective-permute-done | bytes 204832 | tf_op jit(solution)/shard_map/ppermute | solution.py:457
  26.6 1.8 %collective-permute-start.8 = (bf16[416,128]{1,0:T(8,128)(2,1)S(1)}, bf16[416,128]{1,0:T(8,128)(2,1)S(1)}, u32[]{:S(2)}, u32[]{:S(2)}) collective-permute-start(bf16[416,128]{1,0:T(8,128)(2,1)S(1)} %get-tuple-element.54), channel_id=1, source_target_pairs={{0,8},{2,10},{4,12},{6,14},{8,0},{10,2},{12,4},{14,6},{16,24},{18,... | collective-permute-start | bytes 319496 | tf_op jit(solution)/shard_map/ppermute | solution.py:457
  28.7 2.7 %collective-permute-done.8.msg_ref = bf16[416,128]{1,0:T(8,128)(2,1)S(1)} collective-permute-done((bf16[416,128]{1,0:T(8,128)(2,1)S(1)}, bf16[416,128]{1,0:T(8,128)(2,1)S(1)}, u32[]{:S(2)}, u32[]{:S(2)}) %collective-permute-start.8) | collective-permute-done | bytes 106528 | tf_op jit(solution)/shard_map/ppermute | solution.py:457
  31.7 4.3 %collective-permute-start.10 = (bf16[416,128]{1,0:T(8,128)(2,1)S(1)}, bf16[416,128]{1,0:T(8,128)(2,1)S(1)}, u32[]{:S(2)}, u32[]{:S(2)}) collective-permute-start(bf16[416,128]{1,0:T(8,128)(2,1)S(1)} %get-tuple-element.59), channel_id=1, source_target_pairs={{0,16},{2,18},{4,20},{6,22},{8,24},{10,26},{12,28},{14,30},{16,0},... | collective-permute-start | bytes 319496 | tf_op jit(solution)/shard_map/ppermute | solution.py:457
  36.0 3.8 %collective-permute-done.10.msg_ref = bf16[416,128]{1,0:T(8,128)(2,1)S(1)} collective-permute-done((bf16[416,128]{1,0:T(8,128)(2,1)S(1)}, bf16[416,128]{1,0:T(8,128)(2,1)S(1)}, u32[]{:S(2)}, u32[]{:S(2)}) %collective-permute-start.10) | collective-permute-done | bytes 106528 | tf_op jit(solution)/shard_map/ppermute | solution.py:457
  40.7 4.2 %collective-permute-done.11 = bf16[2,2,96,128]{3,2,1,0:T(8,128)(2,1)S(1)} collective-permute-done((bf16[2,2,96,128]{3,2,1,0:T(8,128)(2,1)S(1)}, bf16[2,2,96,128]{3,2,1,0:T(8,128)(2,1)S(1)}, u32[]{:S(2)}, u32[]{:S(2)}) %collective-permute-start.11) | collective-permute-done | bytes 98336 | tf_op jit(solution)/shard_map/ppermute | solution.py:457
  44.9 1.2 %collective-permute-start.13 = (bf16[4,2,96,128]{3,2,1,0:T(8,128)(2,1)S(1)}, bf16[4,2,96,128]{3,2,1,0:T(8,128)(2,1)S(1)}, u32[]{:S(2)}, u32[]{:S(2)}) collective-permute-start(bf16[4,2,96,128]{3,2,1,0:T(8,128)(2,1)S(1)} %pad_maximum_fusion.refs_0_), channel_id=1, source_target_pairs={{0,4},{2,6},{4,0},{6,2},{8,12},{10,14},{12,8},{14,10},{16,20},{18,... | collective-permute-start | bytes 589832 | tf_op jit(solution)/shard_map/ppermute | solution.py:457
  46.1 0.9 %collective-permute-start.16 = (bf16[4,2,24,128]{3,2,1,0:T(8,128)(2,1)S(1)}, bf16[4,2,24,128]{3,2,1,0:T(8,128)(2,1)S(1)}, u32[]{:S(2)}, u32[]{:S(2)}) collective-permute-start(bf16[4,2,24,128]{3,2,1,0:T(8,128)(2,1)S(1)} %pad_maximum_fusion.3), channel_id=1, source_target_pairs={{0,4},{2,6},{4,0},{6,2},{8,12},{10,14},{12,8},{14,10},{16,20},{18,... | collective-permute-start | bytes 147464 | tf_op jit(solution)/shard_map/ppermute | solution.py:457
  47.0 4.2 %collective-permute-done.13.refs_1_ = bf16[4,2,96,128]{3,2,1,0:T(8,128)(2,1)S(1)} collective-permute-done((bf16[4,2,96,128]{3,2,1,0:T(8,128)(2,1)S(1)}, bf16[4,2,96,128]{3,2,1,0:T(8,128)(2,1)S(1)}, u32[]{:S(2)}, u32[]{:S(2)}) %collective-permute-start.13) | collective-permute-done | bytes 196640 | tf_op jit(solution)/shard_map/ppermute | solution.py:457
  51.7 1.0 %shard_map.109.refs_2_ = f32[96,512]{1,0:T(8,128)S(1)} custom-call(bf16[4,2,96,128]{3,2,1,0:T(8,128)(2,1)S(1)} %pad_maximum_fusion.refs_0_, bf16[4,2,96,128]{3,2,1,0:T(8,128)(2,1)S(1)} %collective-permute-done.13.refs_1_, bf16[4,2,96,128]{3,2,1,0:T(8,128)(2,1)S(1)} %collective-permute-done.15.refs_2_, bf16[4096,512]{1,0:T(8,128)(2,1)S(1)} %copy-done), custom_call_target="tpu_custom_call" | custom-call | flops 402653184 | bytes 4194304 | tf_op jit(solution)/shard_map/pallas_call | solution.py:321
  53.4 1.6 %collective-permute-start.17 = (bf16[48,512]{1,0:T(8,128)(2,1)S(1)}, bf16[48,512]{1,0:T(8,128)(2,1)S(1)}, u32[]{:S(2)}, u32[]{:S(2)}) collective-permute-start(bf16[48,512]{1,0:T(8,128)(2,1)S(1)} %get-tuple-element.65.rest_0_), channel_id=1, source_target_pairs={{0,1},{1,0},{2,3},{3,2},{4,5},{5,4},{6,7},{7,6},{8,9},{9,8},{10,11... | collective-permute-start | bytes 147464 | tf_op jit(solution)/shard_map/ppermute | solution.py:538
  55.0 2.3 %shard_map.111 = (bf16[1024,512]{1,0:T(8,128)(2,1)}, bf16[1024,512]{1,0:T(8,128)(2,1)}) custom-call(s32[2,128]{1,0:T(2,128)S(1)} %broadcast_in_dim.15.scal, bf16[1024,512]{1,0:T(8,128)(2,1)S(1)} %bitcast.33, bf16[1024,512]{1,0:T(8,128)(2,1)S(1)} %bitcast.30, bf16[8,2,24,128]{3,2,1,0:T(8,128)(2,1)S(1)} %pad_maximum_fusion.2.mine_ref, ...), custom_call_target="tpu_custom_call" | custom-call | bytes 4194304 | tf_op jit(solution)/shard_map/pallas_call | solution.py:432
  57.6 0.6 %fusion = bf16[1,48,512]{2,1,0:T(8,128)(2,1)} fusion(f32[48,512]{1,0:T(8,128)S(1)} %get-tuple-element.64, bf16[48,512]{1,0:T(8,128)(2,1)S(1)} %collective-permute-done.17), kind=kLoop, calls=%fused_computation.4 | loop fusion | flops 73728 | bytes 196608 | tf_op jit(solution)/shard_map/stack | solution.py:555
  (44 shorter events, 5.4 us)
Async XLA Ops:
  1.5 2.6 %collective-permute-start = (bf16[2,48,128]{2,1,0:T(8,128)(2,1)S(1)}, bf16[2,48,128]{2,1,0:T(8,128)(2,1)S(1)}, u32[]{:S(2)}, u32[]{:S(2)}) collective-permute-start(bf16[2,48,128]{2,1,0:T(8,128)(2,1)S(1)} %get-tuple-element.70), channel_id=1, source_target_pairs={{0,2},{2,0},{4,6},{6,4},{8,10},{10,8},{12,14},{14,12},{16,18},{18,... | collective-permute-start | bytes 73736 | tf_op jit(solution)/shard_map/ppermute | solution.py:457
  4.2 13.0 %collective-permute-start.5 = (bf16[1024,512]{1,0:T(8,128)(2,1)}, bf16[1024,512]{1,0:T(8,128)(2,1)S(1)}, u32[]{:S(2)}, u32[]{:S(2)}) collective-permute-start(bf16[1024,512]{1,0:T(8,128)(2,1)} %bitcast.31), channel_id=1, source_target_pairs={{0,2},{2,0},{4,6},{6,4},{8,10},{10,8},{12,14},{14,12},{16,18},{18,... | collective-permute-start | bytes 3145736 | tf_op jit(solution)/shard_map/ppermute | solution.py:457
  4.3 12.9 %collective-permute-start.6 = (bf16[1024,512]{1,0:T(8,128)(2,1)}, bf16[1024,512]{1,0:T(8,128)(2,1)S(1)}, u32[]{:S(2)}, u32[]{:S(2)}) collective-permute-start(bf16[1024,512]{1,0:T(8,128)(2,1)} %bitcast.28), channel_id=1, source_target_pairs={{0,2},{2,0},{4,6},{6,4},{8,10},{10,8},{12,14},{14,12},{16,18},{18,... | collective-permute-start | bytes 3145736 | tf_op jit(solution)/shard_map/ppermute | solution.py:457
  4.7 6.0 %collective-permute-start.1 = (bf16[1,2,96,128]{3,2,1,0:T(8,128)(2,1)S(1)}, bf16[1,2,96,128]{3,2,1,0:T(8,128)(2,1)S(1)}, u32[]{:S(2)}, u32[]{:S(2)}) collective-permute-start(bf16[1,2,96,128]{3,2,1,0:T(8,128)(2,1)S(1)} %maximum_bitcast_fusion), channel_id=1, source_target_pairs={{0,16},{2,18},{4,20},{6,22},{8,24},{10,26},{12,28},{14,30},{16,0},... | collective-permute-start | bytes 147464 | tf_op jit(solution)/shard_map/ppermute | solution.py:457
  8.4 2.4 %collective-permute-start.2 = (bf16[6,1024]{1,0:T(8,128)(2,1)S(1)}, bf16[6,1024]{1,0:T(8,128)(2,1)S(1)}, u32[]{:S(2)}, u32[]{:S(2)}) collective-permute-start(bf16[6,1024]{1,0:T(8,128)(2,1)S(1)} %pad_maximum_fusion.5.own_ref), channel_id=1, source_target_pairs={{0,2},{2,0},{4,6},{6,4},{8,10},{10,8},{12,14},{14,12},{16,18},{18,... | collective-permute-start | bytes 36872 | tf_op jit(solution)/shard_map/ppermute | solution.py:457
  10.7 4.9 %collective-permute-start.3 = (bf16[2,2,96,128]{3,2,1,0:T(8,128)(2,1)S(1)}, bf16[2,2,96,128]{3,2,1,0:T(8,128)(2,1)S(1)}, u32[]{:S(2)}, u32[]{:S(2)}) collective-permute-start(bf16[2,2,96,128]{3,2,1,0:T(8,128)(2,1)S(1)} %pad_maximum_fusion.1), channel_id=1, source_target_pairs={{0,8},{2,10},{4,12},{6,14},{8,0},{10,2},{12,4},{14,6},{16,24},{18,... | collective-permute-start | bytes 294920 | tf_op jit(solution)/shard_map/ppermute | solution.py:457
  15.6 6.2 %collective-permute-start.4 = (bf16[4,2,96,128]{3,2,1,0:T(8,128)(2,1)S(1)}, bf16[4,2,96,128]{3,2,1,0:T(8,128)(2,1)S(1)}, u32[]{:S(2)}, u32[]{:S(2)}) collective-permute-start(bf16[4,2,96,128]{3,2,1,0:T(8,128)(2,1)S(1)} %constant_dynamic-update-slice_fusion.q_ref), channel_id=1, source_target_pairs={{0,4},{2,6},{4,0},{6,2},{8,12},{10,14},{12,8},{14,10},{16,20},{18,... | collective-permute-start | bytes 589832 | tf_op jit(solution)/shard_map/ppermute | solution.py:457
  17.2 34.5 %copy-start = (bf16[4096,512]{1,0:T(8,128)(2,1)S(1)}, bf16[4096,512]{1,0:T(8,128)(2,1)}, u32[]{:S(2)}) copy-start(bf16[4096,512]{1,0:T(8,128)(2,1)} %refs_1_.1) | copy-start | bytes 12582916
  20.2 6.0 %collective-permute-start.7 = (bf16[800,128]{1,0:T(8,128)(2,1)S(1)}, bf16[800,128]{1,0:T(8,128)(2,1)S(1)}, u32[]{:S(2)}, u32[]{:S(2)}) collective-permute-start(bf16[800,128]{1,0:T(8,128)(2,1)S(1)} %shard_map.104.rest_5_), channel_id=1, source_target_pairs={{0,4},{2,6},{4,0},{6,2},{8,12},{10,14},{12,8},{14,10},{16,20},{18,... | collective-permute-start | bytes 614408 | tf_op jit(solution)/shard_map/ppermute | solution.py:457
  26.6 4.8 %collective-permute-start.8 = (bf16[416,128]{1,0:T(8,128)(2,1)S(1)}, bf16[416,128]{1,0:T(8,128)(2,1)S(1)}, u32[]{:S(2)}, u32[]{:S(2)}) collective-permute-start(bf16[416,128]{1,0:T(8,128)(2,1)S(1)} %get-tuple-element.54), channel_id=1, source_target_pairs={{0,8},{2,10},{4,12},{6,14},{8,0},{10,2},{12,4},{14,6},{16,24},{18,... | collective-permute-start | bytes 319496 | tf_op jit(solution)/shard_map/ppermute | solution.py:457
  28.4 7.6 %collective-permute-start.9 = (bf16[1,2,24,128]{3,2,1,0:T(8,128)(2,1)S(1)}, bf16[1,2,24,128]{3,2,1,0:T(8,128)(2,1)S(1)}, u32[]{:S(2)}, u32[]{:S(2)}) collective-permute-start(bf16[1,2,24,128]{3,2,1,0:T(8,128)(2,1)S(1)} %bitcast.36), channel_id=1, source_target_pairs={{0,8},{2,10},{4,12},{6,14},{8,0},{10,2},{12,4},{14,6},{16,24},{18,... | collective-permute-start | bytes 36872 | tf_op jit(solution)/shard_map/ppermute | solution.py:457
  31.7 8.2 %collective-permute-start.10 = (bf16[416,128]{1,0:T(8,128)(2,1)S(1)}, bf16[416,128]{1,0:T(8,128)(2,1)S(1)}, u32[]{:S(2)}, u32[]{:S(2)}) collective-permute-start(bf16[416,128]{1,0:T(8,128)(2,1)S(1)} %get-tuple-element.59), channel_id=1, source_target_pairs={{0,16},{2,18},{4,20},{6,22},{8,24},{10,26},{12,28},{14,30},{16,0},... | collective-permute-start | bytes 319496 | tf_op jit(solution)/shard_map/ppermute | solution.py:457
  35.9 4.7 %collective-permute-start.12 = (bf16[2,2,24,128]{3,2,1,0:T(8,128)(2,1)S(1)}, bf16[2,2,24,128]{3,2,1,0:T(8,128)(2,1)S(1)}, u32[]{:S(2)}, u32[]{:S(2)}) collective-permute-start(bf16[2,2,24,128]{3,2,1,0:T(8,128)(2,1)S(1)} %pad_maximum_fusion.4), channel_id=1, source_target_pairs={{0,16},{2,18},{4,20},{6,22},{8,24},{10,26},{12,28},{14,30},{16,0},... | collective-permute-start | bytes 73736 | tf_op jit(solution)/shard_map/ppermute | solution.py:457
  40.2 4.7 %collective-permute-start.11 = (bf16[2,2,96,128]{3,2,1,0:T(8,128)(2,1)S(1)}, bf16[2,2,96,128]{3,2,1,0:T(8,128)(2,1)S(1)}, u32[]{:S(2)}, u32[]{:S(2)}) collective-permute-start(bf16[2,2,96,128]{3,2,1,0:T(8,128)(2,1)S(1)} %bitcast.34), channel_id=1, source_target_pairs={{0,8},{2,10},{4,12},{6,14},{8,0},{10,2},{12,4},{14,6},{16,24},{18,... | collective-permute-start | bytes 294920 | tf_op jit(solution)/shard_map/ppermute | solution.py:457
  44.9 6.3 %collective-permute-start.13 = (bf16[4,2,96,128]{3,2,1,0:T(8,128)(2,1)S(1)}, bf16[4,2,96,128]{3,2,1,0:T(8,128)(2,1)S(1)}, u32[]{:S(2)}, u32[]{:S(2)}) collective-permute-start(bf16[4,2,96,128]{3,2,1,0:T(8,128)(2,1)S(1)} %pad_maximum_fusion.refs_0_), channel_id=1, source_target_pairs={{0,4},{2,6},{4,0},{6,2},{8,12},{10,14},{12,8},{14,10},{16,20},{18,... | collective-permute-start | bytes 589832 | tf_op jit(solution)/shard_map/ppermute | solution.py:457
  46.1 5.6 %collective-permute-start.15 = (bf16[4,2,96,128]{3,2,1,0:T(8,128)(2,1)S(1)}, bf16[4,2,96,128]{3,2,1,0:T(8,128)(2,1)S(1)}, u32[]{:S(2)}, u32[]{:S(2)}) collective-permute-start(bf16[4,2,96,128]{3,2,1,0:T(8,128)(2,1)S(1)} %pad_maximum_fusion.refs_0_), channel_id=1, source_target_pairs={{0,2},{2,0},{4,6},{6,4},{8,10},{10,8},{12,14},{14,12},{16,18},{18,... | collective-permute-start | bytes 589832 | tf_op jit(solution)/shard_map/ppermute | solution.py:457
  46.1 5.6 %collective-permute-start.16 = (bf16[4,2,24,128]{3,2,1,0:T(8,128)(2,1)S(1)}, bf16[4,2,24,128]{3,2,1,0:T(8,128)(2,1)S(1)}, u32[]{:S(2)}, u32[]{:S(2)}) collective-permute-start(bf16[4,2,24,128]{3,2,1,0:T(8,128)(2,1)S(1)} %pad_maximum_fusion.3), channel_id=1, source_target_pairs={{0,4},{2,6},{4,0},{6,2},{8,12},{10,14},{12,8},{14,10},{16,20},{18,... | collective-permute-start | bytes 147464 | tf_op jit(solution)/shard_map/ppermute | solution.py:457
  51.1 1.7 %collective-permute-start.14 = (bf16[4,2,96,128]{3,2,1,0:T(8,128)(2,1)S(1)}, bf16[4,2,96,128]{3,2,1,0:T(8,128)(2,1)S(1)}, u32[]{:S(2)}, u32[]{:S(2)}) collective-permute-start(bf16[4,2,96,128]{3,2,1,0:T(8,128)(2,1)S(1)} %collective-permute-done.13.refs_1_), channel_id=1, source_target_pairs={{0,2},{2,0},{4,6},{6,4},{8,10},{10,8},{12,14},{14,12},{16,18},{18,... | collective-permute-start | bytes 589832 | tf_op jit(solution)/shard_map/ppermute | solution.py:457
  51.7 3.3 %copy-start.1 = (bf16[1,1024,512]{2,1,0:T(8,128)(2,1)S(1)}, bf16[1,1024,512]{2,1,0:T(8,128)(2,1)}, u32[]{:S(2)}) copy-start(bf16[1,1024,512]{2,1,0:T(8,128)(2,1)} %param.12) | copy-start | bytes 3145732
  51.7 3.3 %copy-start.2 = (bf16[1,1024,512]{2,1,0:T(8,128)(2,1)S(1)}, bf16[1,1024,512]{2,1,0:T(8,128)(2,1)}, u32[]{:S(2)}) copy-start(bf16[1,1024,512]{2,1,0:T(8,128)(2,1)} %param.11) | copy-start | bytes 3145732
  52.8 2.2 %collective-permute-start.18 = (bf16[8,2,24,128]{3,2,1,0:T(8,128)(2,1)S(1)}, bf16[8,2,24,128]{3,2,1,0:T(8,128)(2,1)S(1)}, u32[]{:S(2)}, u32[]{:S(2)}) collective-permute-start(bf16[8,2,24,128]{3,2,1,0:T(8,128)(2,1)S(1)} %pad_maximum_fusion.2.mine_ref), channel_id=1, source_target_pairs={{0,2},{2,0},{4,6},{6,4},{8,10},{10,8},{12,14},{14,12},{16,18},{18,... | collective-permute-start | bytes 294920 | tf_op jit(solution)/shard_map/ppermute | solution.py:457
  53.4 4.2 %collective-permute-start.17 = (bf16[48,512]{1,0:T(8,128)(2,1)S(1)}, bf16[48,512]{1,0:T(8,128)(2,1)S(1)}, u32[]{:S(2)}, u32[]{:S(2)}) collective-permute-start(bf16[48,512]{1,0:T(8,128)(2,1)S(1)} %get-tuple-element.65.rest_0_), channel_id=1, source_target_pairs={{0,1},{1,0},{2,3},{3,2},{4,5},{5,4},{6,7},{7,6},{8,9},{9,8},{10,11... | collective-permute-start | bytes 147464 | tf_op jit(solution)/shard_map/ppermute | solution.py:538

commit v7 on v6

--- a/solution.py
+++ b/solution.py
@@ -335,15 +335,17 @@
     )(*sources, weight, *partial)
 
 
-def drafts_kernel(split, own_ref, *rest):
-    others, (draft_ref, unit_ref, rows_ref) = rest[:-3], rest[-3:]
-    rows, width = own_ref.shape
+def drafts_kernel(split, *refs):
+    sources, (draft_ref, unit_ref, rows_ref) = refs[:-3], refs[-3:]
+    rows, half = sources[0].shape
+    width = 2 * half
     heads = draft_ref.shape[0]
     core = lax.rem(lax.axis_index("seq"), split)
     rows_ref[...] = jnp.zeros_like(rows_ref)
-    for n, ref in enumerate((own_ref, *others)):
-        rows_ref[n * rows : (n + 1) * rows, :] = ref[...].astype(f32)
-    unit_rows = rows * (1 + len(others))
+    for n in range(split):
+        rows_ref[n * rows : (n + 1) * rows, :half] = sources[2 * n][...].astype(f32)
+        rows_ref[n * rows : (n + 1) * rows, half:] = sources[2 * n + 1][...].astype(f32)
+    unit_rows = rows * split
     for h in range(heads):
         for n in range(2):
             lanes = pl.ds(pl.multiple_of(n * (width // 2) + (core * heads + h) * HD, HD), HD)
@@ -361,18 +363,18 @@
         unit_ref[h] = pad_rows(chip_rows, unit_ref.shape[1]).astype(bf16)
 
 
-def chip_drafts(split, heads, own, others):
-    rows, width = own.shape
+def chip_drafts(split, heads, sources):
+    rows, half = sources[0].shape
     return pl.pallas_call(
         functools.partial(drafts_kernel, split),
-        in_specs=[pl.BlockSpec(memory_space=pltpu.VMEM)] * (1 + len(others)),
+        in_specs=[pl.BlockSpec(memory_space=pltpu.VMEM)] * len(sources),
         out_shape=(
             jax.ShapeDtypeStruct((heads, 2 * LANES, HD), bf16),
             jax.ShapeDtypeStruct((heads, round_up(2 * rows * split, 8), HD), bf16),
         ),
-        scratch_shapes=[pltpu.VMEM((LANES, width), f32)],
+        scratch_shapes=[pltpu.VMEM((LANES, 2 * half), f32)],
         compiler_params=pltpu.CompilerParams(vmem_limit_bytes=VMEM_BYTES),
-    )(own, *others)
+    )(*sources)
 
 
 def append_kernel(rel, split, unit_rows, scal, ck_ref, cv_ref, mine_ref, other_ref, *rest):
@@ -460,7 +462,7 @@
 
     q4 = dq.reshape(local_rows, heads_kv, GROUP, LANES).transpose(1, 0, 2, 3)
     q4 = q4.reshape(heads_kv, local_rows * GROUP, LANES)
-    drafts_own = jnp.concatenate([dk, dv], axis=1)
+    drafts_own = [dk, dv]
     caches, drafts_other = [ck, cv], []
     q = q4
     if split == 2:
@@ -472,7 +474,7 @@
     )
     if split == 2:
         q, drafts_own, *late = lax.optimization_barrier((q, drafts_own, ck, cv))
-        drafts_other = [swap(drafts_own, 0)]
+        drafts_other = [swap(d, 0) for d in drafts_own]
         caches += [swap(c, 0) for c in late]
 
     rel, near = [0], bits[-1]
@@ -487,7 +489,7 @@
                 lax.dynamic_slice_in_dim(c, core * heads * HD, heads * HD, 1) for c in own
             ]
         rel = rel + [r | (1 << bit) // split for r in rel]
-    drafts, chip_rows = chip_drafts(split, heads, drafts_own, drafts_other)
+    drafts, chip_rows = chip_drafts(split, heads, [*drafts_own, *drafts_other])
     rel_far = [r | (1 << near) // split for r in rel]
     q_far = swap(q, near)
 

time: 58.5 us -> 57.8 us (0.988)
  waiting for transfers between devices: 22.3 us -> 20.9 us
  local copies, waits for them, and re-layouts: 2.24 us -> 3.63 us
  other arithmetic: 1.48 us -> 0.76 us
    ppermute x18 -> x19, waiting for transfers between devices: 22.1 us -> 20.7 us  [swap(): return lax.ppermute(x, 'seq', [(i, i ^ 1 << bit) for i in range(n_seq)])]
    unnamed x7 -> x11, local copies, waits for them, and re-layouts: 0.02 us -> 1.42 us
    concatenate x1 -> x0, other arithmetic: 0.72 us -> none  [one_request(): drafts_own = jnp.concatenate([dk, dv], axis=1)]
    ppermute x18 -> x19, starting transfers between devices: 17.5 us -> 17.6 us  [swap(): return lax.ppermute(x, 'seq', [(i, i ^ 1 << bit) for i in range(n_seq)])]
  transfers between devices with their start and end apart: 19 -> 20, of which waited for: 11 -> 11; matrix products, arithmetic and copies ran while one was open for 4% -> 2% of each run, Pallas kernels for 18% -> 18%
where the time goes in v7:
time: 57.8 us; the launch traced here: 57.5 us
  waiting for transfers between devices  20.9 us (36%)
  starting transfers between devices  19.2 us (33%)
  Pallas kernels  11 us (19%)
  local copies, waits for them, and re-layouts  3.63 us (6%)
  between operations  2.12 us (4%)
  other arithmetic  0.76 us (1%)
    ppermute x19, waiting for transfers between devices, swap(): return lax.ppermute(x, 'seq', [(i, i ^ 1 << bit) for i in range(n_seq)])  20.7 us
    ppermute x19, starting transfers between devices, swap(): return lax.ppermute(x, 'seq', [(i, i ^ 1 << bit) for i in range(n_seq)])  17.6 us
    pallas_call x2, Pallas kernels, attend(): pl.pallas_call(functools.partial(attend_kernel, rel, unit_rows, split, as...  5.95 us
    pallas_call x1, Pallas kernels, append(): pl.pallas_call(functools.partial(append_kernel, rel, split, unit_rows), g...  2.35 us
    ppermute x1, starting transfers between devices, one_request(): projected = keep + lax.ppermute(send, 'head', [(0, 1), (1, 0)]).astype(f32)  1.6 us
    pallas_call x2, Pallas kernels, project(): pl.pallas_call(functools.partial(project_kernel, rel, split, n_head, part...  1.58 us
    unnamed x11, local copies, waits for them, and re-layouts  1.42 us
    dynamic_slice x1, local copies, waits for them, and re-layouts, one_request(): lax.dynamic_slice_in_dim(c, core * heads * HD, heads * HD, 1)  1.28 us
  transfers between devices with their start and end apart: 20, of which 11 were waited for; matrix products, arithmetic and copies ran while one was open for 2% of the time, Pallas kernels for 18%

profile of v7, /device:TPU:0, one launch (start us, length us, event | category | flops | bytes accessed | tf_op | source)
XLA Modules:
  0.0 57.5 jit_solution(954225822554842267)
XLA Ops:
  0.6 0.8 %copy_bitcast_fusion.1 = bf16[4,48,128]{2,1,0:T(8,128)(2,1)S(1)} fusion(bf16[1,6,32,128]{3,1,2,0:T(8,128)(2,1)} %bitcast.42), kind=kLoop, calls=%fused_computation.8 | loop fusion | bytes 98304 | tf_op jit(solution)/shard_map/reshape | solution.py:464
  4.0 3.7 %collective-permute-start.1 = (bf16[1,2,96,128]{3,2,1,0:T(8,128)(2,1)S(1)}, bf16[1,2,96,128]{3,2,1,0:T(8,128)(2,1)S(1)}, u32[]{:S(2)}, u32[]{:S(2)}) collective-permute-start(bf16[1,2,96,128]{3,2,1,0:T(8,128)(2,1)S(1)} %maximum_bitcast_fusion), channel_id=1, source_target_pairs={{0,16},{2,18},{4,20},{6,22},{8,24},{10,26},{12,28},{14,30},{16,0},... | collective-permute-start | bytes 147464 | tf_op jit(solution)/shard_map/ppermute | solution.py:459
  8.2 1.8 %collective-permute-done.1 = bf16[1,2,96,128]{3,2,1,0:T(8,128)(2,1)S(1)} collective-permute-done((bf16[1,2,96,128]{3,2,1,0:T(8,128)(2,1)S(1)}, bf16[1,2,96,128]{3,2,1,0:T(8,128)(2,1)S(1)}, u32[]{:S(2)}, u32[]{:S(2)}) %collective-permute-start.1) | collective-permute-done | bytes 49184 | tf_op jit(solution)/shard_map/ppermute | solution.py:459
  10.0 1.9 %collective-permute-start.4 = (bf16[2,2,96,128]{3,2,1,0:T(8,128)(2,1)S(1)}, bf16[2,2,96,128]{3,2,1,0:T(8,128)(2,1)S(1)}, u32[]{:S(2)}, u32[]{:S(2)}) collective-permute-start(bf16[2,2,96,128]{3,2,1,0:T(8,128)(2,1)S(1)} %pad_maximum_fusion.1), channel_id=1, source_target_pairs={{0,8},{2,10},{4,12},{6,14},{8,0},{10,2},{12,4},{14,6},{16,24},{18,... | collective-permute-start | bytes 294920 | tf_op jit(solution)/shard_map/ppermute | solution.py:459
  11.9 0.7 %copy-done.3 = bf16[1,6,512]{2,1,0:T(8,128)(2,1)S(1)} copy-done((bf16[1,6,512]{2,1,0:T(8,128)(2,1)S(1)}, bf16[1,6,512]{2,1,0:T(8,128)(2,1)}, u32[]{:S(2)}) %copy-start.3) | copy-done | bytes 6168
  12.6 0.7 %copy-done.4 = bf16[1,6,512]{2,1,0:T(8,128)(2,1)S(1)} copy-done((bf16[1,6,512]{2,1,0:T(8,128)(2,1)S(1)}, bf16[1,6,512]{2,1,0:T(8,128)(2,1)}, u32[]{:S(2)}) %copy-start.4) | copy-done | bytes 6168
  13.4 1.3 %constant_dynamic-slice_fusion = (bf16[1024,256]{1,0:T(8,128)(2,1)S(1)}, bf16[1024,256]{1,0:T(8,128)(2,1)S(1)}) fusion(bf16[1024,512]{1,0:T(8,128)(2,1)} %bitcast.29, s32[]{:T(128)S(6)} %select_n.20, bf16[1024,512]{1,0:T(8,128)(2,1)} %bitcast.32), kind=kLoop, calls=%fused_computation.12 | loop fusion | bytes 2097156 | tf_op jit(solution)/shard_map/dynamic_slice | solution.py:489
  14.9 1.6 %collective-permute-start.5 = (bf16[4,2,96,128]{3,2,1,0:T(8,128)(2,1)S(1)}, bf16[4,2,96,128]{3,2,1,0:T(8,128)(2,1)S(1)}, u32[]{:S(2)}, u32[]{:S(2)}) collective-permute-start(bf16[4,2,96,128]{3,2,1,0:T(8,128)(2,1)S(1)} %constant_dynamic-update-slice_fusion.q_ref), channel_id=1, source_target_pairs={{0,4},{2,6},{4,0},{6,2},{8,12},{10,14},{12,8},{14,10},{16,20},{18,... | collective-permute-start | bytes 589832 | tf_op jit(solution)/shard_map/ppermute | solution.py:459
  16.5 3.0 %shard_map.104.rest_5_ = bf16[800,128]{1,0:T(8,128)(2,1)S(1)} custom-call(s32[2,128]{1,0:T(2,128)S(1)} %broadcast_in_dim.15.scal, bf16[4,2,96,128]{3,2,1,0:T(8,128)(2,1)S(1)} %constant_dynamic-update-slice_fusion.q_ref, bf16[1024,256]{1,0:T(8,128)(2,1)S(1)} %get-tuple-element.78.rest_0_, bf16[1024,256]{1,0:T(8,128)(2,1)S(1)} %get-tuple-element.77.rest_1_, ...), custom_call_target="tpu_custom_call" | custom-call | flops 855638016 | bytes 2097152 | tf_op jit(solution)/shard_map/pallas_call | solution.py:183
  20.0 1.3 %collective-permute-done.5.q_ref = bf16[4,2,96,128]{3,2,1,0:T(8,128)(2,1)S(1)} collective-permute-done((bf16[4,2,96,128]{3,2,1,0:T(8,128)(2,1)S(1)}, bf16[4,2,96,128]{3,2,1,0:T(8,128)(2,1)S(1)}, u32[]{:S(2)}, u32[]{:S(2)}) %collective-permute-start.5) | collective-permute-done | bytes 196640 | tf_op jit(solution)/shard_map/ppermute | solution.py:459
  21.4 3.0 %shard_map.105 = (f32[768,128]{1,0:T(8,128)S(1)}, f32[16,128]{1,0:T(8,128)S(1)}) custom-call(s32[2,128]{1,0:T(2,128)S(1)} %broadcast_in_dim.15.scal, bf16[4,2,96,128]{3,2,1,0:T(8,128)(2,1)S(1)} %collective-permute-done.5.q_ref, bf16[1024,256]{1,0:T(8,128)(2,1)S(1)} %get-tuple-element.78.rest_0_, bf16[1024,256]{1,0:T(8,128)(2,1)S(1)} %get-tuple-element.77.rest_1_, ...), custom_call_target="tpu_custom_call" | custom-call | flops 855638016 | bytes 2097152 | tf_op jit(solution)/shard_map/pallas_call | solution.py:183
  24.3 1.5 %collective-permute-done.8.msg_ref = bf16[800,128]{1,0:T(8,128)(2,1)S(1)} collective-permute-done((bf16[800,128]{1,0:T(8,128)(2,1)S(1)}, bf16[800,128]{1,0:T(8,128)(2,1)S(1)}, u32[]{:S(2)}, u32[]{:S(2)}) %collective-permute-start.8) | collective-permute-done | bytes 204832 | tf_op jit(solution)/shard_map/ppermute | solution.py:459
  26.2 1.5 %collective-permute-start.9 = (bf16[416,128]{1,0:T(8,128)(2,1)S(1)}, bf16[416,128]{1,0:T(8,128)(2,1)S(1)}, u32[]{:S(2)}, u32[]{:S(2)}) collective-permute-start(bf16[416,128]{1,0:T(8,128)(2,1)S(1)} %get-tuple-element.60), channel_id=1, source_target_pairs={{0,8},{2,10},{4,12},{6,14},{8,0},{10,2},{12,4},{14,6},{16,24},{18,... | collective-permute-start | bytes 319496 | tf_op jit(solution)/shard_map/ppermute | solution.py:459
  28.3 2.7 %collective-permute-done.9.msg_ref = bf16[416,128]{1,0:T(8,128)(2,1)S(1)} collective-permute-done((bf16[416,128]{1,0:T(8,128)(2,1)S(1)}, bf16[416,128]{1,0:T(8,128)(2,1)S(1)}, u32[]{:S(2)}, u32[]{:S(2)}) %collective-permute-start.9) | collective-permute-done | bytes 106528 | tf_op jit(solution)/shard_map/ppermute | solution.py:459
  31.3 3.9 %collective-permute-start.11 = (bf16[416,128]{1,0:T(8,128)(2,1)S(1)}, bf16[416,128]{1,0:T(8,128)(2,1)S(1)}, u32[]{:S(2)}, u32[]{:S(2)}) collective-permute-start(bf16[416,128]{1,0:T(8,128)(2,1)S(1)} %get-tuple-element.65), channel_id=1, source_target_pairs={{0,16},{2,18},{4,20},{6,22},{8,24},{10,26},{12,28},{14,30},{16,0},... | collective-permute-start | bytes 319496 | tf_op jit(solution)/shard_map/ppermute | solution.py:459
  35.3 3.8 %collective-permute-done.11.msg_ref = bf16[416,128]{1,0:T(8,128)(2,1)S(1)} collective-permute-done((bf16[416,128]{1,0:T(8,128)(2,1)S(1)}, bf16[416,128]{1,0:T(8,128)(2,1)S(1)}, u32[]{:S(2)}, u32[]{:S(2)}) %collective-permute-start.11) | collective-permute-done | bytes 106528 | tf_op jit(solution)/shard_map/ppermute | solution.py:459
  40.0 4.2 %collective-permute-done.12 = bf16[2,2,96,128]{3,2,1,0:T(8,128)(2,1)S(1)} collective-permute-done((bf16[2,2,96,128]{3,2,1,0:T(8,128)(2,1)S(1)}, bf16[2,2,96,128]{3,2,1,0:T(8,128)(2,1)S(1)}, u32[]{:S(2)}, u32[]{:S(2)}) %collective-permute-start.12) | collective-permute-done | bytes 98336 | tf_op jit(solution)/shard_map/ppermute | solution.py:459
  44.2 1.2 %collective-permute-start.14 = (bf16[4,2,96,128]{3,2,1,0:T(8,128)(2,1)S(1)}, bf16[4,2,96,128]{3,2,1,0:T(8,128)(2,1)S(1)}, u32[]{:S(2)}, u32[]{:S(2)}) collective-permute-start(bf16[4,2,96,128]{3,2,1,0:T(8,128)(2,1)S(1)} %pad_maximum_fusion.refs_0_), channel_id=1, source_target_pairs={{0,4},{2,6},{4,0},{6,2},{8,12},{10,14},{12,8},{14,10},{16,20},{18,... | collective-permute-start | bytes 589832 | tf_op jit(solution)/shard_map/ppermute | solution.py:459
  45.4 0.9 %collective-permute-start.17 = (bf16[4,2,24,128]{3,2,1,0:T(8,128)(2,1)S(1)}, bf16[4,2,24,128]{3,2,1,0:T(8,128)(2,1)S(1)}, u32[]{:S(2)}, u32[]{:S(2)}) collective-permute-start(bf16[4,2,24,128]{3,2,1,0:T(8,128)(2,1)S(1)} %pad_maximum_fusion.3), channel_id=1, source_target_pairs={{0,4},{2,6},{4,0},{6,2},{8,12},{10,14},{12,8},{14,10},{16,20},{18,... | collective-permute-start | bytes 147464 | tf_op jit(solution)/shard_map/ppermute | solution.py:459
  46.3 4.2 %collective-permute-done.14.refs_1_ = bf16[4,2,96,128]{3,2,1,0:T(8,128)(2,1)S(1)} collective-permute-done((bf16[4,2,96,128]{3,2,1,0:T(8,128)(2,1)S(1)}, bf16[4,2,96,128]{3,2,1,0:T(8,128)(2,1)S(1)}, u32[]{:S(2)}, u32[]{:S(2)}) %collective-permute-start.14) | collective-permute-done | bytes 196640 | tf_op jit(solution)/shard_map/ppermute | solution.py:459
  51.0 1.0 %shard_map.109.refs_2_ = f32[96,512]{1,0:T(8,128)S(1)} custom-call(bf16[4,2,96,128]{3,2,1,0:T(8,128)(2,1)S(1)} %pad_maximum_fusion.refs_0_, bf16[4,2,96,128]{3,2,1,0:T(8,128)(2,1)S(1)} %collective-permute-done.14.refs_1_, bf16[4,2,96,128]{3,2,1,0:T(8,128)(2,1)S(1)} %collective-permute-done.16.refs_2_, bf16[4096,512]{1,0:T(8,128)(2,1)S(1)} %copy-done), custom_call_target="tpu_custom_call" | custom-call | flops 402653184 | bytes 4194304 | tf_op jit(solution)/shard_map/pallas_call | solution.py:321
  52.7 1.6 %collective-permute-start.18 = (bf16[48,512]{1,0:T(8,128)(2,1)S(1)}, bf16[48,512]{1,0:T(8,128)(2,1)S(1)}, u32[]{:S(2)}, u32[]{:S(2)}) collective-permute-start(bf16[48,512]{1,0:T(8,128)(2,1)S(1)} %get-tuple-element.71.rest_0_), channel_id=1, source_target_pairs={{0,1},{1,0},{2,3},{3,2},{4,5},{5,4},{6,7},{7,6},{8,9},{9,8},{10,11... | collective-permute-start | bytes 147464 | tf_op jit(solution)/shard_map/ppermute | solution.py:540
  54.3 2.3 %shard_map.111 = (bf16[1024,512]{1,0:T(8,128)(2,1)}, bf16[1024,512]{1,0:T(8,128)(2,1)}) custom-call(s32[2,128]{1,0:T(2,128)S(1)} %broadcast_in_dim.15.scal, bf16[1024,512]{1,0:T(8,128)(2,1)S(1)} %bitcast.33, bf16[1024,512]{1,0:T(8,128)(2,1)S(1)} %bitcast.30, bf16[8,2,24,128]{3,2,1,0:T(8,128)(2,1)S(1)} %pad_maximum_fusion.2.mine_ref, ...), custom_call_target="tpu_custom_call" | custom-call | bytes 4194304 | tf_op jit(solution)/shard_map/pallas_call | solution.py:434
  56.9 0.6 %fusion = bf16[1,48,512]{2,1,0:T(8,128)(2,1)} fusion(f32[48,512]{1,0:T(8,128)S(1)} %get-tuple-element.70, bf16[48,512]{1,0:T(8,128)(2,1)S(1)} %collective-permute-done.18), kind=kLoop, calls=%fused_computation.4 | loop fusion | flops 73728 | bytes 196608 | tf_op jit(solution)/shard_map/stack | solution.py:557
  (49 shorter events, 6.3 us)
Async XLA Ops:
  1.5 1.9 %collective-permute-start = (bf16[2,48,128]{2,1,0:T(8,128)(2,1)S(1)}, bf16[2,48,128]{2,1,0:T(8,128)(2,1)S(1)}, u32[]{:S(2)}, u32[]{:S(2)}) collective-permute-start(bf16[2,48,128]{2,1,0:T(8,128)(2,1)S(1)} %get-tuple-element.76), channel_id=1, source_target_pairs={{0,2},{2,0},{4,6},{6,4},{8,10},{10,8},{12,14},{14,12},{16,18},{18,... | collective-permute-start | bytes 73736 | tf_op jit(solution)/shard_map/ppermute | solution.py:459
  3.5 13.0 %collective-permute-start.6 = (bf16[1024,512]{1,0:T(8,128)(2,1)}, bf16[1024,512]{1,0:T(8,128)(2,1)S(1)}, u32[]{:S(2)}, u32[]{:S(2)}) collective-permute-start(bf16[1024,512]{1,0:T(8,128)(2,1)} %bitcast.31), channel_id=1, source_target_pairs={{0,2},{2,0},{4,6},{6,4},{8,10},{10,8},{12,14},{14,12},{16,18},{18,... | collective-permute-start | bytes 3145736 | tf_op jit(solution)/shard_map/ppermute | solution.py:459
  3.5 13.0 %collective-permute-start.7 = (bf16[1024,512]{1,0:T(8,128)(2,1)}, bf16[1024,512]{1,0:T(8,128)(2,1)S(1)}, u32[]{:S(2)}, u32[]{:S(2)}) collective-permute-start(bf16[1024,512]{1,0:T(8,128)(2,1)} %bitcast.28), channel_id=1, source_target_pairs={{0,2},{2,0},{4,6},{6,4},{8,10},{10,8},{12,14},{14,12},{16,18},{18,... | collective-permute-start | bytes 3145736 | tf_op jit(solution)/shard_map/ppermute | solution.py:459
  4.0 6.0 %collective-permute-start.1 = (bf16[1,2,96,128]{3,2,1,0:T(8,128)(2,1)S(1)}, bf16[1,2,96,128]{3,2,1,0:T(8,128)(2,1)S(1)}, u32[]{:S(2)}, u32[]{:S(2)}) collective-permute-start(bf16[1,2,96,128]{3,2,1,0:T(8,128)(2,1)S(1)} %maximum_bitcast_fusion), channel_id=1, source_target_pairs={{0,16},{2,18},{4,20},{6,22},{8,24},{10,26},{12,28},{14,30},{16,0},... | collective-permute-start | bytes 147464 | tf_op jit(solution)/shard_map/ppermute | solution.py:459
  7.7 2.4 %collective-permute-start.2 = (bf16[6,512]{1,0:T(8,128)(2,1)}, bf16[6,512]{1,0:T(8,128)(2,1)S(1)}, u32[]{:S(2)}, u32[]{:S(2)}) collective-permute-start(bf16[6,512]{1,0:T(8,128)(2,1)} %bitcast.38), channel_id=1, source_target_pairs={{0,2},{2,0},{4,6},{6,4},{8,10},{10,8},{12,14},{14,12},{16,18},{18,... | collective-permute-start | bytes 18440 | tf_op jit(solution)/shard_map/ppermute | solution.py:459
  7.8 2.2 %collective-permute-start.3 = (bf16[6,512]{1,0:T(8,128)(2,1)}, bf16[6,512]{1,0:T(8,128)(2,1)S(1)}, u32[]{:S(2)}, u32[]{:S(2)}) collective-permute-start(bf16[6,512]{1,0:T(8,128)(2,1)} %bitcast.40), channel_id=1, source_target_pairs={{0,2},{2,0},{4,6},{6,4},{8,10},{10,8},{12,14},{14,12},{16,18},{18,... | collective-permute-start | bytes 18440 | tf_op jit(solution)/shard_map/ppermute | solution.py:459
  10.0 4.9 %collective-permute-start.4 = (bf16[2,2,96,128]{3,2,1,0:T(8,128)(2,1)S(1)}, bf16[2,2,96,128]{3,2,1,0:T(8,128)(2,1)S(1)}, u32[]{:S(2)}, u32[]{:S(2)}) collective-permute-start(bf16[2,2,96,128]{3,2,1,0:T(8,128)(2,1)S(1)} %pad_maximum_fusion.1), channel_id=1, source_target_pairs={{0,8},{2,10},{4,12},{6,14},{8,0},{10,2},{12,4},{14,6},{16,24},{18,... | collective-permute-start | bytes 294920 | tf_op jit(solution)/shard_map/ppermute | solution.py:459
  11.9 0.7 %copy-start.3 = (bf16[1,6,512]{2,1,0:T(8,128)(2,1)S(1)}, bf16[1,6,512]{2,1,0:T(8,128)(2,1)}, u32[]{:S(2)}) copy-start(bf16[1,6,512]{2,1,0:T(8,128)(2,1)} %param.9) | copy-start | bytes 18436
  14.9 6.4 %collective-permute-start.5 = (bf16[4,2,96,128]{3,2,1,0:T(8,128)(2,1)S(1)}, bf16[4,2,96,128]{3,2,1,0:T(8,128)(2,1)S(1)}, u32[]{:S(2)}, u32[]{:S(2)}) collective-permute-start(bf16[4,2,96,128]{3,2,1,0:T(8,128)(2,1)S(1)} %constant_dynamic-update-slice_fusion.q_ref), channel_id=1, source_target_pairs={{0,4},{2,6},{4,0},{6,2},{8,12},{10,14},{12,8},{14,10},{16,20},{18,... | collective-permute-start | bytes 589832 | tf_op jit(solution)/shard_map/ppermute | solution.py:459
  16.5 34.5 %copy-start = (bf16[4096,512]{1,0:T(8,128)(2,1)S(1)}, bf16[4096,512]{1,0:T(8,128)(2,1)}, u32[]{:S(2)}) copy-start(bf16[4096,512]{1,0:T(8,128)(2,1)} %refs_1_.1) | copy-start | bytes 12582916
  19.5 6.3 %collective-permute-start.8 = (bf16[800,128]{1,0:T(8,128)(2,1)S(1)}, bf16[800,128]{1,0:T(8,128)(2,1)S(1)}, u32[]{:S(2)}, u32[]{:S(2)}) collective-permute-start(bf16[800,128]{1,0:T(8,128)(2,1)S(1)} %shard_map.104.rest_5_), channel_id=1, source_target_pairs={{0,4},{2,6},{4,0},{6,2},{8,12},{10,14},{12,8},{14,10},{16,20},{18,... | collective-permute-start | bytes 614408 | tf_op jit(solution)/shard_map/ppermute | solution.py:459
  26.2 4.8 %collective-permute-start.9 = (bf16[416,128]{1,0:T(8,128)(2,1)S(1)}, bf16[416,128]{1,0:T(8,128)(2,1)S(1)}, u32[]{:S(2)}, u32[]{:S(2)}) collective-permute-start(bf16[416,128]{1,0:T(8,128)(2,1)S(1)} %get-tuple-element.60), channel_id=1, source_target_pairs={{0,8},{2,10},{4,12},{6,14},{8,0},{10,2},{12,4},{14,6},{16,24},{18,... | collective-permute-start | bytes 319496 | tf_op jit(solution)/shard_map/ppermute | solution.py:459
  27.7 7.6 %collective-permute-start.10 = (bf16[1,2,24,128]{3,2,1,0:T(8,128)(2,1)S(1)}, bf16[1,2,24,128]{3,2,1,0:T(8,128)(2,1)S(1)}, u32[]{:S(2)}, u32[]{:S(2)}) collective-permute-start(bf16[1,2,24,128]{3,2,1,0:T(8,128)(2,1)S(1)} %bitcast.36), channel_id=1, source_target_pairs={{0,8},{2,10},{4,12},{6,14},{8,0},{10,2},{12,4},{14,6},{16,24},{18,... | collective-permute-start | bytes 36872 | tf_op jit(solution)/shard_map/ppermute | solution.py:459
  31.3 7.9 %collective-permute-start.11 = (bf16[416,128]{1,0:T(8,128)(2,1)S(1)}, bf16[416,128]{1,0:T(8,128)(2,1)S(1)}, u32[]{:S(2)}, u32[]{:S(2)}) collective-permute-start(bf16[416,128]{1,0:T(8,128)(2,1)S(1)} %get-tuple-element.65), channel_id=1, source_target_pairs={{0,16},{2,18},{4,20},{6,22},{8,24},{10,26},{12,28},{14,30},{16,0},... | collective-permute-start | bytes 319496 | tf_op jit(solution)/shard_map/ppermute | solution.py:459
  35.2 4.7 %collective-permute-start.13 = (bf16[2,2,24,128]{3,2,1,0:T(8,128)(2,1)S(1)}, bf16[2,2,24,128]{3,2,1,0:T(8,128)(2,1)S(1)}, u32[]{:S(2)}, u32[]{:S(2)}) collective-permute-start(bf16[2,2,24,128]{3,2,1,0:T(8,128)(2,1)S(1)} %pad_maximum_fusion.4), channel_id=1, source_target_pairs={{0,16},{2,18},{4,20},{6,22},{8,24},{10,26},{12,28},{14,30},{16,0},... | collective-permute-start | bytes 73736 | tf_op jit(solution)/shard_map/ppermute | solution.py:459
  39.5 4.7 %collective-permute-start.12 = (bf16[2,2,96,128]{3,2,1,0:T(8,128)(2,1)S(1)}, bf16[2,2,96,128]{3,2,1,0:T(8,128)(2,1)S(1)}, u32[]{:S(2)}, u32[]{:S(2)}) collective-permute-start(bf16[2,2,96,128]{3,2,1,0:T(8,128)(2,1)S(1)} %bitcast.34), channel_id=1, source_target_pairs={{0,8},{2,10},{4,12},{6,14},{8,0},{10,2},{12,4},{14,6},{16,24},{18,... | collective-permute-start | bytes 294920 | tf_op jit(solution)/shard_map/ppermute | solution.py:459
  44.2 6.3 %collective-permute-start.14 = (bf16[4,2,96,128]{3,2,1,0:T(8,128)(2,1)S(1)}, bf16[4,2,96,128]{3,2,1,0:T(8,128)(2,1)S(1)}, u32[]{:S(2)}, u32[]{:S(2)}) collective-permute-start(bf16[4,2,96,128]{3,2,1,0:T(8,128)(2,1)S(1)} %pad_maximum_fusion.refs_0_), channel_id=1, source_target_pairs={{0,4},{2,6},{4,0},{6,2},{8,12},{10,14},{12,8},{14,10},{16,20},{18,... | collective-permute-start | bytes 589832 | tf_op jit(solution)/shard_map/ppermute | solution.py:459
  45.4 5.6 %collective-permute-start.16 = (bf16[4,2,96,128]{3,2,1,0:T(8,128)(2,1)S(1)}, bf16[4,2,96,128]{3,2,1,0:T(8,128)(2,1)S(1)}, u32[]{:S(2)}, u32[]{:S(2)}) collective-permute-start(bf16[4,2,96,128]{3,2,1,0:T(8,128)(2,1)S(1)} %pad_maximum_fusion.refs_0_), channel_id=1, source_target_pairs={{0,2},{2,0},{4,6},{6,4},{8,10},{10,8},{12,14},{14,12},{16,18},{18,... | collective-permute-start | bytes 589832 | tf_op jit(solution)/shard_map/ppermute | solution.py:459
  45.4 5.6 %collective-permute-start.17 = (bf16[4,2,24,128]{3,2,1,0:T(8,128)(2,1)S(1)}, bf16[4,2,24,128]{3,2,1,0:T(8,128)(2,1)S(1)}, u32[]{:S(2)}, u32[]{:S(2)}) collective-permute-start(bf16[4,2,24,128]{3,2,1,0:T(8,128)(2,1)S(1)} %pad_maximum_fusion.3), channel_id=1, source_target_pairs={{0,4},{2,6},{4,0},{6,2},{8,12},{10,14},{12,8},{14,10},{16,20},{18,... | collective-permute-start | bytes 147464 | tf_op jit(solution)/shard_map/ppermute | solution.py:459
  50.4 1.7 %collective-permute-start.15 = (bf16[4,2,96,128]{3,2,1,0:T(8,128)(2,1)S(1)}, bf16[4,2,96,128]{3,2,1,0:T(8,128)(2,1)S(1)}, u32[]{:S(2)}, u32[]{:S(2)}) collective-permute-start(bf16[4,2,96,128]{3,2,1,0:T(8,128)(2,1)S(1)} %collective-permute-done.14.refs_1_), channel_id=1, source_target_pairs={{0,2},{2,0},{4,6},{6,4},{8,10},{10,8},{12,14},{14,12},{16,18},{18,... | collective-permute-start | bytes 589832 | tf_op jit(solution)/shard_map/ppermute | solution.py:459
  51.0 3.3 %copy-start.1 = (bf16[1,1024,512]{2,1,0:T(8,128)(2,1)S(1)}, bf16[1,1024,512]{2,1,0:T(8,128)(2,1)}, u32[]{:S(2)}) copy-start(bf16[1,1024,512]{2,1,0:T(8,128)(2,1)} %param.12) | copy-start | bytes 3145732
  51.0 3.3 %copy-start.2 = (bf16[1,1024,512]{2,1,0:T(8,128)(2,1)S(1)}, bf16[1,1024,512]{2,1,0:T(8,128)(2,1)}, u32[]{:S(2)}) copy-start(bf16[1,1024,512]{2,1,0:T(8,128)(2,1)} %param.11) | copy-start | bytes 3145732
  52.1 2.3 %collective-permute-start.19 = (bf16[8,2,24,128]{3,2,1,0:T(8,128)(2,1)S(1)}, bf16[8,2,24,128]{3,2,1,0:T(8,128)(2,1)S(1)}, u32[]{:S(2)}, u32[]{:S(2)}) collective-permute-start(bf16[8,2,24,128]{3,2,1,0:T(8,128)(2,1)S(1)} %pad_maximum_fusion.2.mine_ref), channel_id=1, source_target_pairs={{0,2},{2,0},{4,6},{6,4},{8,10},{10,8},{12,14},{14,12},{16,18},{18,... | collective-permute-start | bytes 294920 | tf_op jit(solution)/shard_map/ppermute | solution.py:459
  52.7 4.2 %collective-permute-start.18 = (bf16[48,512]{1,0:T(8,128)(2,1)S(1)}, bf16[48,512]{1,0:T(8,128)(2,1)S(1)}, u32[]{:S(2)}, u32[]{:S(2)}) collective-permute-start(bf16[48,512]{1,0:T(8,128)(2,1)S(1)} %get-tuple-element.71.rest_0_), channel_id=1, source_target_pairs={{0,1},{1,0},{2,3},{3,2},{4,5},{5,4},{6,7},{7,6},{8,9},{9,8},{10,11... | collective-permute-start | bytes 147464 | tf_op jit(solution)/shard_map/ppermute | solution.py:540
  (1 other events, 0.7 us)

commit v8 on v7

--- a/solution.py
+++ b/solution.py
@@ -426,7 +426,7 @@
 
 def append(rel, split, unit_rows, scal, ck, cv, drafts, after):
     rows = ck.shape[0]
-    block = rows // 4 if rows % 64 == 0 else rows
+    block = rows // 2 if rows % 128 == 0 else rows
     cache_spec = pl.BlockSpec((block, ck.shape[1]), lambda i: (i, 0))
     mine, other = drafts[0], drafts[-1]
     draft_spec = pl.BlockSpec(mine.shape, lambda i: (0, 0, 0, 0))

time: 57.8 us -> 57.8 us (level)
  Pallas kernels: 11 us -> 10.2 us
  waiting for transfers between devices: 20.9 us -> 21.6 us
    pallas_call x1, Pallas kernels: 2.35 us -> 1.62 us  [append(): pl.pallas_call(functools.partial(append_kernel, rel, split, unit_rows), g...]
    ppermute x1, waiting for transfers between devices: 0.24 us -> 0.97 us  [one_request(): projected = keep + lax.ppermute(send, 'head', [(0, 1), (1, 0)]).astype(f32)]
  transfers between devices with their start and end apart: 20 -> 20, of which waited for: 11 -> 11; matrix products, arithmetic and copies ran while one was open for 2% -> 2% of each run, Pallas kernels for 18% -> 17%
where the time goes in v8:
time: 57.8 us; the launch traced here: 57.5 us
  waiting for transfers between devices  21.6 us (37%)
  starting transfers between devices  19.2 us (33%)
  Pallas kernels  10.2 us (18%)
  local copies, waits for them, and re-layouts  3.63 us (6%)
  between operations  2.12 us (4%)
  other arithmetic  0.76 us (1%)
    ppermute x19, waiting for transfers between devices, swap(): return lax.ppermute(x, 'seq', [(i, i ^ 1 << bit) for i in range(n_seq)])  20.7 us
    ppermute x19, starting transfers between devices, swap(): return lax.ppermute(x, 'seq', [(i, i ^ 1 << bit) for i in range(n_seq)])  17.6 us
    pallas_call x2, Pallas kernels, attend(): pl.pallas_call(functools.partial(attend_kernel, rel, unit_rows, split, as...  5.95 us
    pallas_call x1, Pallas kernels, append(): pl.pallas_call(functools.partial(append_kernel, rel, split, unit_rows), g...  1.62 us
    ppermute x1, starting transfers between devices, one_request(): projected = keep + lax.ppermute(send, 'head', [(0, 1), (1, 0)]).astype(f32)  1.6 us
    pallas_call x2, Pallas kernels, project(): pl.pallas_call(functools.partial(project_kernel, rel, split, n_head, part...  1.58 us
    unnamed x11, local copies, waits for them, and re-layouts  1.42 us
    dynamic_slice x1, local copies, waits for them, and re-layouts, one_request(): lax.dynamic_slice_in_dim(c, core * heads * HD, heads * HD, 1)  1.28 us
  transfers between devices with their start and end apart: 20, of which 11 were waited for; matrix products, arithmetic and copies ran while one was open for 2% of the time, Pallas kernels for 17%

profile of v8, /device:TPU:0, one launch (start us, length us, event | category | flops | bytes accessed | tf_op | source)
XLA Modules:
  0.0 57.5 jit_solution(5962950310039570670)
XLA Ops:
  0.6 0.8 %copy_bitcast_fusion.1 = bf16[4,48,128]{2,1,0:T(8,128)(2,1)S(1)} fusion(bf16[1,6,32,128]{3,1,2,0:T(8,128)(2,1)} %bitcast.42), kind=kLoop, calls=%fused_computation.8 | loop fusion | bytes 98304 | tf_op jit(solution)/shard_map/reshape | solution.py:464
  4.0 3.7 %collective-permute-start.1 = (bf16[1,2,96,128]{3,2,1,0:T(8,128)(2,1)S(1)}, bf16[1,2,96,128]{3,2,1,0:T(8,128)(2,1)S(1)}, u32[]{:S(2)}, u32[]{:S(2)}) collective-permute-start(bf16[1,2,96,128]{3,2,1,0:T(8,128)(2,1)S(1)} %maximum_bitcast_fusion), channel_id=1, source_target_pairs={{0,16},{2,18},{4,20},{6,22},{8,24},{10,26},{12,28},{14,30},{16,0},... | collective-permute-start | bytes 147464 | tf_op jit(solution)/shard_map/ppermute | solution.py:459
  8.2 1.8 %collective-permute-done.1 = bf16[1,2,96,128]{3,2,1,0:T(8,128)(2,1)S(1)} collective-permute-done((bf16[1,2,96,128]{3,2,1,0:T(8,128)(2,1)S(1)}, bf16[1,2,96,128]{3,2,1,0:T(8,128)(2,1)S(1)}, u32[]{:S(2)}, u32[]{:S(2)}) %collective-permute-start.1) | collective-permute-done | bytes 49184 | tf_op jit(solution)/shard_map/ppermute | solution.py:459
  10.0 1.9 %collective-permute-start.4 = (bf16[2,2,96,128]{3,2,1,0:T(8,128)(2,1)S(1)}, bf16[2,2,96,128]{3,2,1,0:T(8,128)(2,1)S(1)}, u32[]{:S(2)}, u32[]{:S(2)}) collective-permute-start(bf16[2,2,96,128]{3,2,1,0:T(8,128)(2,1)S(1)} %pad_maximum_fusion.1), channel_id=1, source_target_pairs={{0,8},{2,10},{4,12},{6,14},{8,0},{10,2},{12,4},{14,6},{16,24},{18,... | collective-permute-start | bytes 294920 | tf_op jit(solution)/shard_map/ppermute | solution.py:459
  11.9 0.7 %copy-done.3 = bf16[1,6,512]{2,1,0:T(8,128)(2,1)S(1)} copy-done((bf16[1,6,512]{2,1,0:T(8,128)(2,1)S(1)}, bf16[1,6,512]{2,1,0:T(8,128)(2,1)}, u32[]{:S(2)}) %copy-start.3) | copy-done | bytes 6168
  12.6 0.7 %copy-done.4 = bf16[1,6,512]{2,1,0:T(8,128)(2,1)S(1)} copy-done((bf16[1,6,512]{2,1,0:T(8,128)(2,1)S(1)}, bf16[1,6,512]{2,1,0:T(8,128)(2,1)}, u32[]{:S(2)}) %copy-start.4) | copy-done | bytes 6168
  13.4 1.3 %constant_dynamic-slice_fusion = (bf16[1024,256]{1,0:T(8,128)(2,1)S(1)}, bf16[1024,256]{1,0:T(8,128)(2,1)S(1)}) fusion(bf16[1024,512]{1,0:T(8,128)(2,1)} %bitcast.29, s32[]{:T(128)S(6)} %select_n.20, bf16[1024,512]{1,0:T(8,128)(2,1)} %bitcast.32), kind=kLoop, calls=%fused_computation.12 | loop fusion | bytes 2097156 | tf_op jit(solution)/shard_map/dynamic_slice | solution.py:489
  14.9 1.6 %collective-permute-start.5 = (bf16[4,2,96,128]{3,2,1,0:T(8,128)(2,1)S(1)}, bf16[4,2,96,128]{3,2,1,0:T(8,128)(2,1)S(1)}, u32[]{:S(2)}, u32[]{:S(2)}) collective-permute-start(bf16[4,2,96,128]{3,2,1,0:T(8,128)(2,1)S(1)} %constant_dynamic-update-slice_fusion.q_ref), channel_id=1, source_target_pairs={{0,4},{2,6},{4,0},{6,2},{8,12},{10,14},{12,8},{14,10},{16,20},{18,... | collective-permute-start | bytes 589832 | tf_op jit(solution)/shard_map/ppermute | solution.py:459
  16.5 3.0 %shard_map.104.rest_5_ = bf16[800,128]{1,0:T(8,128)(2,1)S(1)} custom-call(s32[2,128]{1,0:T(2,128)S(1)} %broadcast_in_dim.15.scal, bf16[4,2,96,128]{3,2,1,0:T(8,128)(2,1)S(1)} %constant_dynamic-update-slice_fusion.q_ref, bf16[1024,256]{1,0:T(8,128)(2,1)S(1)} %get-tuple-element.78.rest_0_, bf16[1024,256]{1,0:T(8,128)(2,1)S(1)} %get-tuple-element.77.rest_1_, ...), custom_call_target="tpu_custom_call" | custom-call | flops 855638016 | bytes 2097152 | tf_op jit(solution)/shard_map/pallas_call | solution.py:183
  20.0 1.3 %collective-permute-done.5.q_ref = bf16[4,2,96,128]{3,2,1,0:T(8,128)(2,1)S(1)} collective-permute-done((bf16[4,2,96,128]{3,2,1,0:T(8,128)(2,1)S(1)}, bf16[4,2,96,128]{3,2,1,0:T(8,128)(2,1)S(1)}, u32[]{:S(2)}, u32[]{:S(2)}) %collective-permute-start.5) | collective-permute-done | bytes 196640 | tf_op jit(solution)/shard_map/ppermute | solution.py:459
  21.4 3.0 %shard_map.105 = (f32[768,128]{1,0:T(8,128)S(1)}, f32[16,128]{1,0:T(8,128)S(1)}) custom-call(s32[2,128]{1,0:T(2,128)S(1)} %broadcast_in_dim.15.scal, bf16[4,2,96,128]{3,2,1,0:T(8,128)(2,1)S(1)} %collective-permute-done.5.q_ref, bf16[1024,256]{1,0:T(8,128)(2,1)S(1)} %get-tuple-element.78.rest_0_, bf16[1024,256]{1,0:T(8,128)(2,1)S(1)} %get-tuple-element.77.rest_1_, ...), custom_call_target="tpu_custom_call" | custom-call | flops 855638016 | bytes 2097152 | tf_op jit(solution)/shard_map/pallas_call | solution.py:183
  24.3 1.5 %collective-permute-done.8.msg_ref = bf16[800,128]{1,0:T(8,128)(2,1)S(1)} collective-permute-done((bf16[800,128]{1,0:T(8,128)(2,1)S(1)}, bf16[800,128]{1,0:T(8,128)(2,1)S(1)}, u32[]{:S(2)}, u32[]{:S(2)}) %collective-permute-start.8) | collective-permute-done | bytes 204832 | tf_op jit(solution)/shard_map/ppermute | solution.py:459
  26.2 1.5 %collective-permute-start.9 = (bf16[416,128]{1,0:T(8,128)(2,1)S(1)}, bf16[416,128]{1,0:T(8,128)(2,1)S(1)}, u32[]{:S(2)}, u32[]{:S(2)}) collective-permute-start(bf16[416,128]{1,0:T(8,128)(2,1)S(1)} %get-tuple-element.60), channel_id=1, source_target_pairs={{0,8},{2,10},{4,12},{6,14},{8,0},{10,2},{12,4},{14,6},{16,24},{18,... | collective-permute-start | bytes 319496 | tf_op jit(solution)/shard_map/ppermute | solution.py:459
  28.3 2.7 %collective-permute-done.9.msg_ref = bf16[416,128]{1,0:T(8,128)(2,1)S(1)} collective-permute-done((bf16[416,128]{1,0:T(8,128)(2,1)S(1)}, bf16[416,128]{1,0:T(8,128)(2,1)S(1)}, u32[]{:S(2)}, u32[]{:S(2)}) %collective-permute-start.9) | collective-permute-done | bytes 106528 | tf_op jit(solution)/shard_map/ppermute | solution.py:459
  31.3 3.9 %collective-permute-start.11 = (bf16[416,128]{1,0:T(8,128)(2,1)S(1)}, bf16[416,128]{1,0:T(8,128)(2,1)S(1)}, u32[]{:S(2)}, u32[]{:S(2)}) collective-permute-start(bf16[416,128]{1,0:T(8,128)(2,1)S(1)} %get-tuple-element.65), channel_id=1, source_target_pairs={{0,16},{2,18},{4,20},{6,22},{8,24},{10,26},{12,28},{14,30},{16,0},... | collective-permute-start | bytes 319496 | tf_op jit(solution)/shard_map/ppermute | solution.py:459
  35.3 3.8 %collective-permute-done.11.msg_ref = bf16[416,128]{1,0:T(8,128)(2,1)S(1)} collective-permute-done((bf16[416,128]{1,0:T(8,128)(2,1)S(1)}, bf16[416,128]{1,0:T(8,128)(2,1)S(1)}, u32[]{:S(2)}, u32[]{:S(2)}) %collective-permute-start.11) | collective-permute-done | bytes 106528 | tf_op jit(solution)/shard_map/ppermute | solution.py:459
  40.0 4.2 %collective-permute-done.12 = bf16[2,2,96,128]{3,2,1,0:T(8,128)(2,1)S(1)} collective-permute-done((bf16[2,2,96,128]{3,2,1,0:T(8,128)(2,1)S(1)}, bf16[2,2,96,128]{3,2,1,0:T(8,128)(2,1)S(1)}, u32[]{:S(2)}, u32[]{:S(2)}) %collective-permute-start.12) | collective-permute-done | bytes 98336 | tf_op jit(solution)/shard_map/ppermute | solution.py:459
  44.2 1.2 %collective-permute-start.14 = (bf16[4,2,96,128]{3,2,1,0:T(8,128)(2,1)S(1)}, bf16[4,2,96,128]{3,2,1,0:T(8,128)(2,1)S(1)}, u32[]{:S(2)}, u32[]{:S(2)}) collective-permute-start(bf16[4,2,96,128]{3,2,1,0:T(8,128)(2,1)S(1)} %pad_maximum_fusion.refs_0_), channel_id=1, source_target_pairs={{0,4},{2,6},{4,0},{6,2},{8,12},{10,14},{12,8},{14,10},{16,20},{18,... | collective-permute-start | bytes 589832 | tf_op jit(solution)/shard_map/ppermute | solution.py:459
  45.4 0.9 %collective-permute-start.17 = (bf16[4,2,24,128]{3,2,1,0:T(8,128)(2,1)S(1)}, bf16[4,2,24,128]{3,2,1,0:T(8,128)(2,1)S(1)}, u32[]{:S(2)}, u32[]{:S(2)}) collective-permute-start(bf16[4,2,24,128]{3,2,1,0:T(8,128)(2,1)S(1)} %pad_maximum_fusion.3), channel_id=1, source_target_pairs={{0,4},{2,6},{4,0},{6,2},{8,12},{10,14},{12,8},{14,10},{16,20},{18,... | collective-permute-start | bytes 147464 | tf_op jit(solution)/shard_map/ppermute | solution.py:459
  46.3 4.2 %collective-permute-done.14.refs_1_ = bf16[4,2,96,128]{3,2,1,0:T(8,128)(2,1)S(1)} collective-permute-done((bf16[4,2,96,128]{3,2,1,0:T(8,128)(2,1)S(1)}, bf16[4,2,96,128]{3,2,1,0:T(8,128)(2,1)S(1)}, u32[]{:S(2)}, u32[]{:S(2)}) %collective-permute-start.14) | collective-permute-done | bytes 196640 | tf_op jit(solution)/shard_map/ppermute | solution.py:459
  51.0 1.0 %shard_map.109.refs_2_ = f32[96,512]{1,0:T(8,128)S(1)} custom-call(bf16[4,2,96,128]{3,2,1,0:T(8,128)(2,1)S(1)} %pad_maximum_fusion.refs_0_, bf16[4,2,96,128]{3,2,1,0:T(8,128)(2,1)S(1)} %collective-permute-done.14.refs_1_, bf16[4,2,96,128]{3,2,1,0:T(8,128)(2,1)S(1)} %collective-permute-done.16.refs_2_, bf16[4096,512]{1,0:T(8,128)(2,1)S(1)} %copy-done), custom_call_target="tpu_custom_call" | custom-call | flops 402653184 | bytes 4194304 | tf_op jit(solution)/shard_map/pallas_call | solution.py:321
  52.7 1.6 %collective-permute-start.18 = (bf16[48,512]{1,0:T(8,128)(2,1)S(1)}, bf16[48,512]{1,0:T(8,128)(2,1)S(1)}, u32[]{:S(2)}, u32[]{:S(2)}) collective-permute-start(bf16[48,512]{1,0:T(8,128)(2,1)S(1)} %get-tuple-element.71.rest_0_), channel_id=1, source_target_pairs={{0,1},{1,0},{2,3},{3,2},{4,5},{5,4},{6,7},{7,6},{8,9},{9,8},{10,11... | collective-permute-start | bytes 147464 | tf_op jit(solution)/shard_map/ppermute | solution.py:540
  54.3 1.6 %shard_map.111 = (bf16[1024,512]{1,0:T(8,128)(2,1)}, bf16[1024,512]{1,0:T(8,128)(2,1)}) custom-call(s32[2,128]{1,0:T(2,128)S(1)} %broadcast_in_dim.15.scal, bf16[1024,512]{1,0:T(8,128)(2,1)S(1)} %bitcast.33, bf16[1024,512]{1,0:T(8,128)(2,1)S(1)} %bitcast.30, bf16[8,2,24,128]{3,2,1,0:T(8,128)(2,1)S(1)} %pad_maximum_fusion.2.mine_ref, ...), custom_call_target="tpu_custom_call" | custom-call | bytes 4194304 | tf_op jit(solution)/shard_map/pallas_call | solution.py:434
  55.9 1.0 %collective-permute-done.18 = bf16[48,512]{1,0:T(8,128)(2,1)S(1)} collective-permute-done((bf16[48,512]{1,0:T(8,128)(2,1)S(1)}, bf16[48,512]{1,0:T(8,128)(2,1)S(1)}, u32[]{:S(2)}, u32[]{:S(2)}) %collective-permute-start.18) | collective-permute-done | bytes 49184 | tf_op jit(solution)/shard_map/ppermute | solution.py:540
  (49 shorter events, 6.7 us)
Async XLA Ops:
  1.5 1.9 %collective-permute-start = (bf16[2,48,128]{2,1,0:T(8,128)(2,1)S(1)}, bf16[2,48,128]{2,1,0:T(8,128)(2,1)S(1)}, u32[]{:S(2)}, u32[]{:S(2)}) collective-permute-start(bf16[2,48,128]{2,1,0:T(8,128)(2,1)S(1)} %get-tuple-element.76), channel_id=1, source_target_pairs={{0,2},{2,0},{4,6},{6,4},{8,10},{10,8},{12,14},{14,12},{16,18},{18,... | collective-permute-start | bytes 73736 | tf_op jit(solution)/shard_map/ppermute | solution.py:459
  3.5 13.0 %collective-permute-start.6 = (bf16[1024,512]{1,0:T(8,128)(2,1)}, bf16[1024,512]{1,0:T(8,128)(2,1)S(1)}, u32[]{:S(2)}, u32[]{:S(2)}) collective-permute-start(bf16[1024,512]{1,0:T(8,128)(2,1)} %bitcast.31), channel_id=1, source_target_pairs={{0,2},{2,0},{4,6},{6,4},{8,10},{10,8},{12,14},{14,12},{16,18},{18,... | collective-permute-start | bytes 3145736 | tf_op jit(solution)/shard_map/ppermute | solution.py:459
  3.5 13.0 %collective-permute-start.7 = (bf16[1024,512]{1,0:T(8,128)(2,1)}, bf16[1024,512]{1,0:T(8,128)(2,1)S(1)}, u32[]{:S(2)}, u32[]{:S(2)}) collective-permute-start(bf16[1024,512]{1,0:T(8,128)(2,1)} %bitcast.28), channel_id=1, source_target_pairs={{0,2},{2,0},{4,6},{6,4},{8,10},{10,8},{12,14},{14,12},{16,18},{18,... | collective-permute-start | bytes 3145736 | tf_op jit(solution)/shard_map/ppermute | solution.py:459
  4.0 6.0 %collective-permute-start.1 = (bf16[1,2,96,128]{3,2,1,0:T(8,128)(2,1)S(1)}, bf16[1,2,96,128]{3,2,1,0:T(8,128)(2,1)S(1)}, u32[]{:S(2)}, u32[]{:S(2)}) collective-permute-start(bf16[1,2,96,128]{3,2,1,0:T(8,128)(2,1)S(1)} %maximum_bitcast_fusion), channel_id=1, source_target_pairs={{0,16},{2,18},{4,20},{6,22},{8,24},{10,26},{12,28},{14,30},{16,0},... | collective-permute-start | bytes 147464 | tf_op jit(solution)/shard_map/ppermute | solution.py:459
  7.7 2.4 %collective-permute-start.2 = (bf16[6,512]{1,0:T(8,128)(2,1)}, bf16[6,512]{1,0:T(8,128)(2,1)S(1)}, u32[]{:S(2)}, u32[]{:S(2)}) collective-permute-start(bf16[6,512]{1,0:T(8,128)(2,1)} %bitcast.38), channel_id=1, source_target_pairs={{0,2},{2,0},{4,6},{6,4},{8,10},{10,8},{12,14},{14,12},{16,18},{18,... | collective-permute-start | bytes 18440 | tf_op jit(solution)/shard_map/ppermute | solution.py:459
  7.8 2.2 %collective-permute-start.3 = (bf16[6,512]{1,0:T(8,128)(2,1)}, bf16[6,512]{1,0:T(8,128)(2,1)S(1)}, u32[]{:S(2)}, u32[]{:S(2)}) collective-permute-start(bf16[6,512]{1,0:T(8,128)(2,1)} %bitcast.40), channel_id=1, source_target_pairs={{0,2},{2,0},{4,6},{6,4},{8,10},{10,8},{12,14},{14,12},{16,18},{18,... | collective-permute-start | bytes 18440 | tf_op jit(solution)/shard_map/ppermute | solution.py:459
  10.0 4.9 %collective-permute-start.4 = (bf16[2,2,96,128]{3,2,1,0:T(8,128)(2,1)S(1)}, bf16[2,2,96,128]{3,2,1,0:T(8,128)(2,1)S(1)}, u32[]{:S(2)}, u32[]{:S(2)}) collective-permute-start(bf16[2,2,96,128]{3,2,1,0:T(8,128)(2,1)S(1)} %pad_maximum_fusion.1), channel_id=1, source_target_pairs={{0,8},{2,10},{4,12},{6,14},{8,0},{10,2},{12,4},{14,6},{16,24},{18,... | collective-permute-start | bytes 294920 | tf_op jit(solution)/shard_map/ppermute | solution.py:459
  11.9 0.7 %copy-start.3 = (bf16[1,6,512]{2,1,0:T(8,128)(2,1)S(1)}, bf16[1,6,512]{2,1,0:T(8,128)(2,1)}, u32[]{:S(2)}) copy-start(bf16[1,6,512]{2,1,0:T(8,128)(2,1)} %param.9) | copy-start | bytes 18436
  14.9 6.4 %collective-permute-start.5 = (bf16[4,2,96,128]{3,2,1,0:T(8,128)(2,1)S(1)}, bf16[4,2,96,128]{3,2,1,0:T(8,128)(2,1)S(1)}, u32[]{:S(2)}, u32[]{:S(2)}) collective-permute-start(bf16[4,2,96,128]{3,2,1,0:T(8,128)(2,1)S(1)} %constant_dynamic-update-slice_fusion.q_ref), channel_id=1, source_target_pairs={{0,4},{2,6},{4,0},{6,2},{8,12},{10,14},{12,8},{14,10},{16,20},{18,... | collective-permute-start | bytes 589832 | tf_op jit(solution)/shard_map/ppermute | solution.py:459
  16.5 34.5 %copy-start = (bf16[4096,512]{1,0:T(8,128)(2,1)S(1)}, bf16[4096,512]{1,0:T(8,128)(2,1)}, u32[]{:S(2)}) copy-start(bf16[4096,512]{1,0:T(8,128)(2,1)} %refs_1_.1) | copy-start | bytes 12582916
  19.5 6.3 %collective-permute-start.8 = (bf16[800,128]{1,0:T(8,128)(2,1)S(1)}, bf16[800,128]{1,0:T(8,128)(2,1)S(1)}, u32[]{:S(2)}, u32[]{:S(2)}) collective-permute-start(bf16[800,128]{1,0:T(8,128)(2,1)S(1)} %shard_map.104.rest_5_), channel_id=1, source_target_pairs={{0,4},{2,6},{4,0},{6,2},{8,12},{10,14},{12,8},{14,10},{16,20},{18,... | collective-permute-start | bytes 614408 | tf_op jit(solution)/shard_map/ppermute | solution.py:459
  26.2 4.8 %collective-permute-start.9 = (bf16[416,128]{1,0:T(8,128)(2,1)S(1)}, bf16[416,128]{1,0:T(8,128)(2,1)S(1)}, u32[]{:S(2)}, u32[]{:S(2)}) collective-permute-start(bf16[416,128]{1,0:T(8,128)(2,1)S(1)} %get-tuple-element.60), channel_id=1, source_target_pairs={{0,8},{2,10},{4,12},{6,14},{8,0},{10,2},{12,4},{14,6},{16,24},{18,... | collective-permute-start | bytes 319496 | tf_op jit(solution)/shard_map/ppermute | solution.py:459
  27.7 7.6 %collective-permute-start.10 = (bf16[1,2,24,128]{3,2,1,0:T(8,128)(2,1)S(1)}, bf16[1,2,24,128]{3,2,1,0:T(8,128)(2,1)S(1)}, u32[]{:S(2)}, u32[]{:S(2)}) collective-permute-start(bf16[1,2,24,128]{3,2,1,0:T(8,128)(2,1)S(1)} %bitcast.36), channel_id=1, source_target_pairs={{0,8},{2,10},{4,12},{6,14},{8,0},{10,2},{12,4},{14,6},{16,24},{18,... | collective-permute-start | bytes 36872 | tf_op jit(solution)/shard_map/ppermute | solution.py:459
  31.3 7.9 %collective-permute-start.11 = (bf16[416,128]{1,0:T(8,128)(2,1)S(1)}, bf16[416,128]{1,0:T(8,128)(2,1)S(1)}, u32[]{:S(2)}, u32[]{:S(2)}) collective-permute-start(bf16[416,128]{1,0:T(8,128)(2,1)S(1)} %get-tuple-element.65), channel_id=1, source_target_pairs={{0,16},{2,18},{4,20},{6,22},{8,24},{10,26},{12,28},{14,30},{16,0},... | collective-permute-start | bytes 319496 | tf_op jit(solution)/shard_map/ppermute | solution.py:459
  35.2 4.7 %collective-permute-start.13 = (bf16[2,2,24,128]{3,2,1,0:T(8,128)(2,1)S(1)}, bf16[2,2,24,128]{3,2,1,0:T(8,128)(2,1)S(1)}, u32[]{:S(2)}, u32[]{:S(2)}) collective-permute-start(bf16[2,2,24,128]{3,2,1,0:T(8,128)(2,1)S(1)} %pad_maximum_fusion.4), channel_id=1, source_target_pairs={{0,16},{2,18},{4,20},{6,22},{8,24},{10,26},{12,28},{14,30},{16,0},... | collective-permute-start | bytes 73736 | tf_op jit(solution)/shard_map/ppermute | solution.py:459
  39.5 4.7 %collective-permute-start.12 = (bf16[2,2,96,128]{3,2,1,0:T(8,128)(2,1)S(1)}, bf16[2,2,96,128]{3,2,1,0:T(8,128)(2,1)S(1)}, u32[]{:S(2)}, u32[]{:S(2)}) collective-permute-start(bf16[2,2,96,128]{3,2,1,0:T(8,128)(2,1)S(1)} %bitcast.34), channel_id=1, source_target_pairs={{0,8},{2,10},{4,12},{6,14},{8,0},{10,2},{12,4},{14,6},{16,24},{18,... | collective-permute-start | bytes 294920 | tf_op jit(solution)/shard_map/ppermute | solution.py:459
  44.2 6.3 %collective-permute-start.14 = (bf16[4,2,96,128]{3,2,1,0:T(8,128)(2,1)S(1)}, bf16[4,2,96,128]{3,2,1,0:T(8,128)(2,1)S(1)}, u32[]{:S(2)}, u32[]{:S(2)}) collective-permute-start(bf16[4,2,96,128]{3,2,1,0:T(8,128)(2,1)S(1)} %pad_maximum_fusion.refs_0_), channel_id=1, source_target_pairs={{0,4},{2,6},{4,0},{6,2},{8,12},{10,14},{12,8},{14,10},{16,20},{18,... | collective-permute-start | bytes 589832 | tf_op jit(solution)/shard_map/ppermute | solution.py:459
  45.4 5.6 %collective-permute-start.16 = (bf16[4,2,96,128]{3,2,1,0:T(8,128)(2,1)S(1)}, bf16[4,2,96,128]{3,2,1,0:T(8,128)(2,1)S(1)}, u32[]{:S(2)}, u32[]{:S(2)}) collective-permute-start(bf16[4,2,96,128]{3,2,1,0:T(8,128)(2,1)S(1)} %pad_maximum_fusion.refs_0_), channel_id=1, source_target_pairs={{0,2},{2,0},{4,6},{6,4},{8,10},{10,8},{12,14},{14,12},{16,18},{18,... | collective-permute-start | bytes 589832 | tf_op jit(solution)/shard_map/ppermute | solution.py:459
  45.4 5.6 %collective-permute-start.17 = (bf16[4,2,24,128]{3,2,1,0:T(8,128)(2,1)S(1)}, bf16[4,2,24,128]{3,2,1,0:T(8,128)(2,1)S(1)}, u32[]{:S(2)}, u32[]{:S(2)}) collective-permute-start(bf16[4,2,24,128]{3,2,1,0:T(8,128)(2,1)S(1)} %pad_maximum_fusion.3), channel_id=1, source_target_pairs={{0,4},{2,6},{4,0},{6,2},{8,12},{10,14},{12,8},{14,10},{16,20},{18,... | collective-permute-start | bytes 147464 | tf_op jit(solution)/shard_map/ppermute | solution.py:459
  50.4 1.7 %collective-permute-start.15 = (bf16[4,2,96,128]{3,2,1,0:T(8,128)(2,1)S(1)}, bf16[4,2,96,128]{3,2,1,0:T(8,128)(2,1)S(1)}, u32[]{:S(2)}, u32[]{:S(2)}) collective-permute-start(bf16[4,2,96,128]{3,2,1,0:T(8,128)(2,1)S(1)} %collective-permute-done.14.refs_1_), channel_id=1, source_target_pairs={{0,2},{2,0},{4,6},{6,4},{8,10},{10,8},{12,14},{14,12},{16,18},{18,... | collective-permute-start | bytes 589832 | tf_op jit(solution)/shard_map/ppermute | solution.py:459
  51.0 3.3 %copy-start.1 = (bf16[1,1024,512]{2,1,0:T(8,128)(2,1)S(1)}, bf16[1,1024,512]{2,1,0:T(8,128)(2,1)}, u32[]{:S(2)}) copy-start(bf16[1,1024,512]{2,1,0:T(8,128)(2,1)} %param.12) | copy-start | bytes 3145732
  51.0 3.3 %copy-start.2 = (bf16[1,1024,512]{2,1,0:T(8,128)(2,1)S(1)}, bf16[1,1024,512]{2,1,0:T(8,128)(2,1)}, u32[]{:S(2)}) copy-start(bf16[1,1024,512]{2,1,0:T(8,128)(2,1)} %param.11) | copy-start | bytes 3145732
  52.1 2.3 %collective-permute-start.19 = (bf16[8,2,24,128]{3,2,1,0:T(8,128)(2,1)S(1)}, bf16[8,2,24,128]{3,2,1,0:T(8,128)(2,1)S(1)}, u32[]{:S(2)}, u32[]{:S(2)}) collective-permute-start(bf16[8,2,24,128]{3,2,1,0:T(8,128)(2,1)S(1)} %pad_maximum_fusion.2.mine_ref), channel_id=1, source_target_pairs={{0,2},{2,0},{4,6},{6,4},{8,10},{10,8},{12,14},{14,12},{16,18},{18,... | collective-permute-start | bytes 294920 | tf_op jit(solution)/shard_map/ppermute | solution.py:459
  52.7 4.2 %collective-permute-start.18 = (bf16[48,512]{1,0:T(8,128)(2,1)S(1)}, bf16[48,512]{1,0:T(8,128)(2,1)S(1)}, u32[]{:S(2)}, u32[]{:S(2)}) collective-permute-start(bf16[48,512]{1,0:T(8,128)(2,1)S(1)} %get-tuple-element.71.rest_0_), channel_id=1, source_target_pairs={{0,1},{1,0},{2,3},{3,2},{4,5},{5,4},{6,7},{7,6},{8,9},{9,8},{10,11... | collective-permute-start | bytes 147464 | tf_op jit(solution)/shard_map/ppermute | solution.py:540
  (1 other events, 0.7 us)

commit v9 on v8

--- a/solution.py
+++ b/solution.py
@@ -482,9 +482,7 @@
         new = swap(q, bit)
         q = jnp.concatenate([q, new], axis=0)
         if split == 2 and bit == bits[0]:
-            q, drafts_own, drafts_other, *own = lax.optimization_barrier(
-                (q, drafts_own, drafts_other, ck, cv)
-            )
+            q, *own = lax.optimization_barrier((q, ck, cv))
             caches[:2] = [
                 lax.dynamic_slice_in_dim(c, core * heads * HD, heads * HD, 1) for c in own
             ]

time: 57.8 us -> 57.7 us (level)
  starting transfers between devices: 19.2 us -> 18.6 us
where the time goes in v9:
time: 57.7 us; the launch traced here: 57.4 us
  waiting for transfers between devices  22 us (38%)
  starting transfers between devices  18.6 us (32%)
  Pallas kernels  10.3 us (18%)
  local copies, waits for them, and re-layouts  3.62 us (6%)
  between operations  2.11 us (4%)
  other arithmetic  0.76 us (1%)
    ppermute x19, waiting for transfers between devices, swap(): return lax.ppermute(x, 'seq', [(i, i ^ 1 << bit) for i in range(n_seq)])  21 us
    ppermute x19, starting transfers between devices, swap(): return lax.ppermute(x, 'seq', [(i, i ^ 1 << bit) for i in range(n_seq)])  17 us
    pallas_call x2, Pallas kernels, attend(): pl.pallas_call(functools.partial(attend_kernel, rel, unit_rows, split, as...  5.97 us
    pallas_call x1, Pallas kernels, append(): pl.pallas_call(functools.partial(append_kernel, rel, split, unit_rows), g...  1.62 us
    pallas_call x2, Pallas kernels, project(): pl.pallas_call(functools.partial(project_kernel, rel, split, n_head, part...  1.59 us
    ppermute x1, starting transfers between devices, one_request(): projected = keep + lax.ppermute(send, 'head', [(0, 1), (1, 0)]).astype(f32)  1.59 us
    unnamed x11, local copies, waits for them, and re-layouts  1.42 us
    dynamic_slice x1, local copies, waits for them, and re-layouts, one_request(): lax.dynamic_slice_in_dim(c, core * heads * HD, heads * HD, 1)  1.27 us
  transfers between devices with their start and end apart: 20, of which 11 were waited for; matrix products, arithmetic and copies ran while one was open for 2% of the time, Pallas kernels for 17%

profile of v9, /device:TPU:0, one launch (start us, length us, event | category | flops | bytes accessed | tf_op | source)
XLA Modules:
  0.0 57.4 jit_solution(4706961929588201314)
XLA Ops:
  0.6 0.8 %copy_bitcast_fusion.1 = bf16[4,48,128]{2,1,0:T(8,128)(2,1)S(1)} fusion(bf16[1,6,32,128]{3,1,2,0:T(8,128)(2,1)} %bitcast.42), kind=kLoop, calls=%fused_computation.8 | loop fusion | bytes 98304 | tf_op jit(solution)/shard_map/reshape | solution.py:464
  4.0 3.7 %collective-permute-start.1 = (bf16[1,2,96,128]{3,2,1,0:T(8,128)(2,1)S(1)}, bf16[1,2,96,128]{3,2,1,0:T(8,128)(2,1)S(1)}, u32[]{:S(2)}, u32[]{:S(2)}) collective-permute-start(bf16[1,2,96,128]{3,2,1,0:T(8,128)(2,1)S(1)} %maximum_bitcast_fusion), channel_id=1, source_target_pairs={{0,16},{2,18},{4,20},{6,22},{8,24},{10,26},{12,28},{14,30},{16,0},... | collective-permute-start | bytes 147464 | tf_op jit(solution)/shard_map/ppermute | solution.py:459
  8.2 0.9 %collective-permute-done.6.refs_2_ = bf16[6,512]{1,0:T(8,128)(2,1)S(1)} collective-permute-done((bf16[6,512]{1,0:T(8,128)(2,1)}, bf16[6,512]{1,0:T(8,128)(2,1)S(1)}, u32[]{:S(2)}, u32[]{:S(2)}) %collective-permute-start.6) | collective-permute-done | bytes 6176 | tf_op jit(solution)/shard_map/ppermute | solution.py:459
  9.2 0.7 %copy-done.3 = bf16[1,6,512]{2,1,0:T(8,128)(2,1)S(1)} copy-done((bf16[1,6,512]{2,1,0:T(8,128)(2,1)S(1)}, bf16[1,6,512]{2,1,0:T(8,128)(2,1)}, u32[]{:S(2)}) %copy-start.3) | copy-done | bytes 6168
  10.7 1.6 %collective-permute-start.2 = (bf16[2,2,96,128]{3,2,1,0:T(8,128)(2,1)S(1)}, bf16[2,2,96,128]{3,2,1,0:T(8,128)(2,1)S(1)}, u32[]{:S(2)}, u32[]{:S(2)}) collective-permute-start(bf16[2,2,96,128]{3,2,1,0:T(8,128)(2,1)S(1)} %pad_maximum_fusion.1), channel_id=1, source_target_pairs={{0,8},{2,10},{4,12},{6,14},{8,0},{10,2},{12,4},{14,6},{16,24},{18,... | collective-permute-start | bytes 294920 | tf_op jit(solution)/shard_map/ppermute | solution.py:459
  12.4 1.3 %constant_dynamic-slice_fusion = (bf16[1024,256]{1,0:T(8,128)(2,1)S(1)}, bf16[1024,256]{1,0:T(8,128)(2,1)S(1)}) fusion(bf16[1024,512]{1,0:T(8,128)(2,1)} %bitcast.29, s32[]{:T(128)S(6)} %select_n.20, bf16[1024,512]{1,0:T(8,128)(2,1)} %bitcast.32), kind=kLoop, calls=%fused_computation.12 | loop fusion | bytes 2097156 | tf_op jit(solution)/shard_map/dynamic_slice | solution.py:487
  13.6 2.2 %collective-permute-done.2 = bf16[2,2,96,128]{3,2,1,0:T(8,128)(2,1)S(1)} collective-permute-done((bf16[2,2,96,128]{3,2,1,0:T(8,128)(2,1)S(1)}, bf16[2,2,96,128]{3,2,1,0:T(8,128)(2,1)S(1)}, u32[]{:S(2)}, u32[]{:S(2)}) %collective-permute-start.2) | collective-permute-done | bytes 98336 | tf_op jit(solution)/shard_map/ppermute | solution.py:459
  15.8 1.6 %collective-permute-start.3 = (bf16[4,2,96,128]{3,2,1,0:T(8,128)(2,1)S(1)}, bf16[4,2,96,128]{3,2,1,0:T(8,128)(2,1)S(1)}, u32[]{:S(2)}, u32[]{:S(2)}) collective-permute-start(bf16[4,2,96,128]{3,2,1,0:T(8,128)(2,1)S(1)} %constant_dynamic-update-slice_fusion.q_ref), channel_id=1, source_target_pairs={{0,4},{2,6},{4,0},{6,2},{8,12},{10,14},{12,8},{14,10},{16,20},{18,... | collective-permute-start | bytes 589832 | tf_op jit(solution)/shard_map/ppermute | solution.py:459
  17.4 3.0 %shard_map.104.rest_5_ = bf16[800,128]{1,0:T(8,128)(2,1)S(1)} custom-call(s32[2,128]{1,0:T(2,128)S(1)} %broadcast_in_dim.15.scal, bf16[4,2,96,128]{3,2,1,0:T(8,128)(2,1)S(1)} %constant_dynamic-update-slice_fusion.q_ref, bf16[1024,256]{1,0:T(8,128)(2,1)S(1)} %get-tuple-element.70.rest_0_, bf16[1024,256]{1,0:T(8,128)(2,1)S(1)} %get-tuple-element.69.rest_1_, ...), custom_call_target="tpu_custom_call" | custom-call | flops 855638016 | bytes 2097152 | tf_op jit(solution)/shard_map/pallas_call | solution.py:183
  21.0 1.3 %collective-permute-done.3.q_ref = bf16[4,2,96,128]{3,2,1,0:T(8,128)(2,1)S(1)} collective-permute-done((bf16[4,2,96,128]{3,2,1,0:T(8,128)(2,1)S(1)}, bf16[4,2,96,128]{3,2,1,0:T(8,128)(2,1)S(1)}, u32[]{:S(2)}, u32[]{:S(2)}) %collective-permute-start.3) | collective-permute-done | bytes 196640 | tf_op jit(solution)/shard_map/ppermute | solution.py:459
  22.3 3.0 %shard_map.105 = (f32[768,128]{1,0:T(8,128)S(1)}, f32[16,128]{1,0:T(8,128)S(1)}) custom-call(s32[2,128]{1,0:T(2,128)S(1)} %broadcast_in_dim.15.scal, bf16[4,2,96,128]{3,2,1,0:T(8,128)(2,1)S(1)} %collective-permute-done.3.q_ref, bf16[1024,256]{1,0:T(8,128)(2,1)S(1)} %get-tuple-element.70.rest_0_, bf16[1024,256]{1,0:T(8,128)(2,1)S(1)} %get-tuple-element.69.rest_1_, ...), custom_call_target="tpu_custom_call" | custom-call | flops 855638016 | bytes 2097152 | tf_op jit(solution)/shard_map/pallas_call | solution.py:183
  25.3 1.5 %collective-permute-done.8.msg_ref = bf16[800,128]{1,0:T(8,128)(2,1)S(1)} collective-permute-done((bf16[800,128]{1,0:T(8,128)(2,1)S(1)}, bf16[800,128]{1,0:T(8,128)(2,1)S(1)}, u32[]{:S(2)}, u32[]{:S(2)}) %collective-permute-start.8) | collective-permute-done | bytes 204832 | tf_op jit(solution)/shard_map/ppermute | solution.py:459
  27.1 1.6 %collective-permute-start.9 = (bf16[416,128]{1,0:T(8,128)(2,1)S(1)}, bf16[416,128]{1,0:T(8,128)(2,1)S(1)}, u32[]{:S(2)}, u32[]{:S(2)}) collective-permute-start(bf16[416,128]{1,0:T(8,128)(2,1)S(1)} %get-tuple-element.52), channel_id=1, source_target_pairs={{0,8},{2,10},{4,12},{6,14},{8,0},{10,2},{12,4},{14,6},{16,24},{18,... | collective-permute-start | bytes 319496 | tf_op jit(solution)/shard_map/ppermute | solution.py:459
  29.2 2.7 %collective-permute-done.9.msg_ref = bf16[416,128]{1,0:T(8,128)(2,1)S(1)} collective-permute-done((bf16[416,128]{1,0:T(8,128)(2,1)S(1)}, bf16[416,128]{1,0:T(8,128)(2,1)S(1)}, u32[]{:S(2)}, u32[]{:S(2)}) %collective-permute-start.9) | collective-permute-done | bytes 106528 | tf_op jit(solution)/shard_map/ppermute | solution.py:459
  32.2 2.5 %collective-permute-start.11 = (bf16[416,128]{1,0:T(8,128)(2,1)S(1)}, bf16[416,128]{1,0:T(8,128)(2,1)S(1)}, u32[]{:S(2)}, u32[]{:S(2)}) collective-permute-start(bf16[416,128]{1,0:T(8,128)(2,1)S(1)} %get-tuple-element.57), channel_id=1, source_target_pairs={{0,16},{2,18},{4,20},{6,22},{8,24},{10,26},{12,28},{14,30},{16,0},... | collective-permute-start | bytes 319496 | tf_op jit(solution)/shard_map/ppermute | solution.py:459
  35.2 3.8 %collective-permute-done.11.msg_ref = bf16[416,128]{1,0:T(8,128)(2,1)S(1)} collective-permute-done((bf16[416,128]{1,0:T(8,128)(2,1)S(1)}, bf16[416,128]{1,0:T(8,128)(2,1)S(1)}, u32[]{:S(2)}, u32[]{:S(2)}) %collective-permute-start.11) | collective-permute-done | bytes 106528 | tf_op jit(solution)/shard_map/ppermute | solution.py:459
  39.3 0.8 %collective-permute-start.12 = (bf16[2,2,96,128]{3,2,1,0:T(8,128)(2,1)S(1)}, bf16[2,2,96,128]{3,2,1,0:T(8,128)(2,1)S(1)}, u32[]{:S(2)}, u32[]{:S(2)}) collective-permute-start(bf16[2,2,96,128]{3,2,1,0:T(8,128)(2,1)S(1)} %bitcast.34), channel_id=1, source_target_pairs={{0,8},{2,10},{4,12},{6,14},{8,0},{10,2},{12,4},{14,6},{16,24},{18,... | collective-permute-start | bytes 294920 | tf_op jit(solution)/shard_map/ppermute | solution.py:459
  40.1 3.9 %collective-permute-done.12 = bf16[2,2,96,128]{3,2,1,0:T(8,128)(2,1)S(1)} collective-permute-done((bf16[2,2,96,128]{3,2,1,0:T(8,128)(2,1)S(1)}, bf16[2,2,96,128]{3,2,1,0:T(8,128)(2,1)S(1)}, u32[]{:S(2)}, u32[]{:S(2)}) %collective-permute-start.12) | collective-permute-done | bytes 98336 | tf_op jit(solution)/shard_map/ppermute | solution.py:459
  44.0 1.7 %collective-permute-start.14 = (bf16[4,2,96,128]{3,2,1,0:T(8,128)(2,1)S(1)}, bf16[4,2,96,128]{3,2,1,0:T(8,128)(2,1)S(1)}, u32[]{:S(2)}, u32[]{:S(2)}) collective-permute-start(bf16[4,2,96,128]{3,2,1,0:T(8,128)(2,1)S(1)} %pad_maximum_fusion.refs_0_), channel_id=1, source_target_pairs={{0,4},{2,6},{4,0},{6,2},{8,12},{10,14},{12,8},{14,10},{16,20},{18,... | collective-permute-start | bytes 589832 | tf_op jit(solution)/shard_map/ppermute | solution.py:459
  46.1 4.2 %collective-permute-done.14.refs_1_ = bf16[4,2,96,128]{3,2,1,0:T(8,128)(2,1)S(1)} collective-permute-done((bf16[4,2,96,128]{3,2,1,0:T(8,128)(2,1)S(1)}, bf16[4,2,96,128]{3,2,1,0:T(8,128)(2,1)S(1)}, u32[]{:S(2)}, u32[]{:S(2)}) %collective-permute-start.14) | collective-permute-done | bytes 196640 | tf_op jit(solution)/shard_map/ppermute | solution.py:459
  50.9 1.0 %shard_map.109.refs_2_ = f32[96,512]{1,0:T(8,128)S(1)} custom-call(bf16[4,2,96,128]{3,2,1,0:T(8,128)(2,1)S(1)} %pad_maximum_fusion.refs_0_, bf16[4,2,96,128]{3,2,1,0:T(8,128)(2,1)S(1)} %collective-permute-done.14.refs_1_, bf16[4,2,96,128]{3,2,1,0:T(8,128)(2,1)S(1)} %collective-permute-done.16.refs_2_, bf16[4096,512]{1,0:T(8,128)(2,1)S(1)} %copy-done), custom_call_target="tpu_custom_call" | custom-call | flops 402653184 | bytes 4194304 | tf_op jit(solution)/shard_map/pallas_call | solution.py:321
  52.6 1.6 %collective-permute-start.18 = (bf16[48,512]{1,0:T(8,128)(2,1)S(1)}, bf16[48,512]{1,0:T(8,128)(2,1)S(1)}, u32[]{:S(2)}, u32[]{:S(2)}) collective-permute-start(bf16[48,512]{1,0:T(8,128)(2,1)S(1)} %get-tuple-element.63.rest_0_), channel_id=1, source_target_pairs={{0,1},{1,0},{2,3},{3,2},{4,5},{5,4},{6,7},{7,6},{8,9},{9,8},{10,11... | collective-permute-start | bytes 147464 | tf_op jit(solution)/shard_map/ppermute | solution.py:538
  54.2 1.6 %shard_map.111 = (bf16[1024,512]{1,0:T(8,128)(2,1)}, bf16[1024,512]{1,0:T(8,128)(2,1)}) custom-call(s32[2,128]{1,0:T(2,128)S(1)} %broadcast_in_dim.15.scal, bf16[1024,512]{1,0:T(8,128)(2,1)S(1)} %bitcast.33, bf16[1024,512]{1,0:T(8,128)(2,1)S(1)} %bitcast.30, bf16[8,2,24,128]{3,2,1,0:T(8,128)(2,1)S(1)} %pad_maximum_fusion.2.mine_ref, ...), custom_call_target="tpu_custom_call" | custom-call | bytes 4194304 | tf_op jit(solution)/shard_map/pallas_call | solution.py:434
  55.8 1.0 %collective-permute-done.18 = bf16[48,512]{1,0:T(8,128)(2,1)S(1)} collective-permute-done((bf16[48,512]{1,0:T(8,128)(2,1)S(1)}, bf16[48,512]{1,0:T(8,128)(2,1)S(1)}, u32[]{:S(2)}, u32[]{:S(2)}) %collective-permute-start.18) | collective-permute-done | bytes 49184 | tf_op jit(solution)/shard_map/ppermute | solution.py:538
  (49 shorter events, 7.4 us)
Async XLA Ops:
  1.5 1.9 %collective-permute-start = (bf16[2,48,128]{2,1,0:T(8,128)(2,1)S(1)}, bf16[2,48,128]{2,1,0:T(8,128)(2,1)S(1)}, u32[]{:S(2)}, u32[]{:S(2)}) collective-permute-start(bf16[2,48,128]{2,1,0:T(8,128)(2,1)S(1)} %get-tuple-element.68), channel_id=1, source_target_pairs={{0,2},{2,0},{4,6},{6,4},{8,10},{10,8},{12,14},{14,12},{16,18},{18,... | collective-permute-start | bytes 73736 | tf_op jit(solution)/shard_map/ppermute | solution.py:459
  3.5 13.9 %collective-permute-start.4 = (bf16[1024,512]{1,0:T(8,128)(2,1)}, bf16[1024,512]{1,0:T(8,128)(2,1)S(1)}, u32[]{:S(2)}, u32[]{:S(2)}) collective-permute-start(bf16[1024,512]{1,0:T(8,128)(2,1)} %bitcast.31), channel_id=1, source_target_pairs={{0,2},{2,0},{4,6},{6,4},{8,10},{10,8},{12,14},{14,12},{16,18},{18,... | collective-permute-start | bytes 3145736 | tf_op jit(solution)/shard_map/ppermute | solution.py:459
  3.5 13.9 %collective-permute-start.5 = (bf16[1024,512]{1,0:T(8,128)(2,1)}, bf16[1024,512]{1,0:T(8,128)(2,1)S(1)}, u32[]{:S(2)}, u32[]{:S(2)}) collective-permute-start(bf16[1024,512]{1,0:T(8,128)(2,1)} %bitcast.28), channel_id=1, source_target_pairs={{0,2},{2,0},{4,6},{6,4},{8,10},{10,8},{12,14},{14,12},{16,18},{18,... | collective-permute-start | bytes 3145736 | tf_op jit(solution)/shard_map/ppermute | solution.py:459
  4.0 6.7 %collective-permute-start.1 = (bf16[1,2,96,128]{3,2,1,0:T(8,128)(2,1)S(1)}, bf16[1,2,96,128]{3,2,1,0:T(8,128)(2,1)S(1)}, u32[]{:S(2)}, u32[]{:S(2)}) collective-permute-start(bf16[1,2,96,128]{3,2,1,0:T(8,128)(2,1)S(1)} %maximum_bitcast_fusion), channel_id=1, source_target_pairs={{0,16},{2,18},{4,20},{6,22},{8,24},{10,26},{12,28},{14,30},{16,0},... | collective-permute-start | bytes 147464 | tf_op jit(solution)/shard_map/ppermute | solution.py:459
  7.7 1.4 %collective-permute-start.6 = (bf16[6,512]{1,0:T(8,128)(2,1)}, bf16[6,512]{1,0:T(8,128)(2,1)S(1)}, u32[]{:S(2)}, u32[]{:S(2)}) collective-permute-start(bf16[6,512]{1,0:T(8,128)(2,1)} %bitcast.38), channel_id=1, source_target_pairs={{0,2},{2,0},{4,6},{6,4},{8,10},{10,8},{12,14},{14,12},{16,18},{18,... | collective-permute-start | bytes 18440 | tf_op jit(solution)/shard_map/ppermute | solution.py:459
  7.8 1.4 %collective-permute-start.7 = (bf16[6,512]{1,0:T(8,128)(2,1)}, bf16[6,512]{1,0:T(8,128)(2,1)S(1)}, u32[]{:S(2)}, u32[]{:S(2)}) collective-permute-start(bf16[6,512]{1,0:T(8,128)(2,1)} %bitcast.40), channel_id=1, source_target_pairs={{0,2},{2,0},{4,6},{6,4},{8,10},{10,8},{12,14},{14,12},{16,18},{18,... | collective-permute-start | bytes 18440 | tf_op jit(solution)/shard_map/ppermute | solution.py:459
  9.2 0.7 %copy-start.3 = (bf16[1,6,512]{2,1,0:T(8,128)(2,1)S(1)}, bf16[1,6,512]{2,1,0:T(8,128)(2,1)}, u32[]{:S(2)}) copy-start(bf16[1,6,512]{2,1,0:T(8,128)(2,1)} %param.9) | copy-start | bytes 18436
  10.7 5.1 %collective-permute-start.2 = (bf16[2,2,96,128]{3,2,1,0:T(8,128)(2,1)S(1)}, bf16[2,2,96,128]{3,2,1,0:T(8,128)(2,1)S(1)}, u32[]{:S(2)}, u32[]{:S(2)}) collective-permute-start(bf16[2,2,96,128]{3,2,1,0:T(8,128)(2,1)S(1)} %pad_maximum_fusion.1), channel_id=1, source_target_pairs={{0,8},{2,10},{4,12},{6,14},{8,0},{10,2},{12,4},{14,6},{16,24},{18,... | collective-permute-start | bytes 294920 | tf_op jit(solution)/shard_map/ppermute | solution.py:459
  15.8 6.4 %collective-permute-start.3 = (bf16[4,2,96,128]{3,2,1,0:T(8,128)(2,1)S(1)}, bf16[4,2,96,128]{3,2,1,0:T(8,128)(2,1)S(1)}, u32[]{:S(2)}, u32[]{:S(2)}) collective-permute-start(bf16[4,2,96,128]{3,2,1,0:T(8,128)(2,1)S(1)} %constant_dynamic-update-slice_fusion.q_ref), channel_id=1, source_target_pairs={{0,4},{2,6},{4,0},{6,2},{8,12},{10,14},{12,8},{14,10},{16,20},{18,... | collective-permute-start | bytes 589832 | tf_op jit(solution)/shard_map/ppermute | solution.py:459
  17.4 33.4 %copy-start = (bf16[4096,512]{1,0:T(8,128)(2,1)S(1)}, bf16[4096,512]{1,0:T(8,128)(2,1)}, u32[]{:S(2)}) copy-start(bf16[4096,512]{1,0:T(8,128)(2,1)} %refs_1_.1) | copy-start | bytes 12582916
  20.4 6.3 %collective-permute-start.8 = (bf16[800,128]{1,0:T(8,128)(2,1)S(1)}, bf16[800,128]{1,0:T(8,128)(2,1)S(1)}, u32[]{:S(2)}, u32[]{:S(2)}) collective-permute-start(bf16[800,128]{1,0:T(8,128)(2,1)S(1)} %shard_map.104.rest_5_), channel_id=1, source_target_pairs={{0,4},{2,6},{4,0},{6,2},{8,12},{10,14},{12,8},{14,10},{16,20},{18,... | collective-permute-start | bytes 614408 | tf_op jit(solution)/shard_map/ppermute | solution.py:459
  27.1 4.8 %collective-permute-start.9 = (bf16[416,128]{1,0:T(8,128)(2,1)S(1)}, bf16[416,128]{1,0:T(8,128)(2,1)S(1)}, u32[]{:S(2)}, u32[]{:S(2)}) collective-permute-start(bf16[416,128]{1,0:T(8,128)(2,1)S(1)} %get-tuple-element.52), channel_id=1, source_target_pairs={{0,8},{2,10},{4,12},{6,14},{8,0},{10,2},{12,4},{14,6},{16,24},{18,... | collective-permute-start | bytes 319496 | tf_op jit(solution)/shard_map/ppermute | solution.py:459
  28.8 5.9 %collective-permute-start.10 = (bf16[1,2,24,128]{3,2,1,0:T(8,128)(2,1)S(1)}, bf16[1,2,24,128]{3,2,1,0:T(8,128)(2,1)S(1)}, u32[]{:S(2)}, u32[]{:S(2)}) collective-permute-start(bf16[1,2,24,128]{3,2,1,0:T(8,128)(2,1)S(1)} %bitcast.36), channel_id=1, source_target_pairs={{0,8},{2,10},{4,12},{6,14},{8,0},{10,2},{12,4},{14,6},{16,24},{18,... | collective-permute-start | bytes 36872 | tf_op jit(solution)/shard_map/ppermute | solution.py:459
  32.2 6.8 %collective-permute-start.11 = (bf16[416,128]{1,0:T(8,128)(2,1)S(1)}, bf16[416,128]{1,0:T(8,128)(2,1)S(1)}, u32[]{:S(2)}, u32[]{:S(2)}) collective-permute-start(bf16[416,128]{1,0:T(8,128)(2,1)S(1)} %get-tuple-element.57), channel_id=1, source_target_pairs={{0,16},{2,18},{4,20},{6,22},{8,24},{10,26},{12,28},{14,30},{16,0},... | collective-permute-start | bytes 319496 | tf_op jit(solution)/shard_map/ppermute | solution.py:459
  34.7 5.4 %collective-permute-start.13 = (bf16[2,2,24,128]{3,2,1,0:T(8,128)(2,1)S(1)}, bf16[2,2,24,128]{3,2,1,0:T(8,128)(2,1)S(1)}, u32[]{:S(2)}, u32[]{:S(2)}) collective-permute-start(bf16[2,2,24,128]{3,2,1,0:T(8,128)(2,1)S(1)} %pad_maximum_fusion.4), channel_id=1, source_target_pairs={{0,16},{2,18},{4,20},{6,22},{8,24},{10,26},{12,28},{14,30},{16,0},... | collective-permute-start | bytes 73736 | tf_op jit(solution)/shard_map/ppermute | solution.py:459
  39.3 4.7 %collective-permute-start.12 = (bf16[2,2,96,128]{3,2,1,0:T(8,128)(2,1)S(1)}, bf16[2,2,96,128]{3,2,1,0:T(8,128)(2,1)S(1)}, u32[]{:S(2)}, u32[]{:S(2)}) collective-permute-start(bf16[2,2,96,128]{3,2,1,0:T(8,128)(2,1)S(1)} %bitcast.34), channel_id=1, source_target_pairs={{0,8},{2,10},{4,12},{6,14},{8,0},{10,2},{12,4},{14,6},{16,24},{18,... | collective-permute-start | bytes 294920 | tf_op jit(solution)/shard_map/ppermute | solution.py:459
  44.0 6.3 %collective-permute-start.14 = (bf16[4,2,96,128]{3,2,1,0:T(8,128)(2,1)S(1)}, bf16[4,2,96,128]{3,2,1,0:T(8,128)(2,1)S(1)}, u32[]{:S(2)}, u32[]{:S(2)}) collective-permute-start(bf16[4,2,96,128]{3,2,1,0:T(8,128)(2,1)S(1)} %pad_maximum_fusion.refs_0_), channel_id=1, source_target_pairs={{0,4},{2,6},{4,0},{6,2},{8,12},{10,14},{12,8},{14,10},{16,20},{18,... | collective-permute-start | bytes 589832 | tf_op jit(solution)/shard_map/ppermute | solution.py:459
  45.8 5.1 %collective-permute-start.16 = (bf16[4,2,96,128]{3,2,1,0:T(8,128)(2,1)S(1)}, bf16[4,2,96,128]{3,2,1,0:T(8,128)(2,1)S(1)}, u32[]{:S(2)}, u32[]{:S(2)}) collective-permute-start(bf16[4,2,96,128]{3,2,1,0:T(8,128)(2,1)S(1)} %pad_maximum_fusion.refs_0_), channel_id=1, source_target_pairs={{0,2},{2,0},{4,6},{6,4},{8,10},{10,8},{12,14},{14,12},{16,18},{18,... | collective-permute-start | bytes 589832 | tf_op jit(solution)/shard_map/ppermute | solution.py:459
  45.8 5.0 %collective-permute-start.17 = (bf16[4,2,24,128]{3,2,1,0:T(8,128)(2,1)S(1)}, bf16[4,2,24,128]{3,2,1,0:T(8,128)(2,1)S(1)}, u32[]{:S(2)}, u32[]{:S(2)}) collective-permute-start(bf16[4,2,24,128]{3,2,1,0:T(8,128)(2,1)S(1)} %pad_maximum_fusion.3), channel_id=1, source_target_pairs={{0,4},{2,6},{4,0},{6,2},{8,12},{10,14},{12,8},{14,10},{16,20},{18,... | collective-permute-start | bytes 147464 | tf_op jit(solution)/shard_map/ppermute | solution.py:459
  50.3 1.7 %collective-permute-start.15 = (bf16[4,2,96,128]{3,2,1,0:T(8,128)(2,1)S(1)}, bf16[4,2,96,128]{3,2,1,0:T(8,128)(2,1)S(1)}, u32[]{:S(2)}, u32[]{:S(2)}) collective-permute-start(bf16[4,2,96,128]{3,2,1,0:T(8,128)(2,1)S(1)} %collective-permute-done.14.refs_1_), channel_id=1, source_target_pairs={{0,2},{2,0},{4,6},{6,4},{8,10},{10,8},{12,14},{14,12},{16,18},{18,... | collective-permute-start | bytes 589832 | tf_op jit(solution)/shard_map/ppermute | solution.py:459
  50.8 3.3 %copy-start.1 = (bf16[1,1024,512]{2,1,0:T(8,128)(2,1)S(1)}, bf16[1,1024,512]{2,1,0:T(8,128)(2,1)}, u32[]{:S(2)}) copy-start(bf16[1,1024,512]{2,1,0:T(8,128)(2,1)} %param.12) | copy-start | bytes 3145732
  50.8 3.3 %copy-start.2 = (bf16[1,1024,512]{2,1,0:T(8,128)(2,1)S(1)}, bf16[1,1024,512]{2,1,0:T(8,128)(2,1)}, u32[]{:S(2)}) copy-start(bf16[1,1024,512]{2,1,0:T(8,128)(2,1)} %param.11) | copy-start | bytes 3145732
  51.9 2.2 %collective-permute-start.19 = (bf16[8,2,24,128]{3,2,1,0:T(8,128)(2,1)S(1)}, bf16[8,2,24,128]{3,2,1,0:T(8,128)(2,1)S(1)}, u32[]{:S(2)}, u32[]{:S(2)}) collective-permute-start(bf16[8,2,24,128]{3,2,1,0:T(8,128)(2,1)S(1)} %pad_maximum_fusion.2.mine_ref), channel_id=1, source_target_pairs={{0,2},{2,0},{4,6},{6,4},{8,10},{10,8},{12,14},{14,12},{16,18},{18,... | collective-permute-start | bytes 294920 | tf_op jit(solution)/shard_map/ppermute | solution.py:459
  52.6 4.2 %collective-permute-start.18 = (bf16[48,512]{1,0:T(8,128)(2,1)S(1)}, bf16[48,512]{1,0:T(8,128)(2,1)S(1)}, u32[]{:S(2)}, u32[]{:S(2)}) collective-permute-start(bf16[48,512]{1,0:T(8,128)(2,1)S(1)} %get-tuple-element.63.rest_0_), channel_id=1, source_target_pairs={{0,1},{1,0},{2,3},{3,2},{4,5},{5,4},{6,7},{7,6},{8,9},{9,8},{10,11... | collective-permute-start | bytes 147464 | tf_op jit(solution)/shard_map/ppermute | solution.py:538
  (1 other events, 0.7 us)
